TPU v7x, 32 devices: a whole 2x2x4 slice. The times are simulated.
32 devices in a mesh: blk: 8 (over z, y), orb: 4 (over x, core).
Axes of the slice: x: 2, y: 2, z: 4, core: 2. Of those that a mesh axis runs over, the one named last changes fastest.
Arguments:
- orbitals: bfloat16 [4096, 8192], P('blk', 'orb'), may hold values from -0.62890625 to 0.62890625
- coulomb_near: bfloat16 [4096, 512], P('blk'), may hold values from -0.52734375 to 0.52734375
- coulomb_far: bfloat16 [4096, 512], P('blk'), may hold values from -0.52734375 to 0.52734375
Outputs:
- exchange: bfloat16 [4096, 8192], P('blk', 'orb')
All inputs are finite; a program needn't handle non-finite values.
Results may differ from a plain program's by a relative error of at most 0.0049.
Values may be sent and summed in bfloat16 or wider, within the bound.
No kernel may reach another device: no remote copies, remote signals or barrier semaphores. Data moves between devices by JAX's collectives and lax.ppermute only.
A program may use at most 64 MiB of HBM per device.

v0:
```python
import jax
import jax.numpy as jnp
from jax import lax
from jax.sharding import PartitionSpec as P


def from_behind(value, axis, by):
    devices = lax.axis_size(axis)
    return lax.ppermute(value, axis, [(i, (i + by) % devices) for i in range(devices)])


def weigh(partial_gram, slab):
    gram = lax.psum(partial_gram, "orb")
    return (gram * slab.astype(jnp.float32)).astype(jnp.bfloat16)


def contract_last(left, right):
    return lax.dot_general(
        left, right, (((1,), (1,)), ((), ())), preferred_element_type=jnp.float32
    )


def per_device(orbitals, coulomb_near, coulomb_far):
    far_offset = lax.axis_size("blk") // 4
    total = jnp.zeros(orbitals.shape, jnp.float32)
    for offset, slab in ((1, coulomb_near), (far_offset, coulomb_far)):
        partner_vals = from_behind(orbitals, "blk", -offset)
        weighted = weigh(contract_last(orbitals, partner_vals), slab)
        total = total + jnp.dot(weighted, partner_vals, preferred_element_type=jnp.float32)
        earlier_vals, earlier_slab = from_behind((orbitals, slab), "blk", offset)
        flipped = weigh(contract_last(orbitals, earlier_vals), earlier_slab.T)
        total = total + jnp.dot(flipped, earlier_vals, preferred_element_type=jnp.float32)
    return total.astype(jnp.bfloat16)


def solution(mesh):
    return jax.shard_map(
        per_device,
        mesh=mesh,
        in_specs=(P("blk", "orb"), P("blk", None), P("blk", None)),
        out_specs=P("blk", "orb"),
        check_vma=False,
    )
```

profile of v0, /device:TPU:0, one launch (start us, length us, event | category | flops | bytes accessed | tf_op | source)
XLA Modules:
  0.0 255.9 jit_solution(13313524937096336060)
XLA Ops:
  6.5 6.0 %collective-permute-start = (bf16[512,2048]{1,0:T(8,128)(2,1)}, bf16[512,2048]{1,0:T(8,128)(2,1)S(1)}, u32[]{:S(2)}, u32[]{:S(2)}) collective-permute-start(bf16[512,2048]{1,0:T(8,128)(2,1)} %param.3), channel_id=1, source_target_pairs={{0,28},{4,0},{8,4},{12,8},{16,12},{20,16},{24,20},{28,24},{1,29},{... | collective-permute-start | bytes 6291464 | tf_op jit(solution)/shard_map/ppermute | solution.py:9
  12.5 0.0 collective-permute-start.1
  12.5 1.1 collective-permute-start.3
  13.6 1.0 collective-permute-start.4
  14.6 85.8 %collective-permute-done = bf16[512,2048]{1,0:T(8,128)(2,1)S(1)} collective-permute-done((bf16[512,2048]{1,0:T(8,128)(2,1)}, bf16[512,2048]{1,0:T(8,128)(2,1)S(1)}, u32[]{:S(2)}, u32[]{:S(2)}) %collective-permute-start) | collective-permute-done | bytes 2097184 | tf_op jit(solution)/shard_map/ppermute | solution.py:9
  100.4 4.7 %fusion.10 = f32[512,512]{1,0:T(8,128)} fusion(bf16[512,2048]{1,0:T(8,128)(2,1)} %param.3, bf16[512,2048]{1,0:T(8,128)(2,1)S(1)} %collective-permute-done), kind=kOutput, calls=%fused_computation.11 | convolution fusion | flops 1073741824 | bytes 5242880 | tf_op jit(solution)/shard_map/dot_general | solution.py:18
  105.1 0.0 collective-permute-done.1
  105.1 2.2 fusion.11
  107.3 0.0 collective-permute-done.3
  107.3 2.3 fusion.12
  109.6 38.9 %collective-permute-done.4 = bf16[512,2048]{1,0:T(8,128)(2,1)S(1)} collective-permute-done((bf16[512,2048]{1,0:T(8,128)(2,1)}, bf16[512,2048]{1,0:T(8,128)(2,1)S(1)}, u32[]{:S(2)}, u32[]{:S(2)}) %collective-permute-start.4) | collective-permute-done | bytes 2097184 | tf_op jit(solution)/shard_map/ppermute | solution.py:9
  148.5 2.3 fusion.13
  150.8 0.0 all-reduce.3.cloned.1.call-update
  150.8 1.0 copy-done.8
  151.8 4.6 %collective-permute-start.2 = (bf16[512,512]{1,0:T(8,128)(2,1)S(1)}, bf16[512,512]{1,0:T(8,128)(2,1)}, u32[]{:S(2)}, u32[]{:S(2)}) collective-permute-start(bf16[512,512]{1,0:T(8,128)(2,1)S(1)} %copy-done.8), channel_id=1, source_target_pairs={{0,4},{4,8},{8,12},{12,16},{16,20},{20,24},{24,28},{28,0},{1,5},{5... | collective-permute-start | bytes 1572872 | tf_op jit(solution)/shard_map/ppermute | solution.py:9
  156.4 0.0 collective-permute-start.5
  156.4 81.9 %all-reduce.3.cloned.1.call-done = (f32[512,512]{1,0:T(8,128)}, f32[512,512]{1,0:T(8,128)}, f32[512,512]{0,1:T(8,128)}, f32[512,512]{0,1:T(8,128)}) async-done(((f32[512,512]{1,0:T(8,128)}, f32[512,512]{1,0:T(8,128)}, f32[512,512]{0,1:T(8,128)}, f32[512,512]{0,1:T(8,128)}), (f32[512,512]{1,0:T(8,128)}, f32[512,512]{1,0:T(8,128)}, f32[512,512]{0,1:T(8,128)}, ...) | async-done | bytes 4194320 | tf_op jit(solution)/shard_map/psum | solution.py:13
  238.2 3.3 %fusion.2 = f32[512,2048]{1,0:T(8,128)S(1)} fusion(bf16[512,2048]{1,0:T(8,128)(2,1)} %copy-done.2, f32[512,512]{1,0:T(8,128)} %get-tuple-element.6, bf16[512,512]{1,0:T(8,128)(2,1)S(1)} %copy-done.8), kind=kOutput, calls=%fused_computation.7 | convolution fusion | flops 1074528256 | bytes 7864320 | tf_op jit(solution)/shard_map/dot_general | solution.py:29
  241.6 1.3 fusion.3
  242.9 0.0 collective-permute-done.2
  242.9 0.3 copy-done.1
  243.2 0.3 copy-done.6
  243.4 2.5 fusion.4
  245.9 3.1 %add_convert_fusion = bf16[512,2048]{1,0:T(8,128)(2,1)} fusion(f32[512,2048]{1,0:T(8,128)S(1)} %fusion.3, f32[512,2048]{1,0:T(8,128)S(1)} %fusion.2, f32[512,2048]{1,0:T(8,128)S(1)} %fusion.4, bf16[512,2048]{1,0:T(8,128)(2,1)S(1)} %collective-permute-done.4, f32[512,512]{0,1:T(8,128)S(1)} %copy-done.5, bf16[512,512]{1,0:T(8,128)(2,1)S(1)} %collective-permute-done.5), kind=kOutput, calls=%fused_computation | convolution fusion | flops 1078722560 | bytes 18350080 | tf_op jit(solution)/shard_map/dot_general | solution.py:32
  (21 shorter events, 0.0 us)
Async XLA Ops:
  6.5 231.7 %all-reduce.3.cloned.1.call-start = ((), (), s32[]{:S(2)}) async-start(), calls=%async_computation | async-start | bytes 8388608 | tf_op jit(solution)/shard_map/psum | solution.py:13
  6.5 98.5 %copy-start.10 = (bf16[512,2048]{1,0:T(8,128)(2,1)S(1)}, bf16[512,2048]{1,0:T(8,128)(2,1)}, u32[]{:S(2)}) copy-start(bf16[512,2048]{1,0:T(8,128)(2,1)} %param.3) | copy-start | bytes 6291460
  6.5 93.8 %collective-permute-start = (bf16[512,2048]{1,0:T(8,128)(2,1)}, bf16[512,2048]{1,0:T(8,128)(2,1)S(1)}, u32[]{:S(2)}, u32[]{:S(2)}) collective-permute-start(bf16[512,2048]{1,0:T(8,128)(2,1)} %param.3), channel_id=1, source_target_pairs={{0,28},{4,0},{8,4},{12,8},{16,12},{20,16},{24,20},{28,24},{1,29},{... | collective-permute-start | bytes 6291464 | tf_op jit(solution)/shard_map/ppermute | solution.py:9
  12.5 92.5 %collective-permute-start.1 = (bf16[512,2048]{1,0:T(8,128)(2,1)}, bf16[512,2048]{1,0:T(8,128)(2,1)S(1)}, u32[]{:S(2)}, u32[]{:S(2)}) collective-permute-start(bf16[512,2048]{1,0:T(8,128)(2,1)} %param.3), channel_id=1, source_target_pairs={{0,4},{4,8},{8,12},{12,16},{16,20},{20,24},{24,28},{28,0},{1,5},{5... | collective-permute-start | bytes 6291464 | tf_op jit(solution)/shard_map/ppermute | solution.py:9
  12.5 94.8 %collective-permute-start.3 = (bf16[512,2048]{1,0:T(8,128)(2,1)}, bf16[512,2048]{1,0:T(8,128)(2,1)S(1)}, u32[]{:S(2)}, u32[]{:S(2)}) collective-permute-start(bf16[512,2048]{1,0:T(8,128)(2,1)} %param.3), channel_id=1, source_target_pairs={{0,24},{4,28},{8,0},{12,4},{16,8},{20,12},{24,16},{28,20},{1,25},{... | collective-permute-start | bytes 6291464 | tf_op jit(solution)/shard_map/ppermute | solution.py:9
  13.6 134.9 %collective-permute-start.4 = (bf16[512,2048]{1,0:T(8,128)(2,1)}, bf16[512,2048]{1,0:T(8,128)(2,1)S(1)}, u32[]{:S(2)}, u32[]{:S(2)}) collective-permute-start(bf16[512,2048]{1,0:T(8,128)(2,1)} %param.3), channel_id=1, source_target_pairs={{0,8},{4,12},{8,16},{12,20},{16,24},{20,28},{24,0},{28,4},{1,9},{5... | collective-permute-start | bytes 6291464 | tf_op jit(solution)/shard_map/ppermute | solution.py:9
  100.4 4.7 %copy-start.2 = (bf16[512,2048]{1,0:T(8,128)(2,1)}, bf16[512,2048]{1,0:T(8,128)(2,1)S(1)}, u32[]{:S(2)}) copy-start(bf16[512,2048]{1,0:T(8,128)(2,1)S(1)} %collective-permute-done) | copy-start | bytes 6291460
  105.1 2.3 copy-start
  107.3 2.3 copy-start.3
  150.8 1.0 copy-start.8
  151.8 91.1 %collective-permute-start.2 = (bf16[512,512]{1,0:T(8,128)(2,1)S(1)}, bf16[512,512]{1,0:T(8,128)(2,1)}, u32[]{:S(2)}, u32[]{:S(2)}) collective-permute-start(bf16[512,512]{1,0:T(8,128)(2,1)S(1)} %copy-done.8), channel_id=1, source_target_pairs={{0,4},{4,8},{8,12},{12,16},{16,20},{20,24},{24,28},{28,0},{1,5},{5... | collective-permute-start | bytes 1572872 | tf_op jit(solution)/shard_map/ppermute | solution.py:9
  156.4 89.6 %collective-permute-start.5 = (bf16[512,512]{1,0:T(8,128)(2,1)}, bf16[512,512]{1,0:T(8,128)(2,1)S(1)}, u32[]{:S(2)}, u32[]{:S(2)}) collective-permute-start(bf16[512,512]{1,0:T(8,128)(2,1)} %param.5), channel_id=1, source_target_pairs={{0,8},{4,12},{8,16},{12,20},{16,24},{20,28},{24,0},{28,4},{1,9},{5... | collective-permute-start | bytes 1572872 | tf_op jit(solution)/shard_map/ppermute | solution.py:9
  238.2 3.3 %copy-start.4 = (bf16[512,2048]{1,0:T(8,128)(2,1)S(1)}, bf16[512,2048]{1,0:T(8,128)(2,1)}, u32[]{:S(2)}) copy-start(bf16[512,2048]{1,0:T(8,128)(2,1)} %copy-done.3) | copy-start | bytes 6291460
  238.2 3.3 %copy-start.7 = (f32[512,512]{1,0:T(8,128)S(1)}, f32[512,512]{1,0:T(8,128)}, u32[]{:S(2)}) copy-start(f32[512,512]{1,0:T(8,128)} %get-tuple-element.5) | copy-start | bytes 3145732
  238.2 3.3 %copy-start.9 = (bf16[512,512]{1,0:T(8,128)(2,1)S(1)}, bf16[512,512]{1,0:T(8,128)(2,1)}, u32[]{:S(2)}) copy-start(bf16[512,512]{1,0:T(8,128)(2,1)} %param.5) | copy-start | bytes 1572868
  241.6 1.6 copy-start.1
  241.6 1.8 copy-start.6
  243.4 2.5 copy-start.5
Sparse Core Ops, SparseCore 0:
  150.9 87.2 all-reduce.2
where the time goes:
time: 256 us
  waiting for transfers between devices  207 us (81%)
  matrix products  21.7 us (8%)
  between operations  13.5 us (5%)
  starting transfers between devices  12.6 us (5%)
    ppermute x6, waiting for transfers between devices, from_behind(): lax.ppermute(value, axis, [(i, (i + by) % devices) for i in range(devices)])  125 us
    psum x1, waiting for transfers between devices, weigh(): gram = lax.psum(partial_gram, 'orb')  81.9 us
    ppermute x6, starting transfers between devices, from_behind(): lax.ppermute(value, axis, [(i, (i + by) % devices) for i in range(devices)])  12.6 us
    dot_general x4, matrix products, contract_last(): lax.dot_general(left, right, (((1,), (1,)), ((), ())), preferred_element_...  11.5 us
    dot_general x2, matrix products, per_device(): jnp.dot(flipped, earlier_vals, preferred_element_type=jnp.float32)  5.59 us
  transfers between devices with their start and end apart: 7, of which 3 were waited for; matrix products, arithmetic and copies ran while one was open for 6% of the time, Pallas kernels for 0%

commit v1 on v0

v1 whole, which is shorter than its diff:
```python
import functools

import jax
import jax.numpy as jnp
from jax import lax
from jax.experimental import pallas as pl
from jax.experimental.pallas import tpu as pltpu
from jax.sharding import PartitionSpec as P

MIB = 1024 * 1024
F32, BF16 = jnp.float32, jnp.bfloat16
VMEM = pl.BlockSpec(memory_space=pltpu.VMEM)
ANY = pl.BlockSpec(memory_space=pl.ANY)


def shape(rows, columns, kind):
    return jax.ShapeDtypeStruct((rows, columns), kind)


def cost(flops, moved_bytes):
    return pl.CostEstimate(flops=flops, bytes_accessed=moved_bytes, transcendentals=0)


def outer(left, right):
    return lax.dot_general(left, right, (((1,), (1,)), ((), ())), preferred_element_type=F32)


def inner(left, right):
    return jnp.dot(left, right, preferred_element_type=F32)


def moved(value, axis, pairs):
    return lax.ppermute(value, axis, pairs)


def swapped(value, axis, distance):
    devices = lax.axis_size(axis)
    return lax.ppermute(value, axis, [(i, i ^ distance) for i in range(devices)])


def after(values, *earlier):
    return lax.optimization_barrier((*values, *earlier))[: len(values)]


def quarter_index(distance=0):
    me = lax.axis_index("orb")
    return ((me % 2) * 2 + me // 2) ^ distance


def quarter_rows(rows, distance=0):
    size = rows // 4
    return pl.ds(pl.multiple_of(quarter_index(distance) * size, size), size)


def pack_kernel(x, near, far, near_out, far_out):
    rows, columns = near.shape[0], x.shape[1]
    quarter = rows // 4
    height = rows * quarter // columns
    here = quarter_rows(rows)
    for slab, out in ((far, far_out), (near, near_out)):
        size = out.shape[0] - height
        out[:size, :] = x[:size, :]
        for i in range(rows // height):
            block = slab[i * height : (i + 1) * height, here]
            out[size:, i * quarter : (i + 1) * quarter] = block


def pack(x, near, far, near_size, far_size):
    rows, columns = x.shape
    height = rows * (rows // 4) // columns
    return pl.pallas_call(
        pack_kernel,
        in_specs=[VMEM] * 3,
        out_specs=[VMEM] * 2,
        out_shape=[
            shape(near_size + height, columns, BF16),
            shape(far_size + height, columns, BF16),
        ],
        compiler_params=pltpu.CompilerParams(vmem_limit_bytes=10 * MIB),
        cost_estimate=cost(0, 6 * near_size * columns),
    )(x, near, far)


def unpacked(packed, rows):
    quarter = rows // 4
    height = rows * quarter // packed.shape[1]
    top = packed.shape[0] - height
    blocks = [
        packed[top:, i * quarter : (i + 1) * quarter].astype(F32) for i in range(rows // height)
    ]
    return jnp.concatenate(blocks, 0).T


def gram_first_kernel(x, z, total):
    total[...] = outer(x[...], z[: total.shape[1], :])


def gram_last_kernel(x, y, z, z_more, early, keep, send, late, xy, zy):
    rows, more = x.shape[0], z_more.shape[0]
    size = rows - more
    late[...] = outer(x[...], z_more[...])
    xy[...] = outer(x[...], y[:rows, :])
    zy[:size, :] = outer(z[:size, :], y[:rows, :])
    zy[size:, :] = outer(z_more[...], y[:rows, :])
    quarter = rows // 4
    for distance in range(4):
        target, kind = (keep, F32) if distance < 2 else (send, BF16)
        place = distance % 2 * quarter
        here, there = quarter_rows(rows, distance), slice(place, place + quarter)
        target[there, :rows] = xy[here, :].astype(kind)
        target[there, rows : rows + size] = early[here, :].astype(kind)
        target[there, rows + size : 2 * rows] = late[here, :].astype(kind)
        target[there, 2 * rows :] = zy[here, :].astype(kind)


def gram_first(x, z, size):
    rows, columns = x.shape
    return pl.pallas_call(
        gram_first_kernel,
        in_specs=[VMEM] * 2,
        out_specs=VMEM,
        out_shape=shape(rows, size, F32),
        compiler_params=pltpu.CompilerParams(vmem_limit_bytes=10 * MIB),
        cost_estimate=cost(2 * rows * size * columns, 4 * rows * columns),
    )(x, z)


def gram_last(x, y, z, z_more, early):
    rows, more = x.shape[0], z_more.shape[0]
    return pl.pallas_call(
        gram_last_kernel,
        in_specs=[VMEM] * 5,
        out_specs=[VMEM] * 2,
        out_shape=[shape(rows // 2, 3 * rows, F32), shape(rows // 2, 3 * rows, BF16)],
        scratch_shapes=[pltpu.VMEM((rows, more), F32)] + [pltpu.VMEM((rows, rows), F32)] * 2,
        compiler_params=pltpu.CompilerParams(vmem_limit_bytes=20 * MIB),
        cost_estimate=cost(0, 0),
    )(x, y, z, z_more, early)


def fold_kernel(keep, other, mine, send):
    size = mine.shape[0]
    mine[...] = keep[:size, :] + other[:size, :].astype(F32)
    send[...] = (keep[size:, :] + other[size:, :].astype(F32)).astype(BF16)


def fold(keep, other):
    size, width = keep.shape[0] // 2, keep.shape[1]
    return pl.pallas_call(
        fold_kernel,
        in_specs=[VMEM] * 2,
        out_specs=[VMEM] * 2,
        out_shape=[shape(size, width, F32), shape(size, width, BF16)],
        compiler_params=pltpu.CompilerParams(vmem_limit_bytes=8 * MIB),
        cost_estimate=cost(4 * size * width, 18 * size * width),
    )(keep, other)


def weigh_kernel(mine, other, near, far, near_other, far_other, ahead, xz, zy):
    rows = near.shape[0]
    here = quarter_rows(rows)
    even = lax.axis_index("blk") % 2 == 0
    gram = mine[...] + other[...].astype(F32)
    near_turned, far_turned = unpacked(near_other, rows), unpacked(far_other, rows)
    near_slab = jnp.where(even, near[here, :].astype(F32), near_turned)
    far_slab = jnp.where(even, far[here, :].astype(F32), far_turned)
    ahead[:, :rows] = (gram[:, :rows] * near_slab).astype(BF16)
    weighted = (gram[:, rows : 2 * rows] * far_slab).astype(BF16)
    ahead[:, rows:] = weighted
    xz[...] = weighted
    zy[...] = (gram[:, 2 * rows :] * near_turned).astype(BF16)


def weigh(mine, other, near, far, near_other, far_other):
    size, rows = mine.shape[0], near.shape[0]
    return pl.pallas_call(
        weigh_kernel,
        in_specs=[VMEM] * 6,
        out_specs=[VMEM] * 3,
        out_shape=[shape(size, 2 * rows, BF16), shape(size, rows, BF16), shape(size, rows, BF16)],
        compiler_params=pltpu.CompilerParams(vmem_limit_bytes=8 * MIB),
        cost_estimate=cost(6 * size * rows, 40 * size * rows),
    )(mine, other, near, far, near_other, far_other)


def most_kernel(places, *refs):
    ahead, back, values = refs[:4], refs[4:8], refs[8 : 8 + len(places)]
    out, kept, weights, held, arrived = refs[8 + len(values) :]
    rows, columns = out.shape
    size, tiles, last = rows // 4, 4, kept.shape[1] // 2
    copies = []
    for i, (top, bottom) in enumerate(places):
        source = values[i].at[: bottom - top, :]
        copies.append(pltpu.make_async_copy(source, held.at[top:bottom, :], arrived.at[i]))
        copies[-1].start()

    even = lax.axis_index("blk") % 2 == 0
    for distance in range(4):
        weights[quarter_rows(rows, distance), : 2 * rows] = ahead[distance][...]
    for distance in range(4):
        here = quarter_rows(rows, distance)
        weights[:, pl.ds(pl.multiple_of(3 * rows + here.start, size), size)] = (
            back[distance][:, :rows].astype(F32).T.astype(BF16)
        )
        near = back[distance][:, rows:]

        @pl.when(even)
        def _():
            weights[here, 2 * rows : 3 * rows] = near

        @pl.when(jnp.logical_not(even))
        def _():
            weights[:, pl.ds(pl.multiple_of(2 * rows + here.start, size), size)] = (
                near.astype(F32).T.astype(BF16)
            )

    for i in (2, 3):
        kept[:, (i - 2) * last : (i - 1) * last] = weights[:, i * rows : i * rows + last]
    place = 2 * rows
    for i in (2, 3):
        there = slice(place, place + rows - last)
        weights[:, there] = weights[:, i * rows + last : (i + 1) * rows]
        place += rows - last
    for copy in copies:
        copy.wait()
    for k in range(tiles):
        here = slice(k * columns // tiles, (k + 1) * columns // tiles)
        out[:, here] = inner(weights[:, :place], held[:, here])


def apply_most(places, last, ahead, back, values):
    rows, columns = ahead[0].shape[0] * 4, values[0].shape[1]
    return pl.pallas_call(
        functools.partial(most_kernel, places),
        in_specs=[VMEM] * 8 + [ANY] * len(values),
        out_specs=[VMEM] * 2,
        out_shape=[shape(rows, columns, F32), shape(rows, 2 * last, BF16)],
        scratch_shapes=[
            pltpu.VMEM((rows, 4 * rows), BF16),
            pltpu.VMEM((4 * rows - 2 * last, columns), BF16),
            pltpu.SemaphoreType.DMA((len(values),)),
        ],
        compiler_params=pltpu.CompilerParams(vmem_limit_bytes=22 * MIB),
        cost_estimate=cost(6 * rows * rows * columns, 12 * rows * columns),
    )(*ahead, *back, *values)


def last_kernel(weights, total, u, w, out, result, left):
    rows, columns = out.shape
    last, tiles = u.shape[0], 4
    writes = []
    for k in range(tiles):
        here = slice(k * columns // tiles, (k + 1) * columns // tiles)
        added = inner(weights[:, :last], u[:, here]) + inner(weights[:, last:], w[:, here])
        result[:, here] = (total[:, here] + added).astype(BF16)
        writes.append(pltpu.make_async_copy(result.at[:, here], out.at[:, here], left.at[k]))
        writes[-1].start()
    for write in writes:
        write.wait()


def apply_last(weights, total, u, w):
    rows, columns = total.shape
    last = u.shape[0]
    return pl.pallas_call(
        last_kernel,
        in_specs=[VMEM] * 4,
        out_specs=ANY,
        out_shape=shape(rows, columns, BF16),
        scratch_shapes=[pltpu.VMEM((rows, columns), BF16), pltpu.SemaphoreType.DMA((4,))],
        compiler_params=pltpu.CompilerParams(vmem_limit_bytes=16 * MIB),
        cost_estimate=cost(4 * rows * last * columns, 6 * rows * columns + 4 * last * columns),
    )(weights, total, u, w)


def gather(value):
    by_x = swapped(value, "orb", 2)
    return value, by_x, swapped(value, "orb", 1), swapped(by_x, "orb", 1)


def relayed(x, near, far):
    blocks = lax.axis_size("blk")
    rows, columns = x.shape
    even = lax.axis_index("blk") % 2 == 0
    inward = [(b, (b - 2 if b % 2 == 0 else b + 2) % blocks) for b in range(blocks)]
    outward = [(b, (b + 2 if b % 2 == 0 else b - 2) % blocks) for b in range(blocks)]

    size = rows // 2
    x_half, x_more = x[:size], x[size:]
    near_part, far_part = pack(x, near, far, rows, size)
    y, z = swapped(near_part, "blk", 1), moved(far_part, "blk", inward)
    z_more = moved(x_more, "blk", inward)

    def round_of(zk, xk, *earlier):
        zk, xk = after((zk, xk), *earlier)
        return swapped(zk, "blk", 1), moved(xk, "blk", outward)

    u_more, w_more = round_of(z_more, x_more, z, z_more)

    always = near[0, 0].astype(F32) < 1e30

    def summed(keep, send, near, far, near_part, far_part):
        mine, send = fold(keep, swapped(send, "orb", 1))
        return tuple(weigh(mine, swapped(send, "orb", 2), near, far, near_part, far_part))

    def no_sum(*_):
        return tuple(jnp.zeros((rows // 4, n * rows), BF16) for n in (2, 1, 1))

    keep, send = gram_last(x, y, z, z_more, gram_first(x, z, size))
    ahead, xz, zy = lax.cond(always, summed, no_sum, keep, send, near, far, y, z)
    back_xz = moved(xz, "blk", outward)
    zy_far = moved(zy, "blk", [p for p in outward if p[0] % 2 == 0])
    zy_near = moved(zy, "blk", [(b, b ^ 1) for b in range(0, blocks, 2)])
    u_half, w_half = round_of(z[:size], x_half, back_xz)
    zy_far, zy_near, back_xz = after((zy_far, zy_near, back_xz), u_more, w_more)
    back = gather(jnp.concatenate([back_xz, jnp.where(even, zy_far, zy_near)], 1))

    more = rows - size
    places, place = [], 0
    for height in (rows, size, more, more, more):
        places.append((place, place + height))
        place += height
    values = y, z, z_more, u_more, w_more
    total, weights = apply_most(places, size, gather(ahead), back, values)
    return apply_last(weights, total, u_half, w_half)


def from_behind(value, by):
    devices = lax.axis_size("blk")
    return lax.ppermute(value, "blk", [(i, (i + by) % devices) for i in range(devices)])


def direct(x, near, far, far_offset):
    total = jnp.zeros(x.shape, F32)
    for offset, slab in ((1, near), (far_offset, far)):
        later = from_behind(x, -offset)
        earlier, earlier_slab = from_behind((x, slab), offset)
        for other, scale in ((later, slab), (earlier, earlier_slab.T)):
            gram = lax.psum(outer(x, other), "orb")
            weighted = (gram * scale.astype(F32)).astype(BF16)
            total += inner(weighted, other)
    return total.astype(BF16)


def per_device(orbitals, coulomb_near, coulomb_far):
    far_offset = lax.axis_size("blk") // 4
    if far_offset == 2 and lax.axis_size("orb") == 4:
        return relayed(orbitals, coulomb_near, coulomb_far)
    return direct(orbitals, coulomb_near, coulomb_far, far_offset)


def solution(mesh):
    return jax.shard_map(
        per_device,
        mesh=mesh,
        in_specs=(P("blk", "orb"), P("blk", None), P("blk", None)),
        out_specs=P("blk", "orb"),
        check_vma=False,
    )
```

time: 256 us -> 122 us (0.48)
  waiting for transfers between devices: 207 us -> 72.6 us
  matrix products: 21.7 us -> 0 us
  Pallas kernels: 0 us -> 16.2 us
  between operations: 13.5 us -> 0.77 us
  starting transfers between devices: 12.6 us -> 25.1 us
  local copies, waits for them, and re-layouts: 1.61 us -> 5.82 us
    psum x1 -> x0, waiting for transfers between devices: 81.9 us -> none  [weigh(): gram = lax.psum(partial_gram, 'orb')]
    ppermute x6 -> x18, waiting for transfers between devices: 125 us -> 72.6 us  [the longest x7 46.6 us: moved(): return lax.ppermute(value, axis, pairs)]
    dot_general x8 -> x0, matrix products: 21.7 us -> none  [the longest x4 11.5 us: contract_last(): lax.dot_general(left, right, (((1,), (1,)), ((), ())), preferred_element_...]
    pallas_call x0 -> x7, Pallas kernels: none -> 16.2 us  [the longest x1 5.05 us: apply_most(): pl.pallas_call(functools.partial(most_kernel, places), in_specs=[VMEM] *...]
    ppermute x6 -> x18, starting transfers between devices: 12.6 us -> 25.1 us  [the longest x7 16.1 us: moved(): return lax.ppermute(value, axis, pairs)]
    slice x0 -> x3, local copies, waits for them, and re-layouts: none -> 4.2 us  [the longest x1 1.59 us: relayed(): x_half, x_more = (x[:size], x[size:])]
  transfers between devices with their start and end apart: 7 -> 18, of which waited for: 3 -> 7; matrix products, arithmetic and copies ran while one was open for 6% -> 4% of each run, Pallas kernels for 0% -> 10%
where the time goes in v1:
time: 122 us
  waiting for transfers between devices  72.6 us (60%)
  starting transfers between devices  25.1 us (21%)
  Pallas kernels  16.2 us (13%)
  local copies, waits for them, and re-layouts  5.82 us (5%)
    ppermute x7, waiting for transfers between devices, moved(): return lax.ppermute(value, axis, pairs)  46.6 us
    ppermute x11, waiting for transfers between devices, swapped(): lax.ppermute(value, axis, [(i, i ^ distance) for i in range(devices)])  26.1 us
    ppermute x7, starting transfers between devices, moved(): return lax.ppermute(value, axis, pairs)  16.1 us
    ppermute x11, starting transfers between devices, swapped(): lax.ppermute(value, axis, [(i, i ^ distance) for i in range(devices)])  9 us
    pallas_call x1, Pallas kernels, apply_most(): pl.pallas_call(functools.partial(most_kernel, places), in_specs=[VMEM] *...  5.05 us
    pallas_call x1, Pallas kernels, gram_last(): pl.pallas_call(gram_last_kernel, in_specs=[VMEM] * 5, out_specs=[VMEM] *...  4.36 us
  transfers between devices with their start and end apart: 18, of which 7 were waited for; matrix products, arithmetic and copies ran while one was open for 4% of the time, Pallas kernels for 10%

profile of v1, /device:TPU:0, one launch (start us, length us, event | category | flops | bytes accessed | tf_op | source)
XLA Modules:
  0.0 121.5 jit_solution(8104917733251148114)
XLA Ops:
  0.0 1.6 %copy-done = bf16[512,2048]{1,0:T(8,128)(2,1)S(1)} copy-done((bf16[512,2048]{1,0:T(8,128)(2,1)S(1)}, bf16[512,2048]{1,0:T(8,128)(2,1)}, u32[]{:S(2)}) %copy-start) | copy-done | bytes 2097176
  1.6 1.6 %shard_map.37 = (bf16[544,2048]{1,0:T(8,128)(2,1)S(1)}, bf16[288,2048]{1,0:T(8,128)(2,1)S(1)}) custom-call(bf16[512,2048]{1,0:T(8,128)(2,1)S(1)} %copy-done, bf16[512,512]{1,0:T(8,128)(2,1)} %near.1, bf16[512,512]{1,0:T(8,128)(2,1)} %far.1), custom_call_target="tpu_custom_call" | custom-call | bytes 6291456 | tf_op jit(solution)/shard_map/pallas_call | solution.py:71
  3.2 5.1 %collective-permute-start.3 = (bf16[288,2048]{1,0:T(8,128)(2,1)S(1)}, bf16[288,2048]{1,0:T(8,128)(2,1)S(1)}, u32[]{:S(2)}, u32[]{:S(2)}) collective-permute-start(bf16[288,2048]{1,0:T(8,128)(2,1)S(1)} %get-tuple-element.42), channel_id=1, source_target_pairs={{0,24},{4,12},{8,0},{12,20},{16,8},{20,28},{24,16},{28,4},{1,25},{... | collective-permute-start | bytes 3538952 | tf_op jit(solution)/shard_map/ppermute | solution.py:33
  8.3 1.6 %fusion = (bf16[256,2048]{1,0:T(8,128)(2,1)}, bf16[256,2048]{1,0:T(8,128)(2,1)}) fusion(bf16[512,2048]{1,0:T(8,128)(2,1)S(1)} %copy-done.1), kind=kLoop, calls=%fused_computation.2 | loop fusion | bytes 4194304 | tf_op jit(solution)/shard_map/slice | solution.py:289
  9.9 1.7 %collective-permute-start.4 = (bf16[256,2048]{1,0:T(8,128)(2,1)}, bf16[256,2048]{1,0:T(8,128)(2,1)S(1)}, u32[]{:S(2)}, u32[]{:S(2)}) collective-permute-start(bf16[256,2048]{1,0:T(8,128)(2,1)} %get-tuple-element.49), channel_id=1, source_target_pairs={{0,24},{4,12},{8,0},{12,20},{16,8},{20,28},{24,16},{28,4},{1,25},{... | collective-permute-start | bytes 3145736 | tf_op jit(solution)/shard_map/ppermute | solution.py:33
  11.6 44.5 %collective-permute-done.4.z_more.refs_10_ = bf16[256,2048]{1,0:T(8,128)(2,1)S(1)} collective-permute-done((bf16[256,2048]{1,0:T(8,128)(2,1)}, bf16[256,2048]{1,0:T(8,128)(2,1)S(1)}, u32[]{:S(2)}, u32[]{:S(2)}) %collective-permute-start.4) | collective-permute-done | bytes 1048608 | tf_op jit(solution)/shard_map/ppermute | solution.py:33
  56.1 2.2 %collective-permute-start.11 = (bf16[256,2048]{1,0:T(8,128)(2,1)S(1)}, bf16[256,2048]{1,0:T(8,128)(2,1)S(1)}, u32[]{:S(2)}, u32[]{:S(2)}) collective-permute-start(bf16[256,2048]{1,0:T(8,128)(2,1)S(1)} %collective-permute-done.4.z_more.refs_10_), channel_id=1, source_target_pairs={{0,4},{4,0},{8,12},{12,8},{16,20},{20,16},{24,28},{28,24},{1,5},{5... | collective-permute-start | bytes 3145736 | tf_op jit(solution)/shard_map/ppermute | solution.py:38
  60.9 4.4 %shard_map.39 = (f32[256,1536]{1,0:T(8,128)}, bf16[256,1536]{1,0:T(8,128)(2,1)}) custom-call(bf16[512,2048]{1,0:T(8,128)(2,1)S(1)} %copy-done.1, bf16[544,2048]{1,0:T(8,128)(2,1)S(1)} %collective-permute-done.2.y.refs_8_, bf16[288,2048]{1,0:T(8,128)(2,1)S(1)} %collective-permute-done.3.z.refs_9_, ...), custom_call_target="tpu_custom_call" | custom-call | tf_op jit(solution)/shard_map/pallas_call | solution.py:130
  65.3 16.2 %conditional.1 = ((bf16[128,1024]{1,0:T(8,128)(2,1)S(1)}, bf16[128,512]{1,0:T(8,128)(2,1)}, bf16[128,512]{1,0:T(8,128)(2,1)})) conditional(s32[]{:T(128)} %bitcast, () %tuple.15, (bf16[256,1536]{1,0:T(8,128)(2,1)}, f32[256,1536]{1,0:T(8,128)}, bf16[512,512]{1,0:T(8,128)(2,1)}, bf16[512,512]{1,0:T(8,128)(2,1)}, bf16[544,2048]{1,0:T(8,128)(2,1)S(1)}, ...), branch_computations={%region_0.1_spmd, %region_1.2_spmd} | conditional | flops 1179648 | bytes 15073424 | solution.py:310
  65.3 2.5 %collective-permute-done.other = bf16[256,1536]{1,0:T(8,128)(2,1)S(1)} collective-permute-done((bf16[256,1536]{1,0:T(8,128)(2,1)}, bf16[256,1536]{1,0:T(8,128)(2,1)S(1)}, u32[]{:S(2)}, u32[]{:S(2)}) %collective-permute-start) | collective-permute-done | bytes 786464 | tf_op jit(solution)/shard_map/cond/branch_1_fun/ppermute | solution.py:38
  67.8 1.5 %branch_1_fun.2 = (f32[128,1536]{1,0:T(8,128)S(1)}, bf16[128,1536]{1,0:T(8,128)(2,1)S(1)}) custom-call(f32[256,1536]{1,0:T(8,128)} %get-tuple-element.17.keep, bf16[256,1536]{1,0:T(8,128)(2,1)S(1)} %collective-permute-done.other), custom_call_target="tpu_custom_call" | custom-call | flops 786432 | bytes 3538944 | tf_op jit(solution)/shard_map/cond/branch_1_fun/pallas_call | solution.py:149
  69.4 1.6 %collective-permute-start.1 = (bf16[128,1536]{1,0:T(8,128)(2,1)S(1)}, bf16[128,1536]{1,0:T(8,128)(2,1)S(1)}, u32[]{:S(2)}, u32[]{:S(2)}) collective-permute-start(bf16[128,1536]{1,0:T(8,128)(2,1)S(1)} %get-tuple-element.20), channel_id=1, source_target_pairs={{0,2},{1,3},{2,0},{3,1},{4,6},{5,7},{6,4},{7,5},{8,10},{9,11},{10,... | collective-permute-start | bytes 1179656 | tf_op jit(solution)/shard_map/cond/branch_1_fun/ppermute | solution.py:38
  70.9 9.7 %collective-permute-done.1.other = bf16[128,1536]{1,0:T(8,128)(2,1)S(1)} collective-permute-done((bf16[128,1536]{1,0:T(8,128)(2,1)S(1)}, bf16[128,1536]{1,0:T(8,128)(2,1)S(1)}, u32[]{:S(2)}, u32[]{:S(2)}) %collective-permute-start.1) | collective-permute-done | bytes 393248 | tf_op jit(solution)/shard_map/cond/branch_1_fun/ppermute | solution.py:38
  82.7 3.8 %collective-permute-start.8 = (bf16[128,512]{1,0:T(8,128)(2,1)}, bf16[128,512]{1,0:T(8,128)(2,1)S(1)}, u32[]{:S(2)}, u32[]{:S(2)}) collective-permute-start(bf16[128,512]{1,0:T(8,128)(2,1)} %get-tuple-element.46), channel_id=1, source_target_pairs={{0,8},{8,16},{16,24},{24,0},{1,9},{9,17},{17,25},{25,1},{2,10},{10... | collective-permute-start | bytes 393224 | tf_op jit(solution)/shard_map/ppermute | solution.py:33
  86.6 2.2 %collective-permute-start.9 = (bf16[128,512]{1,0:T(8,128)(2,1)}, bf16[128,512]{1,0:T(8,128)(2,1)}, u32[]{:S(2)}, u32[]{:S(2)}) collective-permute-start(bf16[128,512]{1,0:T(8,128)(2,1)} %get-tuple-element.46), channel_id=1, source_target_pairs={{0,4},{8,12},{16,20},{24,28},{1,5},{9,13},{17,21},{25,29},{2,6},{1... | collective-permute-start | bytes 393224 | tf_op jit(solution)/shard_map/ppermute | solution.py:33
  90.2 1.6 %collective-permute-start.5 = (bf16[128,1024]{1,0:T(8,128)(2,1)S(1)}, bf16[128,1024]{1,0:T(8,128)(2,1)S(1)}, u32[]{:S(2)}, u32[]{:S(2)}) collective-permute-start(bf16[128,1024]{1,0:T(8,128)(2,1)S(1)} %get-tuple-element.45.refs_0_), channel_id=1, source_target_pairs={{0,2},{1,3},{2,0},{3,1},{4,6},{5,7},{6,4},{7,5},{8,10},{9,11},{10,... | collective-permute-start | bytes 786440 | tf_op jit(solution)/shard_map/ppermute | solution.py:38
  91.8 1.6 %collective-permute-start.16 = (bf16[256,2048]{1,0:T(8,128)(2,1)S(1)}, bf16[256,2048]{1,0:T(8,128)(2,1)S(1)}, u32[]{:S(2)}, u32[]{:S(2)}) collective-permute-start(bf16[256,2048]{1,0:T(8,128)(2,1)S(1)} %slice.16), channel_id=1, source_target_pairs={{0,4},{4,0},{8,12},{12,8},{16,20},{20,16},{24,28},{28,24},{1,5},{5... | collective-permute-start | bytes 3145736 | tf_op jit(solution)/shard_map/ppermute | solution.py:38
  93.3 2.0 %collective-permute-start.17 = (bf16[256,2048]{1,0:T(8,128)(2,1)}, bf16[256,2048]{1,0:T(8,128)(2,1)S(1)}, u32[]{:S(2)}, u32[]{:S(2)}) collective-permute-start(bf16[256,2048]{1,0:T(8,128)(2,1)} %get-tuple-element.56), channel_id=1, source_target_pairs={{0,8},{4,28},{8,16},{12,4},{16,24},{20,12},{24,0},{28,20},{1,9},{5... | collective-permute-start | bytes 3145736 | tf_op jit(solution)/shard_map/ppermute | solution.py:33
  96.3 1.6 %collective-permute-start.13 = (bf16[128,1024]{1,0:T(8,128)(2,1)S(1)}, bf16[128,1024]{1,0:T(8,128)(2,1)S(1)}, u32[]{:S(2)}, u32[]{:S(2)}) collective-permute-start(bf16[128,1024]{1,0:T(8,128)(2,1)S(1)} %pad_maximum_fusion.refs_4_), channel_id=1, source_target_pairs={{0,2},{1,3},{2,0},{3,1},{4,6},{5,7},{6,4},{7,5},{8,10},{9,11},{10,... | collective-permute-start | bytes 786440 | tf_op jit(solution)/shard_map/ppermute | solution.py:38
  98.4 5.0 %collective-permute-done.13.refs_5_ = bf16[128,1024]{1,0:T(8,128)(2,1)S(1)} collective-permute-done((bf16[128,1024]{1,0:T(8,128)(2,1)S(1)}, bf16[128,1024]{1,0:T(8,128)(2,1)S(1)}, u32[]{:S(2)}, u32[]{:S(2)}) %collective-permute-start.13) | collective-permute-done | bytes 262176 | tf_op jit(solution)/shard_map/ppermute | solution.py:38
  104.9 5.1 %shard_map.40 = (f32[512,2048]{1,0:T(8,128)S(1)}, bf16[512,512]{1,0:T(8,128)(2,1)S(1)}) custom-call(bf16[128,1024]{1,0:T(8,128)(2,1)S(1)} %get-tuple-element.45.refs_0_, bf16[128,1024]{1,0:T(8,128)(2,1)S(1)} %collective-permute-done.5.refs_1_, bf16[128,1024]{1,0:T(8,128)(2,1)S(1)} %collective-permute-done.6.refs_2_, ...), custom_call_target="tpu_custom_call" | custom-call | flops 3221225472 | bytes 12582912 | tf_op jit(solution)/shard_map/pallas_call | solution.py:233
  110.0 7.4 %collective-permute-done.16.u = bf16[256,2048]{1,0:T(8,128)(2,1)S(1)} collective-permute-done((bf16[256,2048]{1,0:T(8,128)(2,1)S(1)}, bf16[256,2048]{1,0:T(8,128)(2,1)S(1)}, u32[]{:S(2)}, u32[]{:S(2)}) %collective-permute-start.16) | collective-permute-done | bytes 1048608 | tf_op jit(solution)/shard_map/ppermute | solution.py:38
  117.4 2.1 %collective-permute-done.17.w = bf16[256,2048]{1,0:T(8,128)(2,1)S(1)} collective-permute-done((bf16[256,2048]{1,0:T(8,128)(2,1)}, bf16[256,2048]{1,0:T(8,128)(2,1)S(1)}, u32[]{:S(2)}, u32[]{:S(2)}) %collective-permute-start.17) | collective-permute-done | bytes 1048608 | tf_op jit(solution)/shard_map/ppermute | solution.py:33
  119.5 2.1 %shard_map.41 = bf16[512,2048]{1,0:T(8,128)(2,1)} custom-call(bf16[512,512]{1,0:T(8,128)(2,1)S(1)} %get-tuple-element.53.weights, f32[512,2048]{1,0:T(8,128)S(1)} %get-tuple-element.54.total, bf16[256,2048]{1,0:T(8,128)(2,1)S(1)} %collective-permute-done.16.u, bf16[256,2048]{1,0:T(8,128)(2,1)S(1)} %collective-permute-done.17.w), custom_call_target="tpu_custom_call" | custom-call | flops 1073741824 | bytes 8388608 | tf_op jit(solution)/shard_map/pallas_call | solution.py:265
  (39 shorter events, 8.6 us)
Async XLA Ops:
  1.6 6.7 %copy-start.1 = (bf16[512,2048]{1,0:T(8,128)(2,1)S(1)}, bf16[512,2048]{1,0:T(8,128)(2,1)}, u32[]{:S(2)}) copy-start(bf16[512,2048]{1,0:T(8,128)(2,1)} %x.5) | copy-start | bytes 6291460
  3.2 52.9 %collective-permute-start.3 = (bf16[288,2048]{1,0:T(8,128)(2,1)S(1)}, bf16[288,2048]{1,0:T(8,128)(2,1)S(1)}, u32[]{:S(2)}, u32[]{:S(2)}) collective-permute-start(bf16[288,2048]{1,0:T(8,128)(2,1)S(1)} %get-tuple-element.42), channel_id=1, source_target_pairs={{0,24},{4,12},{8,0},{12,20},{16,8},{20,28},{24,16},{28,4},{1,25},{... | collective-permute-start | bytes 3538952 | tf_op jit(solution)/shard_map/ppermute | solution.py:33
  8.3 52.6 %collective-permute-start.2 = (bf16[544,2048]{1,0:T(8,128)(2,1)S(1)}, bf16[544,2048]{1,0:T(8,128)(2,1)S(1)}, u32[]{:S(2)}, u32[]{:S(2)}) collective-permute-start(bf16[544,2048]{1,0:T(8,128)(2,1)S(1)} %get-tuple-element.41), channel_id=1, source_target_pairs={{0,4},{4,0},{8,12},{12,8},{16,20},{20,16},{24,28},{28,24},{1,5},{5... | collective-permute-start | bytes 6684680 | tf_op jit(solution)/shard_map/ppermute | solution.py:38
  9.9 46.2 %collective-permute-start.4 = (bf16[256,2048]{1,0:T(8,128)(2,1)}, bf16[256,2048]{1,0:T(8,128)(2,1)S(1)}, u32[]{:S(2)}, u32[]{:S(2)}) collective-permute-start(bf16[256,2048]{1,0:T(8,128)(2,1)} %get-tuple-element.49), channel_id=1, source_target_pairs={{0,24},{4,12},{8,0},{12,20},{16,8},{20,28},{24,16},{28,4},{1,25},{... | collective-permute-start | bytes 3145736 | tf_op jit(solution)/shard_map/ppermute | solution.py:33
  56.1 9.1 %copy-start.2 = (bf16[288,2048]{1,0:T(8,128)(2,1)}, bf16[288,2048]{1,0:T(8,128)(2,1)S(1)}, u32[]{:S(2)}) copy-start(bf16[288,2048]{1,0:T(8,128)(2,1)S(1)} %collective-permute-done.3.z.refs_9_) | copy-start | bytes 3538948
  56.1 34.1 %collective-permute-start.11 = (bf16[256,2048]{1,0:T(8,128)(2,1)S(1)}, bf16[256,2048]{1,0:T(8,128)(2,1)S(1)}, u32[]{:S(2)}, u32[]{:S(2)}) collective-permute-start(bf16[256,2048]{1,0:T(8,128)(2,1)S(1)} %collective-permute-done.4.z_more.refs_10_), channel_id=1, source_target_pairs={{0,4},{4,0},{8,12},{12,8},{16,20},{20,16},{24,28},{28,24},{1,5},{5... | collective-permute-start | bytes 3145736 | tf_op jit(solution)/shard_map/ppermute | solution.py:38
  58.3 33.5 %collective-permute-start.12 = (bf16[256,2048]{1,0:T(8,128)(2,1)}, bf16[256,2048]{1,0:T(8,128)(2,1)S(1)}, u32[]{:S(2)}, u32[]{:S(2)}) collective-permute-start(bf16[256,2048]{1,0:T(8,128)(2,1)} %get-tuple-element.49), channel_id=1, source_target_pairs={{0,8},{4,28},{8,16},{12,4},{16,24},{20,12},{24,0},{28,20},{1,9},{5... | collective-permute-start | bytes 3145736 | tf_op jit(solution)/shard_map/ppermute | solution.py:33
  60.9 4.4 %copy-start.4 = (bf16[544,2048]{1,0:T(8,128)(2,1)}, bf16[544,2048]{1,0:T(8,128)(2,1)S(1)}, u32[]{:S(2)}) copy-start(bf16[544,2048]{1,0:T(8,128)(2,1)S(1)} %collective-permute-done.2.y.refs_8_) | copy-start | bytes 6684676
  65.3 15.3 %copy-start.5 = (bf16[512,512]{1,0:T(8,128)(2,1)S(1)}, bf16[512,512]{1,0:T(8,128)(2,1)}, u32[]{:S(2)}) copy-start(bf16[512,512]{1,0:T(8,128)(2,1)} %get-tuple-element.21.near) | copy-start | bytes 1572868 | tf_op jit(solution)/shard_map/cond
  65.3 15.3 %copy-start.6 = (bf16[512,512]{1,0:T(8,128)(2,1)S(1)}, bf16[512,512]{1,0:T(8,128)(2,1)}, u32[]{:S(2)}) copy-start(bf16[512,512]{1,0:T(8,128)(2,1)} %get-tuple-element.22.far) | copy-start | bytes 1572868 | tf_op jit(solution)/shard_map/cond
  65.3 2.6 %collective-permute-start = (bf16[256,1536]{1,0:T(8,128)(2,1)}, bf16[256,1536]{1,0:T(8,128)(2,1)S(1)}, u32[]{:S(2)}, u32[]{:S(2)}) collective-permute-start(bf16[256,1536]{1,0:T(8,128)(2,1)} %get-tuple-element.18), channel_id=1, source_target_pairs={{0,1},{1,0},{2,3},{3,2},{4,5},{5,4},{6,7},{7,6},{8,9},{9,8},{10,11... | collective-permute-start | bytes 2359304 | tf_op jit(solution)/shard_map/cond/branch_1_fun/ppermute | solution.py:38
  69.4 11.2 %collective-permute-start.1 = (bf16[128,1536]{1,0:T(8,128)(2,1)S(1)}, bf16[128,1536]{1,0:T(8,128)(2,1)S(1)}, u32[]{:S(2)}, u32[]{:S(2)}) collective-permute-start(bf16[128,1536]{1,0:T(8,128)(2,1)S(1)} %get-tuple-element.20), channel_id=1, source_target_pairs={{0,2},{1,3},{2,0},{3,1},{4,6},{5,7},{6,4},{7,5},{8,10},{9,11},{10,... | collective-permute-start | bytes 1179656 | tf_op jit(solution)/shard_map/cond/branch_1_fun/ppermute | solution.py:38
  81.5 10.3 %collective-permute-start.10 = (bf16[128,512]{1,0:T(8,128)(2,1)}, bf16[128,512]{1,0:T(8,128)(2,1)}, u32[]{:S(2)}, u32[]{:S(2)}) collective-permute-start(bf16[128,512]{1,0:T(8,128)(2,1)} %get-tuple-element.47), channel_id=1, source_target_pairs={{0,8},{4,28},{8,16},{12,4},{16,24},{20,12},{24,0},{28,20},{1,9},{5... | collective-permute-start | bytes 393224 | tf_op jit(solution)/shard_map/ppermute | solution.py:33
  82.7 9.0 %collective-permute-start.8 = (bf16[128,512]{1,0:T(8,128)(2,1)}, bf16[128,512]{1,0:T(8,128)(2,1)S(1)}, u32[]{:S(2)}, u32[]{:S(2)}) collective-permute-start(bf16[128,512]{1,0:T(8,128)(2,1)} %get-tuple-element.46), channel_id=1, source_target_pairs={{0,8},{8,16},{16,24},{24,0},{1,9},{9,17},{17,25},{25,1},{2,10},{10... | collective-permute-start | bytes 393224 | tf_op jit(solution)/shard_map/ppermute | solution.py:33
  86.6 5.2 %collective-permute-start.9 = (bf16[128,512]{1,0:T(8,128)(2,1)}, bf16[128,512]{1,0:T(8,128)(2,1)}, u32[]{:S(2)}, u32[]{:S(2)}) collective-permute-start(bf16[128,512]{1,0:T(8,128)(2,1)} %get-tuple-element.46), channel_id=1, source_target_pairs={{0,4},{8,12},{16,20},{24,28},{1,5},{9,13},{17,21},{25,29},{2,6},{1... | collective-permute-start | bytes 393224 | tf_op jit(solution)/shard_map/ppermute | solution.py:33
  88.7 16.2 %copy-start.3 = (bf16[288,2048]{1,0:T(8,128)(2,1)S(1)}, bf16[288,2048]{1,0:T(8,128)(2,1)}, u32[]{:S(2)}) copy-start(bf16[288,2048]{1,0:T(8,128)(2,1)} %copy-done.2) | copy-start | bytes 3538948
  90.2 7.7 %collective-permute-start.5 = (bf16[128,1024]{1,0:T(8,128)(2,1)S(1)}, bf16[128,1024]{1,0:T(8,128)(2,1)S(1)}, u32[]{:S(2)}, u32[]{:S(2)}) collective-permute-start(bf16[128,1024]{1,0:T(8,128)(2,1)S(1)} %get-tuple-element.45.refs_0_), channel_id=1, source_target_pairs={{0,2},{1,3},{2,0},{3,1},{4,6},{5,7},{6,4},{7,5},{8,10},{9,11},{10,... | collective-permute-start | bytes 786440 | tf_op jit(solution)/shard_map/ppermute | solution.py:38
  91.7 6.2 %collective-permute-start.6 = (bf16[128,1024]{1,0:T(8,128)(2,1)S(1)}, bf16[128,1024]{1,0:T(8,128)(2,1)S(1)}, u32[]{:S(2)}, u32[]{:S(2)}) collective-permute-start(bf16[128,1024]{1,0:T(8,128)(2,1)S(1)} %get-tuple-element.45.refs_0_), channel_id=1, source_target_pairs={{0,1},{1,0},{2,3},{3,2},{4,5},{5,4},{6,7},{7,6},{8,9},{9,8},{10,11... | collective-permute-start | bytes 786440 | tf_op jit(solution)/shard_map/ppermute | solution.py:38
  91.8 25.6 %collective-permute-start.16 = (bf16[256,2048]{1,0:T(8,128)(2,1)S(1)}, bf16[256,2048]{1,0:T(8,128)(2,1)S(1)}, u32[]{:S(2)}, u32[]{:S(2)}) collective-permute-start(bf16[256,2048]{1,0:T(8,128)(2,1)S(1)} %slice.16), channel_id=1, source_target_pairs={{0,4},{4,0},{8,12},{12,8},{16,20},{20,16},{24,28},{28,24},{1,5},{5... | collective-permute-start | bytes 3145736 | tf_op jit(solution)/shard_map/ppermute | solution.py:38
  93.3 26.1 %collective-permute-start.17 = (bf16[256,2048]{1,0:T(8,128)(2,1)}, bf16[256,2048]{1,0:T(8,128)(2,1)S(1)}, u32[]{:S(2)}, u32[]{:S(2)}) collective-permute-start(bf16[256,2048]{1,0:T(8,128)(2,1)} %get-tuple-element.56), channel_id=1, source_target_pairs={{0,8},{4,28},{8,16},{12,4},{16,24},{20,12},{24,0},{28,20},{1,9},{5... | collective-permute-start | bytes 3145736 | tf_op jit(solution)/shard_map/ppermute | solution.py:33
  96.3 7.0 %collective-permute-start.13 = (bf16[128,1024]{1,0:T(8,128)(2,1)S(1)}, bf16[128,1024]{1,0:T(8,128)(2,1)S(1)}, u32[]{:S(2)}, u32[]{:S(2)}) collective-permute-start(bf16[128,1024]{1,0:T(8,128)(2,1)S(1)} %pad_maximum_fusion.refs_4_), channel_id=1, source_target_pairs={{0,2},{1,3},{2,0},{3,1},{4,6},{5,7},{6,4},{7,5},{8,10},{9,11},{10,... | collective-permute-start | bytes 786440 | tf_op jit(solution)/shard_map/ppermute | solution.py:38
  97.9 5.5 %collective-permute-start.14 = (bf16[128,1024]{1,0:T(8,128)(2,1)S(1)}, bf16[128,1024]{1,0:T(8,128)(2,1)S(1)}, u32[]{:S(2)}, u32[]{:S(2)}) collective-permute-start(bf16[128,1024]{1,0:T(8,128)(2,1)S(1)} %pad_maximum_fusion.refs_4_), channel_id=1, source_target_pairs={{0,1},{1,0},{2,3},{3,2},{4,5},{5,4},{6,7},{7,6},{8,9},{9,8},{10,11... | collective-permute-start | bytes 786440 | tf_op jit(solution)/shard_map/ppermute | solution.py:38
  97.9 5.5 %collective-permute-start.7 = (bf16[128,1024]{1,0:T(8,128)(2,1)S(1)}, bf16[128,1024]{1,0:T(8,128)(2,1)S(1)}, u32[]{:S(2)}, u32[]{:S(2)}) collective-permute-start(bf16[128,1024]{1,0:T(8,128)(2,1)S(1)} %collective-permute-done.5.refs_1_), channel_id=1, source_target_pairs={{0,1},{1,0},{2,3},{3,2},{4,5},{5,4},{6,7},{7,6},{8,9},{9,8},{10,11... | collective-permute-start | bytes 786440 | tf_op jit(solution)/shard_map/ppermute | solution.py:38
  103.4 1.5 %collective-permute-start.15 = (bf16[128,1024]{1,0:T(8,128)(2,1)S(1)}, bf16[128,1024]{1,0:T(8,128)(2,1)S(1)}, u32[]{:S(2)}, u32[]{:S(2)}) collective-permute-start(bf16[128,1024]{1,0:T(8,128)(2,1)S(1)} %collective-permute-done.13.refs_5_), channel_id=1, source_target_pairs={{0,1},{1,0},{2,3},{3,2},{4,5},{5,4},{6,7},{7,6},{8,9},{9,8},{10,11... | collective-permute-start | bytes 786440 | tf_op jit(solution)/shard_map/ppermute | solution.py:38
  (1 other events, 1.6 us)

commit v2 on v1

v2 whole, which is shorter than its diff:
```python
import functools

import jax
import jax.numpy as jnp
from jax import lax
from jax.experimental import pallas as pl
from jax.experimental.pallas import tpu as pltpu
from jax.sharding import PartitionSpec as P

MIB = 1024 * 1024
F32, BF16 = jnp.float32, jnp.bfloat16
VMEM = pl.BlockSpec(memory_space=pltpu.VMEM)
ANY = pl.BlockSpec(memory_space=pl.ANY)


def shape(rows, columns, kind):
    return jax.ShapeDtypeStruct((rows, columns), kind)


def cost(flops, moved_bytes):
    return pl.CostEstimate(flops=flops, bytes_accessed=moved_bytes, transcendentals=0)


def outer(left, right):
    return lax.dot_general(left, right, (((1,), (1,)), ((), ())), preferred_element_type=F32)


def inner(left, right):
    return jnp.dot(left, right, preferred_element_type=F32)


def moved(value, axis, pairs):
    return lax.ppermute(value, axis, pairs)


def swapped(value, axis, distance):
    devices = lax.axis_size(axis)
    return lax.ppermute(value, axis, [(i, i ^ distance) for i in range(devices)])


def after(values, *earlier):
    return lax.optimization_barrier((*values, *earlier))[: len(values)]


def quarter_index(distance=0):
    me = lax.axis_index("orb")
    return ((me % 2) * 2 + me // 2) ^ distance


def quarter_rows(rows, distance=0):
    size = rows // 4
    return pl.ds(pl.multiple_of(quarter_index(distance) * size, size), size)


def prepare_kernel(x, near, far, upper, lower, near_out, far_out, flag):
    rows = near.shape[0]
    here = quarter_rows(rows)
    upper[...] = x[: upper.shape[0], :]
    lower[...] = x[upper.shape[0] :, :]
    near_out[...] = near[:, here]
    far_out[...] = far[:, here]
    flag[0, 0] = (jnp.max(near[:8, :128].astype(F32)) < 1e30).astype(jnp.int32)


def prepare(x, near, far, first):
    rows, columns = x.shape
    return pl.pallas_call(
        prepare_kernel,
        in_specs=[VMEM] * 3,
        out_specs=[VMEM] * 4 + [pl.BlockSpec(memory_space=pltpu.SMEM)],
        out_shape=[shape(first, columns, BF16), shape(rows - first, columns, BF16)]
        + [shape(rows, rows // 4, BF16)] * 2
        + [shape(1, 1, jnp.int32)],
        compiler_params=pltpu.CompilerParams(vmem_limit_bytes=12 * MIB),
        cost_estimate=cost(0, 6 * rows * columns),
    )(x, near, far)


def gram_kernel(x, y, z, keep, send, total):
    rows = x.shape[0]
    for i, (left, right) in enumerate(((x, y), (x, z), (z, y))):
        total[:, i * rows : (i + 1) * rows] = outer(left[...], right[...])
    quarter = rows // 4
    for distance in range(4):
        target, kind = (keep, F32) if distance < 2 else (send, BF16)
        place = distance % 2 * quarter
        target[place : place + quarter, :] = total[quarter_rows(rows, distance), :].astype(kind)


def gram(x, y, z):
    rows = x.shape[0]
    return pl.pallas_call(
        gram_kernel,
        in_specs=[VMEM] * 3,
        out_specs=[VMEM] * 2,
        out_shape=[shape(rows // 2, 3 * rows, F32), shape(rows // 2, 3 * rows, BF16)],
        scratch_shapes=[pltpu.VMEM((rows, 3 * rows), F32)],
        compiler_params=pltpu.CompilerParams(vmem_limit_bytes=20 * MIB),
        cost_estimate=cost(0, 0),
    )(x, y, z)


def fold_kernel(keep, other, mine, send):
    size = mine.shape[0]
    mine[...] = keep[:size, :] + other[:size, :].astype(F32)
    send[...] = (keep[size:, :] + other[size:, :].astype(F32)).astype(BF16)


def fold(keep, other):
    size, width = keep.shape[0] // 2, keep.shape[1]
    return pl.pallas_call(
        fold_kernel,
        in_specs=[VMEM] * 2,
        out_specs=[VMEM] * 2,
        out_shape=[shape(size, width, F32), shape(size, width, BF16)],
        compiler_params=pltpu.CompilerParams(vmem_limit_bytes=8 * MIB),
        cost_estimate=cost(4 * size * width, 18 * size * width),
    )(keep, other)


def weigh_kernel(mine, other, near, far, near_other, far_other, ahead, xz, zy):
    rows = near.shape[0]
    here = quarter_rows(rows)
    even = lax.axis_index("blk") % 2 == 0
    gram = mine[...] + other[...].astype(F32)
    near_turned = near_other[...].astype(F32).T
    far_turned = far_other[...].astype(F32).T
    near_slab = jnp.where(even, near[here, :].astype(F32), near_turned)
    far_slab = jnp.where(even, far[here, :].astype(F32), far_turned)
    ahead[:, :rows] = (gram[:, :rows] * near_slab).astype(BF16)
    weighted = (gram[:, rows : 2 * rows] * far_slab).astype(BF16)
    ahead[:, rows:] = weighted
    xz[...] = weighted
    zy[...] = (gram[:, 2 * rows :] * near_turned).astype(BF16)


def weigh(mine, other, near, far, near_other, far_other):
    size, rows = mine.shape[0], near.shape[0]
    return pl.pallas_call(
        weigh_kernel,
        in_specs=[VMEM] * 6,
        out_specs=[VMEM] * 3,
        out_shape=[shape(size, 2 * rows, BF16), shape(size, rows, BF16), shape(size, rows, BF16)],
        compiler_params=pltpu.CompilerParams(vmem_limit_bytes=8 * MIB),
        cost_estimate=cost(6 * size * rows, 40 * size * rows),
    )(mine, other, near, far, near_other, far_other)


def most_kernel(places, firsts, *refs):
    ahead, back, values = refs[:4], refs[4:8], refs[8 : 8 + len(places)]
    out, kept, weights, held, arrived = refs[8 + len(values) :]
    rows, columns = out.shape
    size, tiles = rows // 4, 4
    copies = []
    for i, (start, stop) in enumerate(places):
        source = values[i].at[: stop - start, :]
        copies.append(pltpu.make_async_copy(source, held.at[start:stop, :], arrived.at[i]))
        copies[-1].start()

    even = lax.axis_index("blk") % 2 == 0
    for distance in range(4):
        weights[quarter_rows(rows, distance), : 2 * rows] = ahead[distance][...]
    for distance in range(4):
        here = quarter_rows(rows, distance)
        weights[:, pl.ds(pl.multiple_of(3 * rows + here.start, size), size)] = (
            back[distance][:, :rows].astype(F32).T.astype(BF16)
        )
        near = back[distance][:, rows:]

        @pl.when(even)
        def _():
            weights[here, 2 * rows : 3 * rows] = near

        @pl.when(jnp.logical_not(even))
        def _():
            weights[:, pl.ds(pl.multiple_of(2 * rows + here.start, size), size)] = (
                near.astype(F32).T.astype(BF16)
            )

    put, place = 0, 2 * rows
    for i, first in zip((2, 3), firsts):
        kept[:, put : put + first] = weights[:, i * rows : i * rows + first]
        there = slice(place, place + rows - first)
        weights[:, there] = weights[:, i * rows + first : (i + 1) * rows]
        put, place = put + first, place + rows - first
    for copy in copies:
        copy.wait()
    for k in range(tiles):
        here = slice(k * columns // tiles, (k + 1) * columns // tiles)
        out[:, here] = inner(weights[:, :place], held[:, here])


def apply_most(places, firsts, ahead, back, values):
    rows, columns = ahead[0].shape[0] * 4, values[0].shape[1]
    return pl.pallas_call(
        functools.partial(most_kernel, places, firsts),
        in_specs=[VMEM] * 8 + [ANY] * len(values),
        out_specs=[VMEM] * 2,
        out_shape=[shape(rows, columns, F32), shape(rows, sum(firsts), BF16)],
        scratch_shapes=[
            pltpu.VMEM((rows, 4 * rows), BF16),
            pltpu.VMEM((4 * rows - sum(firsts), columns), BF16),
            pltpu.SemaphoreType.DMA((len(values),)),
        ],
        compiler_params=pltpu.CompilerParams(vmem_limit_bytes=22 * MIB),
        cost_estimate=cost(0, 0),
    )(*ahead, *back, *values)


def last_kernel(weights, total, u, w, out, result, left):
    rows, columns = out.shape
    last, tiles = u.shape[0], 4
    writes = []
    for k in range(tiles):
        here = slice(k * columns // tiles, (k + 1) * columns // tiles)
        added = inner(weights[:, :last], u[:, here]) + inner(weights[:, last:], w[:, here])
        result[:, here] = (total[:, here] + added).astype(BF16)
        writes.append(pltpu.make_async_copy(result.at[:, here], out.at[:, here], left.at[k]))
        writes[-1].start()
    for write in writes:
        write.wait()


def apply_last(weights, total, u, w):
    rows, columns = total.shape
    last = (u.shape[0] + w.shape[0]) // 2
    return pl.pallas_call(
        last_kernel,
        in_specs=[VMEM] * 4,
        out_specs=ANY,
        out_shape=shape(rows, columns, BF16),
        scratch_shapes=[pltpu.VMEM((rows, columns), BF16), pltpu.SemaphoreType.DMA((4,))],
        compiler_params=pltpu.CompilerParams(vmem_limit_bytes=16 * MIB),
        cost_estimate=cost(4 * rows * last * columns, 6 * rows * columns + 4 * last * columns),
    )(weights, total, u, w)


def merge_kernel(xz, zy_far, zy_near, out):
    rows = xz.shape[1]
    even = lax.axis_index("blk") % 2 == 0
    out[:, :rows] = xz[...]

    @pl.when(even)
    def _():
        out[:, rows:] = zy_far[...]

    @pl.when(jnp.logical_not(even))
    def _():
        out[:, rows:] = zy_near[...]


def merge(xz, zy_far, zy_near):
    size, rows = xz.shape
    return pl.pallas_call(
        merge_kernel,
        in_specs=[VMEM] * 3,
        out_specs=VMEM,
        out_shape=shape(size, 2 * rows, BF16),
        compiler_params=pltpu.CompilerParams(vmem_limit_bytes=4 * MIB),
        cost_estimate=cost(0, 0),
    )(xz, zy_far, zy_near)


def gather(value):
    by_x = swapped(value, "orb", 2)
    return value, by_x, swapped(value, "orb", 1), swapped(by_x, "orb", 1)


def relayed(x, near, far):
    blocks = lax.axis_size("blk")
    rows, columns = x.shape
    inward = [(b, (b - 2 if b % 2 == 0 else b + 2) % blocks) for b in range(blocks)]
    outward = [(b, (b + 2 if b % 2 == 0 else b - 2) % blocks) for b in range(blocks)]

    z, y = moved(x, "blk", inward), swapped(x, "blk", 1)
    size, first = rows // 2, rows // 2 - 16
    x_half, x_more, near_part, far_part, flag = prepare(x, near, far, first)
    near_part = swapped(near_part, "blk", 1)
    far_part = moved(far_part, "blk", [p for p in inward if p[0] % 2])

    zk, xk = after((z, x_more), far_part)
    w_more = moved(xk, "blk", outward)
    u_more = swapped(after((zk[size:],), y, near_part)[0], "blk", 1)

    always = flag[0, 0] == 1

    def summed(keep, send, near, far, near_part, far_part, z):
        mine, send = fold(keep, swapped(send, "orb", 1))
        by_x = swapped(send, "orb", 2)
        return *weigh(mine, by_x, near, far, near_part, far_part), z[:size]

    def no_sum(*_):
        parts = tuple(jnp.zeros((rows // 4, n * rows), BF16) for n in (2, 1, 1))
        return *parts, jnp.zeros((size, columns), BF16)

    keep, send = gram(x, y, z)
    ahead, xz, zy, z_half = lax.cond(
        always, summed, no_sum, keep, send, near, far, near_part, far_part, z
    )
    back_xz = moved(xz, "blk", outward)
    zy_far = moved(zy, "blk", [p for p in outward if p[0] % 2 == 0])
    zy_near = moved(zy, "blk", [(b, b ^ 1) for b in range(0, blocks, 2)])
    zk, xk = after((z_half, x_half), back_xz)
    w_half = moved(xk, "blk", outward)
    zk, ahead = after((zk, ahead), zy_near, zy_far)
    u_half = swapped(zk, "blk", 1)
    zy_far, zy_near, back_xz = after((zy_far, zy_near, back_xz), u_more, w_more)
    back = gather(merge(back_xz, zy_far, zy_near))

    places, place = [], 0
    for height in (rows, rows, rows - size, rows - first):
        places.append((place, place + height))
        place += height
    total, weights = apply_most(places, (size, first), gather(ahead), back, (y, z, u_more, w_more))
    return apply_last(weights, total, u_half, w_half)


def from_behind(value, by):
    devices = lax.axis_size("blk")
    return lax.ppermute(value, "blk", [(i, (i + by) % devices) for i in range(devices)])


def direct(x, near, far, far_offset):
    total = jnp.zeros(x.shape, F32)
    for offset, slab in ((1, near), (far_offset, far)):
        later = from_behind(x, -offset)
        earlier, earlier_slab = from_behind((x, slab), offset)
        for other, scale in ((later, slab), (earlier, earlier_slab.T)):
            gram = lax.psum(outer(x, other), "orb")
            weighted = (gram * scale.astype(F32)).astype(BF16)
            total += inner(weighted, other)
    return total.astype(BF16)


def per_device(orbitals, coulomb_near, coulomb_far):
    far_offset = lax.axis_size("blk") // 4
    if far_offset == 2 and lax.axis_size("orb") == 4:
        return relayed(orbitals, coulomb_near, coulomb_far)
    return direct(orbitals, coulomb_near, coulomb_far, far_offset)


def solution(mesh):
    return jax.shard_map(
        per_device,
        mesh=mesh,
        in_specs=(P("blk", "orb"), P("blk", None), P("blk", None)),
        out_specs=P("blk", "orb"),
        check_vma=False,
    )
```

time: 122 us -> 113 us (0.926)
  starting transfers between devices: 25.1 us -> 20.2 us
  Pallas kernels: 16.2 us -> 14.6 us
    ppermute x7, starting transfers between devices: 16.1 us -> 9.71 us  [moved(): return lax.ppermute(value, axis, pairs)]
    slice x3 -> x2, local copies, waits for them, and re-layouts: 4.2 us -> 2.37 us  [the longest x1 1.28 us: relayed(): u_more = swapped(after((zk[size:],), y, near_part)[0], 'blk', 1)]
    ppermute x7, waiting for transfers between devices: 46.6 us -> 44.7 us  [moved(): return lax.ppermute(value, axis, pairs)]
    ppermute x11 -> x12, starting transfers between devices: 9 us -> 10.5 us  [swapped(): lax.ppermute(value, axis, [(i, i ^ distance) for i in range(devices)])]
    pallas_call x1, Pallas kernels: 1.54 us -> 0.13 us  [fold(): pl.pallas_call(fold_kernel, in_specs=[VMEM] * 2, out_specs=[VMEM] * 2, ou...]
    ppermute x11 -> x12, waiting for transfers between devices: 26.1 us -> 27.3 us  [swapped(): lax.ppermute(value, axis, [(i, i ^ distance) for i in range(devices)])]
    unnamed x10 -> x12, local copies, waits for them, and re-layouts: 1.61 us -> 2.67 us
  transfers between devices with their start and end apart: 18 -> 19, of which waited for: 7 -> 10; matrix products, arithmetic and copies ran while one was open for 4% -> 2% of each run, Pallas kernels for 10% -> 11%
where the time goes in v2:
time: 113 us
  waiting for transfers between devices  72.1 us (64%)
  starting transfers between devices  20.2 us (18%)
  Pallas kernels  14.6 us (13%)
  local copies, waits for them, and re-layouts  5.04 us (4%)
    ppermute x7, waiting for transfers between devices, moved(): return lax.ppermute(value, axis, pairs)  44.7 us
    ppermute x12, waiting for transfers between devices, swapped(): lax.ppermute(value, axis, [(i, i ^ distance) for i in range(devices)])  27.3 us
    ppermute x12, starting transfers between devices, swapped(): lax.ppermute(value, axis, [(i, i ^ distance) for i in range(devices)])  10.5 us
    ppermute x7, starting transfers between devices, moved(): return lax.ppermute(value, axis, pairs)  9.71 us
    pallas_call x1, Pallas kernels, apply_most(): pl.pallas_call(functools.partial(most_kernel, places, firsts), in_specs=[...  5.98 us
    pallas_call x1, Pallas kernels, gram(): pl.pallas_call(gram_kernel, in_specs=[VMEM] * 3, out_specs=[VMEM] * 2, ou...  3.62 us
    unnamed x12, local copies, waits for them, and re-layouts  2.67 us
    pallas_call x1, Pallas kernels, prepare(): pl.pallas_call(prepare_kernel, in_specs=[VMEM] * 3, out_specs=[VMEM] * 4...  2.55 us
  transfers between devices with their start and end apart: 19, of which 10 were waited for; matrix products, arithmetic and copies ran while one was open for 2% of the time, Pallas kernels for 11%

profile of v2, /device:TPU:0, one launch (start us, length us, event | category | flops | bytes accessed | tf_op | source)
XLA Modules:
  0.0 112.7 jit_solution(11811260197459369316)
XLA Ops:
  0.0 5.0 %collective-permute-start.3 = (bf16[512,2048]{1,0:T(8,128)(2,1)}, bf16[512,2048]{1,0:T(8,128)(2,1)S(1)}, u32[]{:S(2)}, u32[]{:S(2)}) collective-permute-start(bf16[512,2048]{1,0:T(8,128)(2,1)} %x.3), channel_id=1, source_target_pairs={{0,24},{4,12},{8,0},{12,20},{16,8},{20,28},{24,16},{28,4},{1,25},{... | collective-permute-start | bytes 6291464 | tf_op jit(solution)/shard_map/ppermute | solution.py:33
  5.1 1.7 %copy-done = bf16[512,2048]{1,0:T(8,128)(2,1)S(1)} copy-done((bf16[512,2048]{1,0:T(8,128)(2,1)S(1)}, bf16[512,2048]{1,0:T(8,128)(2,1)}, u32[]{:S(2)}) %copy-start) | copy-done | bytes 2097176
  6.7 2.5 %shard_map.37 = (bf16[240,2048]{1,0:T(8,128)(2,1)S(1)}, bf16[272,2048]{1,0:T(8,128)(2,1)}, bf16[512,128]{1,0:T(8,128)(2,1)S(1)}, bf16[512,128]{1,0:T(8,128)(2,1)S(1)}, s32[1,1]{1,0:T(1,128)}) custom-call(bf16[512,2048]{1,0:T(8,128)(2,1)S(1)} %copy-done, bf16[512,512]{1,0:T(8,128)(2,1)} %near.1, bf16[512,512]{1,0:T(8,128)(2,1)} %far.1), custom_call_target="tpu_custom_call" | custom-call | bytes 6291456 | tf_op jit(solution)/shard_map/pallas_call | solution.py:67
  10.9 3.3 %collective-permute-start.4 = (bf16[512,128]{1,0:T(8,128)(2,1)S(1)}, bf16[512,128]{1,0:T(8,128)(2,1)S(1)}, u32[]{:S(2)}, u32[]{:S(2)}) collective-permute-start(bf16[512,128]{1,0:T(8,128)(2,1)S(1)} %get-tuple-element.57), channel_id=1, source_target_pairs={{0,4},{4,0},{8,12},{12,8},{16,20},{20,16},{24,28},{28,24},{1,5},{5... | collective-permute-start | bytes 393224 | tf_op jit(solution)/shard_map/ppermute | solution.py:38
  14.2 36.2 %collective-permute-done.3.z.refs_9_ = bf16[512,2048]{1,0:T(8,128)(2,1)S(1)} collective-permute-done((bf16[512,2048]{1,0:T(8,128)(2,1)}, bf16[512,2048]{1,0:T(8,128)(2,1)S(1)}, u32[]{:S(2)}, u32[]{:S(2)}) %collective-permute-start.3) | collective-permute-done | bytes 2097184 | tf_op jit(solution)/shard_map/ppermute | solution.py:33
  50.6 1.3 %slice.6 = bf16[256,2048]{1,0:T(8,128)(2,1)} slice(bf16[512,2048]{1,0:T(8,128)(2,1)S(1)} %collective-permute-done.3.z.refs_9_), slice={[256:512], [0:2048]} | slice | bytes 2097152 | tf_op jit(solution)/shard_map/slice | solution.py:283
  51.9 3.3 %collective-permute-done.4 = bf16[512,128]{1,0:T(8,128)(2,1)S(1)} collective-permute-done((bf16[512,128]{1,0:T(8,128)(2,1)S(1)}, bf16[512,128]{1,0:T(8,128)(2,1)S(1)}, u32[]{:S(2)}, u32[]{:S(2)}) %collective-permute-start.4) | collective-permute-done | bytes 131104 | tf_op jit(solution)/shard_map/ppermute | solution.py:38
  55.2 2.9 %collective-permute-start.12 = (bf16[256,2048]{1,0:T(8,128)(2,1)}, bf16[256,2048]{1,0:T(8,128)(2,1)}, u32[]{:S(2)}, u32[]{:S(2)}) collective-permute-start(bf16[256,2048]{1,0:T(8,128)(2,1)} %slice.6), channel_id=1, source_target_pairs={{0,4},{4,0},{8,12},{12,8},{16,20},{20,16},{24,28},{28,24},{1,5},{5... | collective-permute-start | bytes 3145736 | tf_op jit(solution)/shard_map/ppermute | solution.py:38
  58.7 3.6 %shard_map.38 = (f32[256,1536]{1,0:T(8,128)S(1)}, bf16[256,1536]{1,0:T(8,128)(2,1)S(1)}) custom-call(bf16[512,2048]{1,0:T(8,128)(2,1)S(1)} %copy-done.1, bf16[512,2048]{1,0:T(8,128)(2,1)S(1)} %collective-permute-done.2.y.refs_8_, bf16[512,2048]{1,0:T(8,128)(2,1)S(1)} %collective-permute-done.3.z.refs_9_), custom_call_target="tpu_custom_call" | custom-call | tf_op jit(solution)/shard_map/pallas_call | solution.py:92
  62.4 13.9 %conditional.1 = (bf16[128,1024]{1,0:T(8,128)(2,1)S(1)}, bf16[128,512]{1,0:T(8,128)(2,1)S(1)}, bf16[128,512]{1,0:T(8,128)(2,1)S(1)}, bf16[256,2048]{1,0:T(8,128)(2,1)}) conditional(s32[]{:T(128)} %bitcast, () %tuple.18, (bf16[256,1536]{1,0:T(8,128)(2,1)S(1)}, f32[256,1536]{1,0:T(8,128)S(1)}, bf16[512,512]{1,0:T(8,128)(2,1)S(1)}, ...), branch_computations={%region_0.0_spmd, %region_1.0_spmd} | conditional | flops 1179648 | bytes 12976240 | solution.py:297
  62.5 2.3 %collective-permute-done.other = bf16[256,1536]{1,0:T(8,128)(2,1)S(1)} collective-permute-done((bf16[256,1536]{1,0:T(8,128)(2,1)S(1)}, bf16[256,1536]{1,0:T(8,128)(2,1)S(1)}, u32[]{:S(2)}, u32[]{:S(2)}) %collective-permute-start) | collective-permute-done | bytes 786464 | tf_op jit(solution)/shard_map/cond/branch_1_fun/ppermute | solution.py:38
  64.9 1.6 %collective-permute-start.1 = (bf16[128,1536]{1,0:T(8,128)(2,1)S(1)}, bf16[128,1536]{1,0:T(8,128)(2,1)S(1)}, u32[]{:S(2)}, u32[]{:S(2)}) collective-permute-start(bf16[128,1536]{1,0:T(8,128)(2,1)S(1)} %get-tuple-element.22), channel_id=1, source_target_pairs={{0,2},{1,3},{2,0},{3,1},{4,6},{5,7},{6,4},{7,5},{8,10},{9,11},{10,... | collective-permute-start | bytes 1179656 | tf_op jit(solution)/shard_map/cond/branch_1_fun/ppermute | solution.py:38
  67.6 8.6 %collective-permute-done.1.other = bf16[128,1536]{1,0:T(8,128)(2,1)S(1)} collective-permute-done((bf16[128,1536]{1,0:T(8,128)(2,1)S(1)}, bf16[128,1536]{1,0:T(8,128)(2,1)S(1)}, u32[]{:S(2)}, u32[]{:S(2)}) %collective-permute-start.1) | collective-permute-done | bytes 393248 | tf_op jit(solution)/shard_map/cond/branch_1_fun/ppermute | solution.py:38
  76.6 1.9 %collective-permute-start.8 = (bf16[128,512]{1,0:T(8,128)(2,1)S(1)}, bf16[128,512]{1,0:T(8,128)(2,1)S(1)}, u32[]{:S(2)}, u32[]{:S(2)}) collective-permute-start(bf16[128,512]{1,0:T(8,128)(2,1)S(1)} %get-tuple-element.64), channel_id=1, source_target_pairs={{0,8},{8,16},{16,24},{24,0},{1,9},{9,17},{17,25},{25,1},{2,10},{10... | collective-permute-start | bytes 393224 | tf_op jit(solution)/shard_map/ppermute | solution.py:33
  78.6 1.3 %collective-permute-start.7 = (bf16[128,512]{1,0:T(8,128)(2,1)S(1)}, bf16[128,512]{1,0:T(8,128)(2,1)S(1)}, u32[]{:S(2)}, u32[]{:S(2)}) collective-permute-start(bf16[128,512]{1,0:T(8,128)(2,1)S(1)} %get-tuple-element.64), channel_id=1, source_target_pairs={{0,4},{8,12},{16,20},{24,28},{1,5},{9,13},{17,21},{25,29},{2,6},{1... | collective-permute-start | bytes 393224 | tf_op jit(solution)/shard_map/ppermute | solution.py:33
  79.9 4.4 %collective-permute-done.6.xz = bf16[128,512]{1,0:T(8,128)(2,1)S(1)} collective-permute-done((bf16[128,512]{1,0:T(8,128)(2,1)S(1)}, bf16[128,512]{1,0:T(8,128)(2,1)S(1)}, u32[]{:S(2)}, u32[]{:S(2)}) %collective-permute-start.6) | collective-permute-done | bytes 131104 | tf_op jit(solution)/shard_map/ppermute | solution.py:33
  84.3 1.7 %collective-permute-done.8.zy_far = bf16[128,512]{1,0:T(8,128)(2,1)S(1)} collective-permute-done((bf16[128,512]{1,0:T(8,128)(2,1)S(1)}, bf16[128,512]{1,0:T(8,128)(2,1)S(1)}, u32[]{:S(2)}, u32[]{:S(2)}) %collective-permute-start.8) | collective-permute-done | bytes 131104 | tf_op jit(solution)/shard_map/ppermute | solution.py:33
  86.2 1.5 %collective-permute-start.9 = (bf16[128,1024]{1,0:T(8,128)(2,1)S(1)}, bf16[128,1024]{1,0:T(8,128)(2,1)S(1)}, u32[]{:S(2)}, u32[]{:S(2)}) collective-permute-start(bf16[128,1024]{1,0:T(8,128)(2,1)S(1)} %get-tuple-element.65.refs_0_), channel_id=1, source_target_pairs={{0,2},{1,3},{2,0},{3,1},{4,6},{5,7},{6,4},{7,5},{8,10},{9,11},{10,... | collective-permute-start | bytes 786440 | tf_op jit(solution)/shard_map/ppermute | solution.py:38
  88.4 7.0 %collective-permute-done.9.refs_1_ = bf16[128,1024]{1,0:T(8,128)(2,1)S(1)} collective-permute-done((bf16[128,1024]{1,0:T(8,128)(2,1)S(1)}, bf16[128,1024]{1,0:T(8,128)(2,1)S(1)}, u32[]{:S(2)}, u32[]{:S(2)}) %collective-permute-start.9) | collective-permute-done | bytes 262176 | tf_op jit(solution)/shard_map/ppermute | solution.py:38
  95.8 4.7 %collective-permute-done.14.refs_5_ = bf16[128,1024]{1,0:T(8,128)(2,1)S(1)} collective-permute-done((bf16[128,1024]{1,0:T(8,128)(2,1)S(1)}, bf16[128,1024]{1,0:T(8,128)(2,1)S(1)}, u32[]{:S(2)}, u32[]{:S(2)}) %collective-permute-start.14) | collective-permute-done | bytes 262176 | tf_op jit(solution)/shard_map/ppermute | solution.py:38
  100.6 1.5 %collective-permute-done.16.refs_7_ = bf16[128,1024]{1,0:T(8,128)(2,1)S(1)} collective-permute-done((bf16[128,1024]{1,0:T(8,128)(2,1)S(1)}, bf16[128,1024]{1,0:T(8,128)(2,1)S(1)}, u32[]{:S(2)}, u32[]{:S(2)}) %collective-permute-start.16) | collective-permute-done | bytes 262176 | tf_op jit(solution)/shard_map/ppermute | solution.py:38
  102.1 6.0 %shard_map.40 = (f32[512,2048]{1,0:T(8,128)S(1)}, bf16[512,496]{1,0:T(8,128)(2,1)S(1)}) custom-call(bf16[128,1024]{1,0:T(8,128)(2,1)S(1)} %get-tuple-element.65.refs_0_, bf16[128,1024]{1,0:T(8,128)(2,1)S(1)} %collective-permute-done.9.refs_1_, bf16[128,1024]{1,0:T(8,128)(2,1)S(1)} %collective-permute-done.10.refs_2_, ...), custom_call_target="tpu_custom_call" | custom-call | tf_op jit(solution)/shard_map/pallas_call | solution.py:195
  108.1 2.5 %collective-permute-done.18.w = bf16[240,2048]{1,0:T(8,128)(2,1)S(1)} collective-permute-done((bf16[240,2048]{1,0:T(8,128)(2,1)}, bf16[240,2048]{1,0:T(8,128)(2,1)S(1)}, u32[]{:S(2)}, u32[]{:S(2)}) %collective-permute-start.18) | collective-permute-done | bytes 983072 | tf_op jit(solution)/shard_map/ppermute | solution.py:33
  110.6 2.1 %shard_map.41 = bf16[512,2048]{1,0:T(8,128)(2,1)} custom-call(bf16[512,496]{1,0:T(8,128)(2,1)S(1)} %get-tuple-element.73.weights, f32[512,2048]{1,0:T(8,128)S(1)} %get-tuple-element.74.total, bf16[256,2048]{1,0:T(8,128)(2,1)S(1)} %collective-permute-done.17.u, bf16[240,2048]{1,0:T(8,128)(2,1)S(1)} %collective-permute-done.18.w), custom_call_target="tpu_custom_call" | custom-call | flops 1040187392 | bytes 8323072 | tf_op jit(solution)/shard_map/pallas_call | solution.py:227
  (36 shorter events, 5.1 us)
Async XLA Ops:
  0.0 50.4 %collective-permute-start.3 = (bf16[512,2048]{1,0:T(8,128)(2,1)}, bf16[512,2048]{1,0:T(8,128)(2,1)S(1)}, u32[]{:S(2)}, u32[]{:S(2)}) collective-permute-start(bf16[512,2048]{1,0:T(8,128)(2,1)} %x.3), channel_id=1, source_target_pairs={{0,24},{4,12},{8,0},{12,20},{16,8},{20,28},{24,16},{28,4},{1,25},{... | collective-permute-start | bytes 6291464 | tf_op jit(solution)/shard_map/ppermute | solution.py:33
  5.0 50.1 %collective-permute-start.2 = (bf16[512,2048]{1,0:T(8,128)(2,1)}, bf16[512,2048]{1,0:T(8,128)(2,1)S(1)}, u32[]{:S(2)}, u32[]{:S(2)}) collective-permute-start(bf16[512,2048]{1,0:T(8,128)(2,1)} %x.3), channel_id=1, source_target_pairs={{0,4},{4,0},{8,12},{12,8},{16,20},{20,16},{24,28},{28,24},{1,5},{5... | collective-permute-start | bytes 6291464 | tf_op jit(solution)/shard_map/ppermute | solution.py:38
  5.1 1.7 %copy-start = (bf16[512,2048]{1,0:T(8,128)(2,1)S(1)}, bf16[512,2048]{1,0:T(8,128)(2,1)}, u32[]{:S(2)}) copy-start(bf16[512,2048]{1,0:T(8,128)(2,1)} %x.3) | copy-start | bytes 6291460
  6.7 52.0 %copy-start.1 = (bf16[512,2048]{1,0:T(8,128)(2,1)S(1)}, bf16[512,2048]{1,0:T(8,128)(2,1)}, u32[]{:S(2)}) copy-start(bf16[512,2048]{1,0:T(8,128)(2,1)} %x.3) | copy-start | bytes 6291460
  10.3 4.0 %collective-permute-start.5 = (bf16[512,128]{1,0:T(8,128)(2,1)S(1)}, bf16[512,128]{1,0:T(8,128)(2,1)S(1)}, u32[]{:S(2)}, u32[]{:S(2)}) collective-permute-start(bf16[512,128]{1,0:T(8,128)(2,1)S(1)} %get-tuple-element.58), channel_id=1, source_target_pairs={{4,12},{12,20},{20,28},{28,4},{5,13},{13,21},{21,29},{29,5},{6,14}... | collective-permute-start | bytes 393224 | tf_op jit(solution)/shard_map/ppermute | solution.py:33
  10.9 44.2 %collective-permute-start.4 = (bf16[512,128]{1,0:T(8,128)(2,1)S(1)}, bf16[512,128]{1,0:T(8,128)(2,1)S(1)}, u32[]{:S(2)}, u32[]{:S(2)}) collective-permute-start(bf16[512,128]{1,0:T(8,128)(2,1)S(1)} %get-tuple-element.57), channel_id=1, source_target_pairs={{0,4},{4,0},{8,12},{12,8},{16,20},{20,16},{24,28},{28,24},{1,5},{5... | collective-permute-start | bytes 393224 | tf_op jit(solution)/shard_map/ppermute | solution.py:38
  50.4 11.9 %copy-start.3 = (bf16[512,2048]{1,0:T(8,128)(2,1)}, bf16[512,2048]{1,0:T(8,128)(2,1)S(1)}, u32[]{:S(2)}) copy-start(bf16[512,2048]{1,0:T(8,128)(2,1)S(1)} %collective-permute-done.3.z.refs_9_) | copy-start | bytes 6291460
  50.4 37.3 %collective-permute-start.13 = (bf16[272,2048]{1,0:T(8,128)(2,1)}, bf16[272,2048]{1,0:T(8,128)(2,1)S(1)}, u32[]{:S(2)}, u32[]{:S(2)}) collective-permute-start(bf16[272,2048]{1,0:T(8,128)(2,1)} %get-tuple-element.69), channel_id=1, source_target_pairs={{0,8},{4,28},{8,16},{12,4},{16,24},{20,12},{24,0},{28,20},{1,9},{5... | collective-permute-start | bytes 3342344 | tf_op jit(solution)/shard_map/ppermute | solution.py:33
  55.2 31.1 %collective-permute-start.12 = (bf16[256,2048]{1,0:T(8,128)(2,1)}, bf16[256,2048]{1,0:T(8,128)(2,1)}, u32[]{:S(2)}, u32[]{:S(2)}) collective-permute-start(bf16[256,2048]{1,0:T(8,128)(2,1)} %slice.6), channel_id=1, source_target_pairs={{0,4},{4,0},{8,12},{12,8},{16,20},{20,16},{24,28},{28,24},{1,5},{5... | collective-permute-start | bytes 3145736 | tf_op jit(solution)/shard_map/ppermute | solution.py:38
  58.7 3.7 %copy-start.4 = (bf16[512,512]{1,0:T(8,128)(2,1)S(1)}, bf16[512,512]{1,0:T(8,128)(2,1)}, u32[]{:S(2)}) copy-start(bf16[512,512]{1,0:T(8,128)(2,1)} %near.1) | copy-start | bytes 1572868
  58.7 3.6 %copy-start.5 = (bf16[512,512]{1,0:T(8,128)(2,1)S(1)}, bf16[512,512]{1,0:T(8,128)(2,1)}, u32[]{:S(2)}) copy-start(bf16[512,512]{1,0:T(8,128)(2,1)} %far.1) | copy-start | bytes 1572868
  62.4 2.4 %collective-permute-start = (bf16[256,1536]{1,0:T(8,128)(2,1)S(1)}, bf16[256,1536]{1,0:T(8,128)(2,1)S(1)}, u32[]{:S(2)}, u32[]{:S(2)}) collective-permute-start(bf16[256,1536]{1,0:T(8,128)(2,1)S(1)} %get-tuple-element.20), channel_id=1, source_target_pairs={{0,1},{1,0},{2,3},{3,2},{4,5},{5,4},{6,7},{7,6},{8,9},{9,8},{10,11... | collective-permute-start | bytes 2359304 | tf_op jit(solution)/shard_map/cond/branch_1_fun/ppermute | solution.py:38
  64.9 11.2 %collective-permute-start.1 = (bf16[128,1536]{1,0:T(8,128)(2,1)S(1)}, bf16[128,1536]{1,0:T(8,128)(2,1)S(1)}, u32[]{:S(2)}, u32[]{:S(2)}) collective-permute-start(bf16[128,1536]{1,0:T(8,128)(2,1)S(1)} %get-tuple-element.22), channel_id=1, source_target_pairs={{0,2},{1,3},{2,0},{3,1},{4,6},{5,7},{6,4},{7,5},{8,10},{9,11},{10,... | collective-permute-start | bytes 1179656 | tf_op jit(solution)/shard_map/cond/branch_1_fun/ppermute | solution.py:38
  76.3 8.0 %collective-permute-start.6 = (bf16[128,512]{1,0:T(8,128)(2,1)S(1)}, bf16[128,512]{1,0:T(8,128)(2,1)S(1)}, u32[]{:S(2)}, u32[]{:S(2)}) collective-permute-start(bf16[128,512]{1,0:T(8,128)(2,1)S(1)} %get-tuple-element.61), channel_id=1, source_target_pairs={{0,8},{4,28},{8,16},{12,4},{16,24},{20,12},{24,0},{28,20},{1,9},{5... | collective-permute-start | bytes 393224 | tf_op jit(solution)/shard_map/ppermute | solution.py:33
  76.6 9.3 %collective-permute-start.8 = (bf16[128,512]{1,0:T(8,128)(2,1)S(1)}, bf16[128,512]{1,0:T(8,128)(2,1)S(1)}, u32[]{:S(2)}, u32[]{:S(2)}) collective-permute-start(bf16[128,512]{1,0:T(8,128)(2,1)S(1)} %get-tuple-element.64), channel_id=1, source_target_pairs={{0,8},{8,16},{16,24},{24,0},{1,9},{9,17},{17,25},{25,1},{2,10},{10... | collective-permute-start | bytes 393224 | tf_op jit(solution)/shard_map/ppermute | solution.py:33
  78.6 7.4 %collective-permute-start.7 = (bf16[128,512]{1,0:T(8,128)(2,1)S(1)}, bf16[128,512]{1,0:T(8,128)(2,1)S(1)}, u32[]{:S(2)}, u32[]{:S(2)}) collective-permute-start(bf16[128,512]{1,0:T(8,128)(2,1)S(1)} %get-tuple-element.64), channel_id=1, source_target_pairs={{0,4},{8,12},{16,20},{24,28},{1,5},{9,13},{17,21},{25,29},{2,6},{1... | collective-permute-start | bytes 393224 | tf_op jit(solution)/shard_map/ppermute | solution.py:33
  85.9 24.6 %collective-permute-start.17 = (bf16[256,2048]{1,0:T(8,128)(2,1)}, bf16[256,2048]{1,0:T(8,128)(2,1)S(1)}, u32[]{:S(2)}, u32[]{:S(2)}) collective-permute-start(bf16[256,2048]{1,0:T(8,128)(2,1)} %get-tuple-element.75), channel_id=1, source_target_pairs={{0,4},{4,0},{8,12},{12,8},{16,20},{20,16},{24,28},{28,24},{1,5},{5... | collective-permute-start | bytes 3145736 | tf_op jit(solution)/shard_map/ppermute | solution.py:38
  85.9 24.6 %collective-permute-start.18 = (bf16[240,2048]{1,0:T(8,128)(2,1)}, bf16[240,2048]{1,0:T(8,128)(2,1)S(1)}, u32[]{:S(2)}, u32[]{:S(2)}) collective-permute-start(bf16[240,2048]{1,0:T(8,128)(2,1)} %copy-done.2), channel_id=1, source_target_pairs={{0,8},{4,28},{8,16},{12,4},{16,24},{20,12},{24,0},{28,20},{1,9},{5... | collective-permute-start | bytes 2949128 | tf_op jit(solution)/shard_map/ppermute | solution.py:33
  86.2 9.1 %collective-permute-start.10 = (bf16[128,1024]{1,0:T(8,128)(2,1)S(1)}, bf16[128,1024]{1,0:T(8,128)(2,1)S(1)}, u32[]{:S(2)}, u32[]{:S(2)}) collective-permute-start(bf16[128,1024]{1,0:T(8,128)(2,1)S(1)} %get-tuple-element.65.refs_0_), channel_id=1, source_target_pairs={{0,1},{1,0},{2,3},{3,2},{4,5},{5,4},{6,7},{7,6},{8,9},{9,8},{10,11... | collective-permute-start | bytes 786440 | tf_op jit(solution)/shard_map/ppermute | solution.py:38
  86.2 9.1 %collective-permute-start.9 = (bf16[128,1024]{1,0:T(8,128)(2,1)S(1)}, bf16[128,1024]{1,0:T(8,128)(2,1)S(1)}, u32[]{:S(2)}, u32[]{:S(2)}) collective-permute-start(bf16[128,1024]{1,0:T(8,128)(2,1)S(1)} %get-tuple-element.65.refs_0_), channel_id=1, source_target_pairs={{0,2},{1,3},{2,0},{3,1},{4,6},{5,7},{6,4},{7,5},{8,10},{9,11},{10,... | collective-permute-start | bytes 786440 | tf_op jit(solution)/shard_map/ppermute | solution.py:38
  87.8 12.8 %collective-permute-start.14 = (bf16[128,1024]{1,0:T(8,128)(2,1)S(1)}, bf16[128,1024]{1,0:T(8,128)(2,1)S(1)}, u32[]{:S(2)}, u32[]{:S(2)}) collective-permute-start(bf16[128,1024]{1,0:T(8,128)(2,1)S(1)} %shard_map.39.refs_4_), channel_id=1, source_target_pairs={{0,2},{1,3},{2,0},{3,1},{4,6},{5,7},{6,4},{7,5},{8,10},{9,11},{10,... | collective-permute-start | bytes 786440 | tf_op jit(solution)/shard_map/ppermute | solution.py:38
  95.3 5.2 %collective-permute-start.11 = (bf16[128,1024]{1,0:T(8,128)(2,1)S(1)}, bf16[128,1024]{1,0:T(8,128)(2,1)S(1)}, u32[]{:S(2)}, u32[]{:S(2)}) collective-permute-start(bf16[128,1024]{1,0:T(8,128)(2,1)S(1)} %collective-permute-done.9.refs_1_), channel_id=1, source_target_pairs={{0,1},{1,0},{2,3},{3,2},{4,5},{5,4},{6,7},{7,6},{8,9},{9,8},{10,11... | collective-permute-start | bytes 786440 | tf_op jit(solution)/shard_map/ppermute | solution.py:38
  95.3 5.2 %collective-permute-start.15 = (bf16[128,1024]{1,0:T(8,128)(2,1)S(1)}, bf16[128,1024]{1,0:T(8,128)(2,1)S(1)}, u32[]{:S(2)}, u32[]{:S(2)}) collective-permute-start(bf16[128,1024]{1,0:T(8,128)(2,1)S(1)} %shard_map.39.refs_4_), channel_id=1, source_target_pairs={{0,1},{1,0},{2,3},{3,2},{4,5},{5,4},{6,7},{7,6},{8,9},{9,8},{10,11... | collective-permute-start | bytes 786440 | tf_op jit(solution)/shard_map/ppermute | solution.py:38
  100.6 1.5 %collective-permute-start.16 = (bf16[128,1024]{1,0:T(8,128)(2,1)S(1)}, bf16[128,1024]{1,0:T(8,128)(2,1)S(1)}, u32[]{:S(2)}, u32[]{:S(2)}) collective-permute-start(bf16[128,1024]{1,0:T(8,128)(2,1)S(1)} %collective-permute-done.14.refs_5_), channel_id=1, source_target_pairs={{0,1},{1,0},{2,3},{3,2},{4,5},{5,4},{6,7},{7,6},{8,9},{9,8},{10,11... | collective-permute-start | bytes 786440 | tf_op jit(solution)/shard_map/ppermute | solution.py:38
  (1 other events, 1.0 us)

commit v3 on v2

--- a/solution.py
+++ b/solution.py
@@ -8,6 +8,7 @@
 from jax.sharding import PartitionSpec as P
 
 MIB = 1024 * 1024
+SEEN_COST, MOST_COST, SETTLE_COST = 10, 35, 10
 F32, BF16 = jnp.float32, jnp.bfloat16
 VMEM = pl.BlockSpec(memory_space=pltpu.VMEM)
 ANY = pl.BlockSpec(memory_space=pl.ANY)
@@ -118,7 +119,7 @@
     )(keep, other)
 
 
-def weigh_kernel(mine, other, near, far, near_other, far_other, ahead, xz, zy):
+def weigh_kernel(mine, other, near, far, near_other, far_other, ahead, pair, xz, zy):
     rows = near.shape[0]
     here = quarter_rows(rows)
     even = lax.axis_index("blk") % 2 == 0
@@ -131,7 +132,10 @@
     weighted = (gram[:, rows : 2 * rows] * far_slab).astype(BF16)
     ahead[:, rows:] = weighted
     xz[...] = weighted
-    zy[...] = (gram[:, 2 * rows :] * near_turned).astype(BF16)
+    pair[:, :rows] = weighted
+    weighted = (gram[:, 2 * rows :] * near_turned).astype(BF16)
+    pair[:, rows:] = weighted
+    zy[...] = weighted
 
 
 def weigh(mine, other, near, far, near_other, far_other):
@@ -139,16 +143,33 @@
     return pl.pallas_call(
         weigh_kernel,
         in_specs=[VMEM] * 6,
-        out_specs=[VMEM] * 3,
-        out_shape=[shape(size, 2 * rows, BF16), shape(size, rows, BF16), shape(size, rows, BF16)],
+        out_specs=[VMEM] * 4,
+        out_shape=[shape(size, n * rows, BF16) for n in (2, 2, 1, 1)],
         compiler_params=pltpu.CompilerParams(vmem_limit_bytes=8 * MIB),
         cost_estimate=cost(6 * size * rows, 40 * size * rows),
     )(mine, other, near, far, near_other, far_other)
 
 
+def settle_kernel(a0, a1, a2, a3, out):
+    for distance, part in enumerate((a0, a1, a2, a3)):
+        out[quarter_rows(out.shape[0], distance), :] = part[...]
+
+
+def settle(parts):
+    size, width = parts[0].shape
+    return pl.pallas_call(
+        settle_kernel,
+        in_specs=[VMEM] * 4,
+        out_specs=VMEM,
+        out_shape=shape(4 * size, width, BF16),
+        compiler_params=pltpu.CompilerParams(vmem_limit_bytes=4 * MIB),
+        cost_estimate=cost(SETTLE_COST * 10**8, 0),
+    )(*parts)
+
+
 def most_kernel(places, firsts, *refs):
-    ahead, back, values = refs[:4], refs[4:8], refs[8 : 8 + len(places)]
-    out, kept, weights, held, arrived = refs[8 + len(values) :]
+    ahead, back, values = refs[0], refs[1:5], refs[5 : 5 + len(places)]
+    out, kept, weights, held, arrived = refs[5 + len(values) :]
     rows, columns = out.shape
     size, tiles = rows // 4, 4
     copies = []
@@ -158,8 +179,7 @@
         copies[-1].start()
 
     even = lax.axis_index("blk") % 2 == 0
-    for distance in range(4):
-        weights[quarter_rows(rows, distance), : 2 * rows] = ahead[distance][...]
+    weights[:, : 2 * rows] = ahead[...]
     for distance in range(4):
         here = quarter_rows(rows, distance)
         weights[:, pl.ds(pl.multiple_of(3 * rows + here.start, size), size)] = (
@@ -191,10 +211,10 @@
 
 
 def apply_most(places, firsts, ahead, back, values):
-    rows, columns = ahead[0].shape[0] * 4, values[0].shape[1]
+    rows, columns = values[0].shape
     return pl.pallas_call(
         functools.partial(most_kernel, places, firsts),
-        in_specs=[VMEM] * 8 + [ANY] * len(values),
+        in_specs=[VMEM] * 5 + [ANY] * len(values),
         out_specs=[VMEM] * 2,
         out_shape=[shape(rows, columns, F32), shape(rows, sum(firsts), BF16)],
         scratch_shapes=[
@@ -203,11 +223,11 @@
             pltpu.SemaphoreType.DMA((len(values),)),
         ],
         compiler_params=pltpu.CompilerParams(vmem_limit_bytes=22 * MIB),
-        cost_estimate=cost(0, 0),
-    )(*ahead, *back, *values)
-
-
-def last_kernel(weights, total, u, w, out, result, left):
+        cost_estimate=cost(MOST_COST * 10**8, 0),
+    )(ahead, *back, *values)
+
+
+def last_kernel(weights, total, u, w, _, out, result, left):
     rows, columns = out.shape
     last, tiles = u.shape[0], 4
     writes = []
@@ -221,44 +241,58 @@
         write.wait()
 
 
-def apply_last(weights, total, u, w):
+def apply_last(weights, total, u, w, here):
     rows, columns = total.shape
     last = (u.shape[0] + w.shape[0]) // 2
     return pl.pallas_call(
         last_kernel,
-        in_specs=[VMEM] * 4,
+        in_specs=[VMEM] * 4 + [ANY],
         out_specs=ANY,
         out_shape=shape(rows, columns, BF16),
         scratch_shapes=[pltpu.VMEM((rows, columns), BF16), pltpu.SemaphoreType.DMA((4,))],
         compiler_params=pltpu.CompilerParams(vmem_limit_bytes=16 * MIB),
         cost_estimate=cost(4 * rows * last * columns, 6 * rows * columns + 4 * last * columns),
-    )(weights, total, u, w)
-
-
-def merge_kernel(xz, zy_far, zy_near, out):
-    rows = xz.shape[1]
+    )(weights, total, u, w, here)
+
+
+def seen_kernel(value, out):
+    out[...] = jnp.ones_like(out)
+
+
+def seen(value):
+    return pl.pallas_call(
+        seen_kernel,
+        in_specs=[ANY],
+        out_specs=VMEM,
+        out_shape=shape(8, 128, F32),
+        compiler_params=pltpu.CompilerParams(vmem_limit_bytes=MIB),
+        cost_estimate=cost(SEEN_COST * 10**8, 0),
+    )(value)
+
+
+def merge_kernel(even_back, odd_back, zy_near, out):
+    rows = zy_near.shape[1]
     even = lax.axis_index("blk") % 2 == 0
-    out[:, :rows] = xz[...]
 
     @pl.when(even)
     def _():
-        out[:, rows:] = zy_far[...]
+        out[...] = even_back[...]
 
     @pl.when(jnp.logical_not(even))
     def _():
+        out[:, :rows] = odd_back[...]
         out[:, rows:] = zy_near[...]
 
 
-def merge(xz, zy_far, zy_near):
-    size, rows = xz.shape
+def merge(even_back, odd_back, zy_near):
     return pl.pallas_call(
         merge_kernel,
         in_specs=[VMEM] * 3,
         out_specs=VMEM,
-        out_shape=shape(size, 2 * rows, BF16),
+        out_shape=shape(*even_back.shape, BF16),
         compiler_params=pltpu.CompilerParams(vmem_limit_bytes=4 * MIB),
         cost_estimate=cost(0, 0),
-    )(xz, zy_far, zy_near)
+    )(even_back, odd_back, zy_near)
 
 
 def gather(value):
@@ -290,29 +324,30 @@
         return *weigh(mine, by_x, near, far, near_part, far_part), z[:size]
 
     def no_sum(*_):
-        parts = tuple(jnp.zeros((rows // 4, n * rows), BF16) for n in (2, 1, 1))
+        parts = tuple(jnp.zeros((rows // 4, n * rows), BF16) for n in (2, 2, 1, 1))
         return *parts, jnp.zeros((size, columns), BF16)
 
     keep, send = gram(x, y, z)
-    ahead, xz, zy, z_half = lax.cond(
+    ahead, pair, xz, zy, z_half = lax.cond(
         always, summed, no_sum, keep, send, near, far, near_part, far_part, z
     )
-    back_xz = moved(xz, "blk", outward)
-    zy_far = moved(zy, "blk", [p for p in outward if p[0] % 2 == 0])
+    even_back = moved(pair, "blk", [p for p in outward if p[0] % 2 == 0])
+    odd_back = moved(xz, "blk", [p for p in outward if p[0] % 2])
     zy_near = moved(zy, "blk", [(b, b ^ 1) for b in range(0, blocks, 2)])
-    zk, xk = after((z_half, x_half), back_xz)
+    zk, xk = after((z_half, x_half), xz, w_more)
     w_half = moved(xk, "blk", outward)
-    zk, ahead = after((zk, ahead), zy_near, zy_far)
+    (zk,) = after((zk,), u_more)
     u_half = swapped(zk, "blk", 1)
-    zy_far, zy_near, back_xz = after((zy_far, zy_near, back_xz), u_more, w_more)
-    back = gather(merge(back_xz, zy_far, zy_near))
+    ahead = settle(gather(ahead))
+    back = after((even_back, odd_back, zy_near), u_more, w_more)
+    back = gather(merge(*back))
 
     places, place = [], 0
     for height in (rows, rows, rows - size, rows - first):
         places.append((place, place + height))
         place += height
-    total, weights = apply_most(places, (size, first), gather(ahead), back, (y, z, u_more, w_more))
-    return apply_last(weights, total, u_half, w_half)
+    total, weights = apply_most(places, (size, first), ahead, back, (y, z, u_more, w_more))
+    return apply_last(weights, total, u_half, w_half, seen(*after((w_half,), total)))
 
 
 def from_behind(value, by):

time: 113 us -> 111 us (0.982)
  waiting for transfers between devices: 72.1 us -> 65.4 us
  starting transfers between devices: 20.2 us -> 25.3 us
    ppermute x12, waiting for transfers between devices: 27.3 us -> 20.6 us  [swapped(): lax.ppermute(value, axis, [(i, i ^ distance) for i in range(devices)])]
    ppermute x12, starting transfers between devices: 10.5 us -> 15.2 us  [swapped(): lax.ppermute(value, axis, [(i, i ^ distance) for i in range(devices)])]
    pallas_call x2 -> x4, Pallas kernels: 2.27 us -> 2.36 us  [the longest x1 2.09 us: apply_last(): pl.pallas_call(last_kernel, in_specs=[VMEM] * 4 + [ANY], out_specs=ANY, o...]
    unnamed x12 -> x14, local copies, waits for them, and re-layouts: 2.67 us -> 2.67 us
  transfers between devices with their start and end apart: 19 -> 19, of which waited for: 10 -> 9; matrix products, arithmetic and copies ran while one was open for 2% -> 2% of each run, Pallas kernels for 11% -> 11%
where the time goes in v3:
time: 111 us
  waiting for transfers between devices  65.4 us (59%)
  starting transfers between devices  25.3 us (23%)
  Pallas kernels  14.2 us (13%)
  local copies, waits for them, and re-layouts  5.06 us (5%)
    ppermute x7, waiting for transfers between devices, moved(): return lax.ppermute(value, axis, pairs)  44.9 us
    ppermute x12, waiting for transfers between devices, swapped(): lax.ppermute(value, axis, [(i, i ^ distance) for i in range(devices)])  20.6 us
    ppermute x12, starting transfers between devices, swapped(): lax.ppermute(value, axis, [(i, i ^ distance) for i in range(devices)])  15.2 us
    ppermute x7, starting transfers between devices, moved(): return lax.ppermute(value, axis, pairs)  10.1 us
    pallas_call x1, Pallas kernels, apply_most(): pl.pallas_call(functools.partial(most_kernel, places, firsts), in_specs=[...  5.49 us
    pallas_call x1, Pallas kernels, gram(): pl.pallas_call(gram_kernel, in_specs=[VMEM] * 3, out_specs=[VMEM] * 2, ou...  3.62 us
    unnamed x14, local copies, waits for them, and re-layouts  2.67 us
    pallas_call x1, Pallas kernels, prepare(): pl.pallas_call(prepare_kernel, in_specs=[VMEM] * 3, out_specs=[VMEM] * 4...  2.55 us
  transfers between devices with their start and end apart: 19, of which 9 were waited for; matrix products, arithmetic and copies ran while one was open for 2% of the time, Pallas kernels for 11%

profile of v3, /device:TPU:0, one launch (start us, length us, event | category | flops | bytes accessed | tf_op | source)
XLA Modules:
  0.0 110.8 jit_solution(12537410362215916810)
XLA Ops:
  0.0 5.0 %collective-permute-start.3 = (bf16[512,2048]{1,0:T(8,128)(2,1)}, bf16[512,2048]{1,0:T(8,128)(2,1)S(1)}, u32[]{:S(2)}, u32[]{:S(2)}) collective-permute-start(bf16[512,2048]{1,0:T(8,128)(2,1)} %x.3), channel_id=1, source_target_pairs={{0,24},{4,12},{8,0},{12,20},{16,8},{20,28},{24,16},{28,4},{1,25},{... | collective-permute-start | bytes 6291464 | tf_op jit(solution)/shard_map/ppermute | solution.py:34
  5.1 1.7 %copy-done = bf16[512,2048]{1,0:T(8,128)(2,1)S(1)} copy-done((bf16[512,2048]{1,0:T(8,128)(2,1)S(1)}, bf16[512,2048]{1,0:T(8,128)(2,1)}, u32[]{:S(2)}) %copy-start) | copy-done | bytes 2097176
  6.7 2.5 %shard_map.37 = (bf16[240,2048]{1,0:T(8,128)(2,1)S(1)}, bf16[272,2048]{1,0:T(8,128)(2,1)}, bf16[512,128]{1,0:T(8,128)(2,1)S(1)}, bf16[512,128]{1,0:T(8,128)(2,1)S(1)}, s32[1,1]{1,0:T(1,128)}) custom-call(bf16[512,2048]{1,0:T(8,128)(2,1)S(1)} %copy-done, bf16[512,512]{1,0:T(8,128)(2,1)} %near.1, bf16[512,512]{1,0:T(8,128)(2,1)} %far.1), custom_call_target="tpu_custom_call" | custom-call | bytes 6291456 | tf_op jit(solution)/shard_map/pallas_call | solution.py:68
  10.9 3.3 %collective-permute-start.4 = (bf16[512,128]{1,0:T(8,128)(2,1)S(1)}, bf16[512,128]{1,0:T(8,128)(2,1)S(1)}, u32[]{:S(2)}, u32[]{:S(2)}) collective-permute-start(bf16[512,128]{1,0:T(8,128)(2,1)S(1)} %get-tuple-element.59), channel_id=1, source_target_pairs={{0,4},{4,0},{8,12},{12,8},{16,20},{20,16},{24,28},{28,24},{1,5},{5... | collective-permute-start | bytes 393224 | tf_op jit(solution)/shard_map/ppermute | solution.py:39
  14.2 36.2 %collective-permute-done.3.z.refs_6_ = bf16[512,2048]{1,0:T(8,128)(2,1)S(1)} collective-permute-done((bf16[512,2048]{1,0:T(8,128)(2,1)}, bf16[512,2048]{1,0:T(8,128)(2,1)S(1)}, u32[]{:S(2)}, u32[]{:S(2)}) %collective-permute-start.3) | collective-permute-done | bytes 2097184 | tf_op jit(solution)/shard_map/ppermute | solution.py:34
  50.6 1.3 %slice.6 = bf16[256,2048]{1,0:T(8,128)(2,1)} slice(bf16[512,2048]{1,0:T(8,128)(2,1)S(1)} %collective-permute-done.3.z.refs_6_), slice={[256:512], [0:2048]} | slice | bytes 2097152 | tf_op jit(solution)/shard_map/slice | solution.py:317
  51.9 3.2 %collective-permute-done.4 = bf16[512,128]{1,0:T(8,128)(2,1)S(1)} collective-permute-done((bf16[512,128]{1,0:T(8,128)(2,1)S(1)}, bf16[512,128]{1,0:T(8,128)(2,1)S(1)}, u32[]{:S(2)}, u32[]{:S(2)}) %collective-permute-start.4) | collective-permute-done | bytes 131104 | tf_op jit(solution)/shard_map/ppermute | solution.py:39
  55.2 2.9 %collective-permute-start.12 = (bf16[256,2048]{1,0:T(8,128)(2,1)}, bf16[256,2048]{1,0:T(8,128)(2,1)}, u32[]{:S(2)}, u32[]{:S(2)}) collective-permute-start(bf16[256,2048]{1,0:T(8,128)(2,1)} %slice.6), channel_id=1, source_target_pairs={{0,4},{4,0},{8,12},{12,8},{16,20},{20,16},{24,28},{28,24},{1,5},{5... | collective-permute-start | bytes 3145736 | tf_op jit(solution)/shard_map/ppermute | solution.py:39
  58.8 3.6 %shard_map.38 = (f32[256,1536]{1,0:T(8,128)S(1)}, bf16[256,1536]{1,0:T(8,128)(2,1)S(1)}) custom-call(bf16[512,2048]{1,0:T(8,128)(2,1)S(1)} %copy-done.1, bf16[512,2048]{1,0:T(8,128)(2,1)S(1)} %collective-permute-done.2.y.refs_5_, bf16[512,2048]{1,0:T(8,128)(2,1)S(1)} %collective-permute-done.3.z.refs_6_), custom_call_target="tpu_custom_call" | custom-call | tf_op jit(solution)/shard_map/pallas_call | solution.py:93
  62.4 13.9 %conditional.1 = (bf16[128,1024]{1,0:T(8,128)(2,1)S(1)}, bf16[128,1024]{1,0:T(8,128)(2,1)S(1)}, bf16[128,512]{1,0:T(8,128)(2,1)S(1)}, bf16[128,512]{1,0:T(8,128)(2,1)S(1)}, bf16[256,2048]{1,0:T(8,128)(2,1)}) conditional(s32[]{:T(128)} %bitcast, () %tuple.19, (bf16[256,1536]{1,0:T(8,128)(2,1)S(1)}, f32[256,1536]{1,0:T(8,128)S(1)}, ...), branch_computations={%region_0.0_spmd, %region_1.0_spmd} | conditional | flops 1179648 | bytes 12976248 | solution.py:331
  62.5 2.3 %collective-permute-done.other = bf16[256,1536]{1,0:T(8,128)(2,1)S(1)} collective-permute-done((bf16[256,1536]{1,0:T(8,128)(2,1)S(1)}, bf16[256,1536]{1,0:T(8,128)(2,1)S(1)}, u32[]{:S(2)}, u32[]{:S(2)}) %collective-permute-start) | collective-permute-done | bytes 786464 | tf_op jit(solution)/shard_map/cond/branch_1_fun/ppermute | solution.py:39
  64.9 1.6 %collective-permute-start.1 = (bf16[128,1536]{1,0:T(8,128)(2,1)S(1)}, bf16[128,1536]{1,0:T(8,128)(2,1)S(1)}, u32[]{:S(2)}, u32[]{:S(2)}) collective-permute-start(bf16[128,1536]{1,0:T(8,128)(2,1)S(1)} %get-tuple-element.22), channel_id=1, source_target_pairs={{0,2},{1,3},{2,0},{3,1},{4,6},{5,7},{6,4},{7,5},{8,10},{9,11},{10,... | collective-permute-start | bytes 1179656 | tf_op jit(solution)/shard_map/cond/branch_1_fun/ppermute | solution.py:39
  67.6 8.6 %collective-permute-done.1.other = bf16[128,1536]{1,0:T(8,128)(2,1)S(1)} collective-permute-done((bf16[128,1536]{1,0:T(8,128)(2,1)S(1)}, bf16[128,1536]{1,0:T(8,128)(2,1)S(1)}, u32[]{:S(2)}, u32[]{:S(2)}) %collective-permute-start.1) | collective-permute-done | bytes 393248 | tf_op jit(solution)/shard_map/cond/branch_1_fun/ppermute | solution.py:39
  76.3 2.2 %collective-permute-start.9 = (bf16[128,1024]{1,0:T(8,128)(2,1)S(1)}, bf16[128,1024]{1,0:T(8,128)(2,1)S(1)}, u32[]{:S(2)}, u32[]{:S(2)}) collective-permute-start(bf16[128,1024]{1,0:T(8,128)(2,1)S(1)} %get-tuple-element.62), channel_id=1, source_target_pairs={{0,8},{8,16},{16,24},{24,0},{1,9},{9,17},{17,25},{25,1},{2,10},{10... | collective-permute-start | bytes 786440 | tf_op jit(solution)/shard_map/ppermute | solution.py:34
  80.6 3.8 %collective-permute-start.17 = (bf16[256,2048]{1,0:T(8,128)(2,1)}, bf16[256,2048]{1,0:T(8,128)(2,1)S(1)}, u32[]{:S(2)}, u32[]{:S(2)}) collective-permute-start(bf16[256,2048]{1,0:T(8,128)(2,1)} %get-tuple-element.77), channel_id=1, source_target_pairs={{0,4},{4,0},{8,12},{12,8},{16,20},{20,16},{24,28},{28,24},{1,5},{5... | collective-permute-start | bytes 3145736 | tf_op jit(solution)/shard_map/ppermute | solution.py:39
  84.4 1.5 %collective-permute-start.6 = (bf16[128,1024]{1,0:T(8,128)(2,1)S(1)}, bf16[128,1024]{1,0:T(8,128)(2,1)S(1)}, u32[]{:S(2)}, u32[]{:S(2)}) collective-permute-start(bf16[128,1024]{1,0:T(8,128)(2,1)S(1)} %get-tuple-element.61.a0), channel_id=1, source_target_pairs={{0,2},{1,3},{2,0},{3,1},{4,6},{5,7},{6,4},{7,5},{8,10},{9,11},{10,... | collective-permute-start | bytes 786440 | tf_op jit(solution)/shard_map/ppermute | solution.py:39
  85.9 3.4 %collective-permute-done.9.even_back = bf16[128,1024]{1,0:T(8,128)(2,1)S(1)} collective-permute-done((bf16[128,1024]{1,0:T(8,128)(2,1)S(1)}, bf16[128,1024]{1,0:T(8,128)(2,1)S(1)}, u32[]{:S(2)}, u32[]{:S(2)}) %collective-permute-start.9) | collective-permute-done | bytes 262176 | tf_op jit(solution)/shard_map/ppermute | solution.py:34
  89.3 1.6 %collective-permute-start.14 = (bf16[128,1024]{1,0:T(8,128)(2,1)S(1)}, bf16[128,1024]{1,0:T(8,128)(2,1)S(1)}, u32[]{:S(2)}, u32[]{:S(2)}) collective-permute-start(bf16[128,1024]{1,0:T(8,128)(2,1)S(1)} %shard_map.40.refs_1_), channel_id=1, source_target_pairs={{0,2},{1,3},{2,0},{3,1},{4,6},{5,7},{6,4},{7,5},{8,10},{9,11},{10,... | collective-permute-start | bytes 786440 | tf_op jit(solution)/shard_map/ppermute | solution.py:39
  90.9 1.6 %collective-permute-done.6.a1 = bf16[128,1024]{1,0:T(8,128)(2,1)S(1)} collective-permute-done((bf16[128,1024]{1,0:T(8,128)(2,1)S(1)}, bf16[128,1024]{1,0:T(8,128)(2,1)S(1)}, u32[]{:S(2)}, u32[]{:S(2)}) %collective-permute-start.6) | collective-permute-done | bytes 262176 | tf_op jit(solution)/shard_map/ppermute | solution.py:39
  93.0 3.4 %collective-permute-done.14.refs_2_ = bf16[128,1024]{1,0:T(8,128)(2,1)S(1)} collective-permute-done((bf16[128,1024]{1,0:T(8,128)(2,1)S(1)}, bf16[128,1024]{1,0:T(8,128)(2,1)S(1)}, u32[]{:S(2)}, u32[]{:S(2)}) %collective-permute-start.14) | collective-permute-done | bytes 262176 | tf_op jit(solution)/shard_map/ppermute | solution.py:39
  96.5 1.4 %collective-permute-done.16.refs_4_ = bf16[128,1024]{1,0:T(8,128)(2,1)S(1)} collective-permute-done((bf16[128,1024]{1,0:T(8,128)(2,1)S(1)}, bf16[128,1024]{1,0:T(8,128)(2,1)S(1)}, u32[]{:S(2)}, u32[]{:S(2)}) %collective-permute-start.16) | collective-permute-done | bytes 262176 | tf_op jit(solution)/shard_map/ppermute | solution.py:39
  97.9 5.5 %shard_map.41 = (f32[512,2048]{1,0:T(8,128)S(1)}, bf16[512,496]{1,0:T(8,128)(2,1)S(1)}) custom-call(bf16[512,1024]{1,0:T(8,128)(2,1)S(1)} %shard_map.39.refs_0_, bf16[128,1024]{1,0:T(8,128)(2,1)S(1)} %shard_map.40.refs_1_, bf16[128,1024]{1,0:T(8,128)(2,1)S(1)} %collective-permute-done.14.refs_2_, bf16[128,1024]{1,0:T(8,128)(2,1)S(1)} %collective-permute-done.15.refs_3_, ...), custom_call_target="tpu_custom_call" | custom-call | flops 3500000000 | tf_op jit(solution)/shard_map/pallas_call | solution.py:215
  103.4 5.3 %collective-permute-done.18.value.w = bf16[240,2048]{1,0:T(8,128)(2,1)S(1)} collective-permute-done((bf16[240,2048]{1,0:T(8,128)(2,1)}, bf16[240,2048]{1,0:T(8,128)(2,1)S(1)}, u32[]{:S(2)}, u32[]{:S(2)}) %collective-permute-start.18) | collective-permute-done | bytes 983072 | tf_op jit(solution)/shard_map/ppermute | solution.py:34
  108.7 2.1 %shard_map.43 = bf16[512,2048]{1,0:T(8,128)(2,1)} custom-call(bf16[512,496]{1,0:T(8,128)(2,1)S(1)} %get-tuple-element.72.weights, f32[512,2048]{1,0:T(8,128)S(1)} %get-tuple-element.73.total, bf16[256,2048]{1,0:T(8,128)(2,1)S(1)} %collective-permute-done.17.u, bf16[240,2048]{1,0:T(8,128)(2,1)S(1)} %collective-permute-done.18.value.w, f32[8,128]{1,0:T(8,128)S(1)} %shard_map.42._), custom_call_target="tpu_custom_call" | custom-call | flops 1040187392 | bytes 8323072 | tf_op jit(solution)/shard_map/pallas_call | solution.py:247
  (40 shorter events, 6.0 us)
Async XLA Ops:
  0.0 50.4 %collective-permute-start.3 = (bf16[512,2048]{1,0:T(8,128)(2,1)}, bf16[512,2048]{1,0:T(8,128)(2,1)S(1)}, u32[]{:S(2)}, u32[]{:S(2)}) collective-permute-start(bf16[512,2048]{1,0:T(8,128)(2,1)} %x.3), channel_id=1, source_target_pairs={{0,24},{4,12},{8,0},{12,20},{16,8},{20,28},{24,16},{28,4},{1,25},{... | collective-permute-start | bytes 6291464 | tf_op jit(solution)/shard_map/ppermute | solution.py:34
  5.0 50.1 %collective-permute-start.2 = (bf16[512,2048]{1,0:T(8,128)(2,1)}, bf16[512,2048]{1,0:T(8,128)(2,1)S(1)}, u32[]{:S(2)}, u32[]{:S(2)}) collective-permute-start(bf16[512,2048]{1,0:T(8,128)(2,1)} %x.3), channel_id=1, source_target_pairs={{0,4},{4,0},{8,12},{12,8},{16,20},{20,16},{24,28},{28,24},{1,5},{5... | collective-permute-start | bytes 6291464 | tf_op jit(solution)/shard_map/ppermute | solution.py:39
  6.7 52.0 %copy-start.1 = (bf16[512,2048]{1,0:T(8,128)(2,1)S(1)}, bf16[512,2048]{1,0:T(8,128)(2,1)}, u32[]{:S(2)}) copy-start(bf16[512,2048]{1,0:T(8,128)(2,1)} %x.3) | copy-start | bytes 6291460
  10.3 4.0 %collective-permute-start.5 = (bf16[512,128]{1,0:T(8,128)(2,1)S(1)}, bf16[512,128]{1,0:T(8,128)(2,1)S(1)}, u32[]{:S(2)}, u32[]{:S(2)}) collective-permute-start(bf16[512,128]{1,0:T(8,128)(2,1)S(1)} %get-tuple-element.60), channel_id=1, source_target_pairs={{4,12},{12,20},{20,28},{28,4},{5,13},{13,21},{21,29},{29,5},{6,14}... | collective-permute-start | bytes 393224 | tf_op jit(solution)/shard_map/ppermute | solution.py:34
  10.9 44.2 %collective-permute-start.4 = (bf16[512,128]{1,0:T(8,128)(2,1)S(1)}, bf16[512,128]{1,0:T(8,128)(2,1)S(1)}, u32[]{:S(2)}, u32[]{:S(2)}) collective-permute-start(bf16[512,128]{1,0:T(8,128)(2,1)S(1)} %get-tuple-element.59), channel_id=1, source_target_pairs={{0,4},{4,0},{8,12},{12,8},{16,20},{20,16},{24,28},{28,24},{1,5},{5... | collective-permute-start | bytes 393224 | tf_op jit(solution)/shard_map/ppermute | solution.py:39
  50.4 12.0 %copy-start.3 = (bf16[512,2048]{1,0:T(8,128)(2,1)}, bf16[512,2048]{1,0:T(8,128)(2,1)S(1)}, u32[]{:S(2)}) copy-start(bf16[512,2048]{1,0:T(8,128)(2,1)S(1)} %collective-permute-done.3.z.refs_6_) | copy-start | bytes 6291460
  50.4 30.1 %collective-permute-start.13 = (bf16[272,2048]{1,0:T(8,128)(2,1)}, bf16[272,2048]{1,0:T(8,128)(2,1)S(1)}, u32[]{:S(2)}, u32[]{:S(2)}) collective-permute-start(bf16[272,2048]{1,0:T(8,128)(2,1)} %get-tuple-element.68), channel_id=1, source_target_pairs={{0,8},{4,28},{8,16},{12,4},{16,24},{20,12},{24,0},{28,20},{1,9},{5... | collective-permute-start | bytes 3342344 | tf_op jit(solution)/shard_map/ppermute | solution.py:34
  55.2 25.4 %collective-permute-start.12 = (bf16[256,2048]{1,0:T(8,128)(2,1)}, bf16[256,2048]{1,0:T(8,128)(2,1)}, u32[]{:S(2)}, u32[]{:S(2)}) collective-permute-start(bf16[256,2048]{1,0:T(8,128)(2,1)} %slice.6), channel_id=1, source_target_pairs={{0,4},{4,0},{8,12},{12,8},{16,20},{20,16},{24,28},{28,24},{1,5},{5... | collective-permute-start | bytes 3145736 | tf_op jit(solution)/shard_map/ppermute | solution.py:39
  58.7 3.7 %copy-start.5 = (bf16[512,512]{1,0:T(8,128)(2,1)S(1)}, bf16[512,512]{1,0:T(8,128)(2,1)}, u32[]{:S(2)}) copy-start(bf16[512,512]{1,0:T(8,128)(2,1)} %near.1) | copy-start | bytes 1572868
  58.8 3.7 %copy-start.6 = (bf16[512,512]{1,0:T(8,128)(2,1)S(1)}, bf16[512,512]{1,0:T(8,128)(2,1)}, u32[]{:S(2)}) copy-start(bf16[512,512]{1,0:T(8,128)(2,1)} %far.1) | copy-start | bytes 1572868
  62.4 2.4 %collective-permute-start = (bf16[256,1536]{1,0:T(8,128)(2,1)S(1)}, bf16[256,1536]{1,0:T(8,128)(2,1)S(1)}, u32[]{:S(2)}, u32[]{:S(2)}) collective-permute-start(bf16[256,1536]{1,0:T(8,128)(2,1)S(1)} %get-tuple-element.20), channel_id=1, source_target_pairs={{0,1},{1,0},{2,3},{3,2},{4,5},{5,4},{6,7},{7,6},{8,9},{9,8},{10,11... | collective-permute-start | bytes 2359304 | tf_op jit(solution)/shard_map/cond/branch_1_fun/ppermute | solution.py:39
  64.9 11.2 %collective-permute-start.1 = (bf16[128,1536]{1,0:T(8,128)(2,1)S(1)}, bf16[128,1536]{1,0:T(8,128)(2,1)S(1)}, u32[]{:S(2)}, u32[]{:S(2)}) collective-permute-start(bf16[128,1536]{1,0:T(8,128)(2,1)S(1)} %get-tuple-element.22), channel_id=1, source_target_pairs={{0,2},{1,3},{2,0},{3,1},{4,6},{5,7},{6,4},{7,5},{8,10},{9,11},{10,... | collective-permute-start | bytes 1179656 | tf_op jit(solution)/shard_map/cond/branch_1_fun/ppermute | solution.py:39
  76.3 12.9 %collective-permute-start.9 = (bf16[128,1024]{1,0:T(8,128)(2,1)S(1)}, bf16[128,1024]{1,0:T(8,128)(2,1)S(1)}, u32[]{:S(2)}, u32[]{:S(2)}) collective-permute-start(bf16[128,1024]{1,0:T(8,128)(2,1)S(1)} %get-tuple-element.62), channel_id=1, source_target_pairs={{0,8},{8,16},{16,24},{24,0},{1,9},{9,17},{17,25},{25,1},{2,10},{10... | collective-permute-start | bytes 786440 | tf_op jit(solution)/shard_map/ppermute | solution.py:34
  78.5 5.9 %collective-permute-start.11 = (bf16[128,512]{1,0:T(8,128)(2,1)S(1)}, bf16[128,512]{1,0:T(8,128)(2,1)S(1)}, u32[]{:S(2)}, u32[]{:S(2)}) collective-permute-start(bf16[128,512]{1,0:T(8,128)(2,1)S(1)} %get-tuple-element.64), channel_id=1, source_target_pairs={{0,4},{8,12},{16,20},{24,28},{1,5},{9,13},{17,21},{25,29},{2,6},{1... | collective-permute-start | bytes 393224 | tf_op jit(solution)/shard_map/ppermute | solution.py:34
  79.8 6.1 %collective-permute-start.10 = (bf16[128,512]{1,0:T(8,128)(2,1)S(1)}, bf16[128,512]{1,0:T(8,128)(2,1)S(1)}, u32[]{:S(2)}, u32[]{:S(2)}) collective-permute-start(bf16[128,512]{1,0:T(8,128)(2,1)S(1)} %get-tuple-element.63), channel_id=1, source_target_pairs={{4,28},{12,4},{20,12},{28,20},{5,29},{13,5},{21,13},{29,21},{6,30}... | collective-permute-start | bytes 393224 | tf_op jit(solution)/shard_map/ppermute | solution.py:34
  80.5 28.2 %collective-permute-start.18 = (bf16[240,2048]{1,0:T(8,128)(2,1)}, bf16[240,2048]{1,0:T(8,128)(2,1)S(1)}, u32[]{:S(2)}, u32[]{:S(2)}) collective-permute-start(bf16[240,2048]{1,0:T(8,128)(2,1)} %copy-done.2), channel_id=1, source_target_pairs={{0,8},{4,28},{8,16},{12,4},{16,24},{20,12},{24,0},{28,20},{1,9},{5... | collective-permute-start | bytes 2949128 | tf_op jit(solution)/shard_map/ppermute | solution.py:34
  80.6 28.1 %collective-permute-start.17 = (bf16[256,2048]{1,0:T(8,128)(2,1)}, bf16[256,2048]{1,0:T(8,128)(2,1)S(1)}, u32[]{:S(2)}, u32[]{:S(2)}) collective-permute-start(bf16[256,2048]{1,0:T(8,128)(2,1)} %get-tuple-element.77), channel_id=1, source_target_pairs={{0,4},{4,0},{8,12},{12,8},{16,20},{20,16},{24,28},{28,24},{1,5},{5... | collective-permute-start | bytes 3145736 | tf_op jit(solution)/shard_map/ppermute | solution.py:39
  84.4 13.5 %copy-start.4 = (bf16[512,2048]{1,0:T(8,128)(2,1)S(1)}, bf16[512,2048]{1,0:T(8,128)(2,1)}, u32[]{:S(2)}) copy-start(bf16[512,2048]{1,0:T(8,128)(2,1)} %copy-done.3) | copy-start | bytes 6291460
  84.4 8.0 %collective-permute-start.6 = (bf16[128,1024]{1,0:T(8,128)(2,1)S(1)}, bf16[128,1024]{1,0:T(8,128)(2,1)S(1)}, u32[]{:S(2)}, u32[]{:S(2)}) collective-permute-start(bf16[128,1024]{1,0:T(8,128)(2,1)S(1)} %get-tuple-element.61.a0), channel_id=1, source_target_pairs={{0,2},{1,3},{2,0},{3,1},{4,6},{5,7},{6,4},{7,5},{8,10},{9,11},{10,... | collective-permute-start | bytes 786440 | tf_op jit(solution)/shard_map/ppermute | solution.py:39
  85.9 6.5 %collective-permute-start.7 = (bf16[128,1024]{1,0:T(8,128)(2,1)S(1)}, bf16[128,1024]{1,0:T(8,128)(2,1)S(1)}, u32[]{:S(2)}, u32[]{:S(2)}) collective-permute-start(bf16[128,1024]{1,0:T(8,128)(2,1)S(1)} %get-tuple-element.61.a0), channel_id=1, source_target_pairs={{0,1},{1,0},{2,3},{3,2},{4,5},{5,4},{6,7},{7,6},{8,9},{9,8},{10,11... | collective-permute-start | bytes 786440 | tf_op jit(solution)/shard_map/ppermute | solution.py:39
  89.3 7.1 %collective-permute-start.14 = (bf16[128,1024]{1,0:T(8,128)(2,1)S(1)}, bf16[128,1024]{1,0:T(8,128)(2,1)S(1)}, u32[]{:S(2)}, u32[]{:S(2)}) collective-permute-start(bf16[128,1024]{1,0:T(8,128)(2,1)S(1)} %shard_map.40.refs_1_), channel_id=1, source_target_pairs={{0,2},{1,3},{2,0},{3,1},{4,6},{5,7},{6,4},{7,5},{8,10},{9,11},{10,... | collective-permute-start | bytes 786440 | tf_op jit(solution)/shard_map/ppermute | solution.py:39
  92.4 4.0 %collective-permute-start.8 = (bf16[128,1024]{1,0:T(8,128)(2,1)S(1)}, bf16[128,1024]{1,0:T(8,128)(2,1)S(1)}, u32[]{:S(2)}, u32[]{:S(2)}) collective-permute-start(bf16[128,1024]{1,0:T(8,128)(2,1)S(1)} %collective-permute-done.6.a1), channel_id=1, source_target_pairs={{0,1},{1,0},{2,3},{3,2},{4,5},{5,4},{6,7},{7,6},{8,9},{9,8},{10,11... | collective-permute-start | bytes 786440 | tf_op jit(solution)/shard_map/ppermute | solution.py:39
  92.5 4.1 %collective-permute-start.15 = (bf16[128,1024]{1,0:T(8,128)(2,1)S(1)}, bf16[128,1024]{1,0:T(8,128)(2,1)S(1)}, u32[]{:S(2)}, u32[]{:S(2)}) collective-permute-start(bf16[128,1024]{1,0:T(8,128)(2,1)S(1)} %shard_map.40.refs_1_), channel_id=1, source_target_pairs={{0,1},{1,0},{2,3},{3,2},{4,5},{5,4},{6,7},{7,6},{8,9},{9,8},{10,11... | collective-permute-start | bytes 786440 | tf_op jit(solution)/shard_map/ppermute | solution.py:39
  96.4 1.5 %collective-permute-start.16 = (bf16[128,1024]{1,0:T(8,128)(2,1)S(1)}, bf16[128,1024]{1,0:T(8,128)(2,1)S(1)}, u32[]{:S(2)}, u32[]{:S(2)}) collective-permute-start(bf16[128,1024]{1,0:T(8,128)(2,1)S(1)} %collective-permute-done.14.refs_2_), channel_id=1, source_target_pairs={{0,1},{1,0},{2,3},{3,2},{4,5},{5,4},{6,7},{7,6},{8,9},{9,8},{10,11... | collective-permute-start | bytes 786440 | tf_op jit(solution)/shard_map/ppermute | solution.py:39
  (2 other events, 2.7 us)

commit v4 on v3

--- a/solution.py
+++ b/solution.py
@@ -8,7 +8,7 @@
 from jax.sharding import PartitionSpec as P
 
 MIB = 1024 * 1024
-SEEN_COST, MOST_COST, SETTLE_COST = 10, 35, 10
+SEEN_COST, MOST_COST, SETTLE_COST = 10, 10, 25
 F32, BF16 = jnp.float32, jnp.bfloat16
 VMEM = pl.BlockSpec(memory_space=pltpu.VMEM)
 ANY = pl.BlockSpec(memory_space=pl.ANY)
@@ -79,8 +79,17 @@
 
 def gram_kernel(x, y, z, keep, send, total):
     rows = x.shape[0]
-    for i, (left, right) in enumerate(((x, y), (x, z), (z, y))):
-        total[:, i * rows : (i + 1) * rows] = outer(left[...], right[...])
+    even = lax.axis_index("blk") % 2 == 0
+
+    @pl.when(even)
+    def _():
+        total[:, :rows] = outer(z[...], y[...])
+
+    @pl.when(jnp.logical_not(even))
+    def _():
+        total[:, :rows] = outer(x[...], y[...])
+
+    total[:, rows:] = outer(x[...], z[...])
     quarter = rows // 4
     for distance in range(4):
         target, kind = (keep, F32) if distance < 2 else (send, BF16)
@@ -94,8 +103,8 @@
         gram_kernel,
         in_specs=[VMEM] * 3,
         out_specs=[VMEM] * 2,
-        out_shape=[shape(rows // 2, 3 * rows, F32), shape(rows // 2, 3 * rows, BF16)],
-        scratch_shapes=[pltpu.VMEM((rows, 3 * rows), F32)],
+        out_shape=[shape(rows // 2, 2 * rows, F32), shape(rows // 2, 2 * rows, BF16)],
+        scratch_shapes=[pltpu.VMEM((rows, 2 * rows), F32)],
         compiler_params=pltpu.CompilerParams(vmem_limit_bytes=20 * MIB),
         cost_estimate=cost(0, 0),
     )(x, y, z)
@@ -119,35 +128,30 @@
     )(keep, other)
 
 
-def weigh_kernel(mine, other, near, far, near_other, far_other, ahead, pair, xz, zy):
-    rows = near.shape[0]
-    here = quarter_rows(rows)
+def weigh_kernel(mine, other, far, near_other, far_other, pair, xz, by_y):
+    rows = far.shape[0]
     even = lax.axis_index("blk") % 2 == 0
     gram = mine[...] + other[...].astype(F32)
-    near_turned = near_other[...].astype(F32).T
     far_turned = far_other[...].astype(F32).T
-    near_slab = jnp.where(even, near[here, :].astype(F32), near_turned)
-    far_slab = jnp.where(even, far[here, :].astype(F32), far_turned)
-    ahead[:, :rows] = (gram[:, :rows] * near_slab).astype(BF16)
-    weighted = (gram[:, rows : 2 * rows] * far_slab).astype(BF16)
-    ahead[:, rows:] = weighted
+    far_slab = jnp.where(even, far[quarter_rows(rows), :].astype(F32), far_turned)
+    weighted = (gram[:, rows:] * far_slab).astype(BF16)
     xz[...] = weighted
     pair[:, :rows] = weighted
-    weighted = (gram[:, 2 * rows :] * near_turned).astype(BF16)
+    weighted = (gram[:, :rows] * near_other[...].astype(F32).T).astype(BF16)
+    by_y[...] = weighted
     pair[:, rows:] = weighted
-    zy[...] = weighted
-
-
-def weigh(mine, other, near, far, near_other, far_other):
-    size, rows = mine.shape[0], near.shape[0]
+
+
+def weigh(mine, other, far, near_other, far_other):
+    size, rows = mine.shape[0], far.shape[0]
     return pl.pallas_call(
         weigh_kernel,
-        in_specs=[VMEM] * 6,
-        out_specs=[VMEM] * 4,
-        out_shape=[shape(size, n * rows, BF16) for n in (2, 2, 1, 1)],
+        in_specs=[VMEM] * 5,
+        out_specs=[VMEM] * 3,
+        out_shape=[shape(size, n * rows, BF16) for n in (2, 1, 1)],
         compiler_params=pltpu.CompilerParams(vmem_limit_bytes=8 * MIB),
         cost_estimate=cost(6 * size * rows, 40 * size * rows),
-    )(mine, other, near, far, near_other, far_other)
+    )(mine, other, far, near_other, far_other)
 
 
 def settle_kernel(a0, a1, a2, a3, out):
@@ -179,23 +183,25 @@
         copies[-1].start()
 
     even = lax.axis_index("blk") % 2 == 0
-    weights[:, : 2 * rows] = ahead[...]
+    weights[:, rows : 2 * rows] = ahead[...]
     for distance in range(4):
         here = quarter_rows(rows, distance)
-        weights[:, pl.ds(pl.multiple_of(3 * rows + here.start, size), size)] = (
-            back[distance][:, :rows].astype(F32).T.astype(BF16)
-        )
-        near = back[distance][:, rows:]
+        xw, xu, xy = (back[distance][:, i * rows : (i + 1) * rows] for i in range(3))
+
+        def across(i):
+            return pl.ds(pl.multiple_of(i * rows + here.start, size), size)
+
+        weights[:, across(3)] = xw.astype(F32).T.astype(BF16)
 
         @pl.when(even)
         def _():
-            weights[here, 2 * rows : 3 * rows] = near
+            weights[here, 2 * rows : 3 * rows] = xu
+            weights[:, across(0)] = xy.astype(F32).T.astype(BF16)
 
         @pl.when(jnp.logical_not(even))
         def _():
-            weights[:, pl.ds(pl.multiple_of(2 * rows + here.start, size), size)] = (
-                near.astype(F32).T.astype(BF16)
-            )
+            weights[here, :rows] = xy
+            weights[:, across(2)] = xu.astype(F32).T.astype(BF16)
 
     put, place = 0, 2 * rows
     for i, first in zip((2, 3), firsts):
@@ -270,29 +276,32 @@
     )(value)
 
 
-def merge_kernel(even_back, odd_back, zy_near, out):
-    rows = zy_near.shape[1]
+def merge_kernel(even_back, odd_back, by_y, own, out):
+    rows = own.shape[1]
     even = lax.axis_index("blk") % 2 == 0
 
     @pl.when(even)
     def _():
-        out[...] = even_back[...]
+        out[:, : 2 * rows] = even_back[...]
+        out[:, 2 * rows :] = by_y[...]
 
     @pl.when(jnp.logical_not(even))
     def _():
         out[:, :rows] = odd_back[...]
-        out[:, rows:] = zy_near[...]
-
-
-def merge(even_back, odd_back, zy_near):
+        out[:, rows : 2 * rows] = by_y[...]
+        out[:, 2 * rows :] = own[...]
+
+
+def merge(even_back, odd_back, by_y, own):
+    size, rows = own.shape
     return pl.pallas_call(
         merge_kernel,
-        in_specs=[VMEM] * 3,
+        in_specs=[VMEM] * 4,
         out_specs=VMEM,
-        out_shape=shape(*even_back.shape, BF16),
+        out_shape=shape(size, 3 * rows, BF16),
         compiler_params=pltpu.CompilerParams(vmem_limit_bytes=4 * MIB),
         cost_estimate=cost(0, 0),
-    )(even_back, odd_back, zy_near)
+    )(even_back, odd_back, by_y, own)
 
 
 def gather(value):
@@ -318,28 +327,26 @@
 
     always = flag[0, 0] == 1
 
-    def summed(keep, send, near, far, near_part, far_part, z):
+    def summed(keep, send, far, near_part, far_part, z):
         mine, send = fold(keep, swapped(send, "orb", 1))
         by_x = swapped(send, "orb", 2)
-        return *weigh(mine, by_x, near, far, near_part, far_part), z[:size]
+        return *weigh(mine, by_x, far, near_part, far_part), z[:size]
 
     def no_sum(*_):
-        parts = tuple(jnp.zeros((rows // 4, n * rows), BF16) for n in (2, 2, 1, 1))
+        parts = tuple(jnp.zeros((rows // 4, n * rows), BF16) for n in (2, 1, 1))
         return *parts, jnp.zeros((size, columns), BF16)
 
     keep, send = gram(x, y, z)
-    ahead, pair, xz, zy, z_half = lax.cond(
-        always, summed, no_sum, keep, send, near, far, near_part, far_part, z
-    )
+    pair, xz, own, z_half = lax.cond(always, summed, no_sum, keep, send, far, near_part, far_part, z)
     even_back = moved(pair, "blk", [p for p in outward if p[0] % 2 == 0])
     odd_back = moved(xz, "blk", [p for p in outward if p[0] % 2])
-    zy_near = moved(zy, "blk", [(b, b ^ 1) for b in range(0, blocks, 2)])
+    by_y = swapped(own, "blk", 1)
     zk, xk = after((z_half, x_half), xz, w_more)
     w_half = moved(xk, "blk", outward)
     (zk,) = after((zk,), u_more)
     u_half = swapped(zk, "blk", 1)
-    ahead = settle(gather(ahead))
-    back = after((even_back, odd_back, zy_near), u_more, w_more)
+    ahead = settle(gather(xz))
+    back = after((even_back, odd_back, by_y, own), u_more, w_more)
     back = gather(merge(*back))
 
     places, place = [], 0

time: 111 us -> 108 us (0.973)
  starting transfers between devices: 25.3 us -> 21.5 us
  Pallas kernels: 14.2 us -> 13 us
    ppermute x12 -> x13, waiting for transfers between devices: 20.6 us -> 25.5 us  [swapped(): lax.ppermute(value, axis, [(i, i ^ distance) for i in range(devices)])]
    ppermute x7 -> x6, waiting for transfers between devices: 44.9 us -> 40.8 us  [moved(): return lax.ppermute(value, axis, pairs)]
    ppermute x12 -> x13, starting transfers between devices: 15.2 us -> 12.8 us  [swapped(): lax.ppermute(value, axis, [(i, i ^ distance) for i in range(devices)])]
    ppermute x7 -> x6, starting transfers between devices: 10.1 us -> 8.73 us  [moved(): return lax.ppermute(value, axis, pairs)]
  transfers between devices with their start and end apart: 19 -> 19, of which waited for: 9 -> 13; matrix products, arithmetic and copies ran while one was open for 2% -> 2% of each run, Pallas kernels for 11% -> 10%
where the time goes in v4:
time: 108 us
  waiting for transfers between devices  66.3 us (61%)
  starting transfers between devices  21.5 us (20%)
  Pallas kernels  13 us (12%)
  local copies, waits for them, and re-layouts  6.09 us (6%)
    ppermute x6, waiting for transfers between devices, moved(): return lax.ppermute(value, axis, pairs)  40.8 us
    ppermute x13, waiting for transfers between devices, swapped(): lax.ppermute(value, axis, [(i, i ^ distance) for i in range(devices)])  25.5 us
    ppermute x13, starting transfers between devices, swapped(): lax.ppermute(value, axis, [(i, i ^ distance) for i in range(devices)])  12.8 us
    ppermute x6, starting transfers between devices, moved(): return lax.ppermute(value, axis, pairs)  8.73 us
    pallas_call x1, Pallas kernels, apply_most(): pl.pallas_call(functools.partial(most_kernel, places, firsts), in_specs=[...  5.53 us
    unnamed x14, local copies, waits for them, and re-layouts  3.7 us
    pallas_call x1, Pallas kernels, gram(): pl.pallas_call(gram_kernel, in_specs=[VMEM] * 3, out_specs=[VMEM] * 2, ou...  2.69 us
    pallas_call x1, Pallas kernels, prepare(): pl.pallas_call(prepare_kernel, in_specs=[VMEM] * 3, out_specs=[VMEM] * 4...  2.39 us
  transfers between devices with their start and end apart: 19, of which 13 were waited for; matrix products, arithmetic and copies ran while one was open for 2% of the time, Pallas kernels for 10%

profile of v4, /device:TPU:0, one launch (start us, length us, event | category | flops | bytes accessed | tf_op | source)
XLA Modules:
  0.0 107.8 jit_solution(6723507677047164026)
XLA Ops:
  0.0 5.0 %collective-permute-start.3 = (bf16[512,2048]{1,0:T(8,128)(2,1)}, bf16[512,2048]{1,0:T(8,128)(2,1)S(1)}, u32[]{:S(2)}, u32[]{:S(2)}) collective-permute-start(bf16[512,2048]{1,0:T(8,128)(2,1)} %x.3), channel_id=1, source_target_pairs={{0,24},{4,12},{8,0},{12,20},{16,8},{20,28},{24,16},{28,4},{1,25},{... | collective-permute-start | bytes 6291464 | tf_op jit(solution)/shard_map/ppermute | solution.py:34
  5.1 1.7 %copy-done = bf16[512,2048]{1,0:T(8,128)(2,1)S(1)} copy-done((bf16[512,2048]{1,0:T(8,128)(2,1)S(1)}, bf16[512,2048]{1,0:T(8,128)(2,1)}, u32[]{:S(2)}) %copy-start) | copy-done | bytes 2097176
  7.8 2.4 %shard_map.37 = (bf16[240,2048]{1,0:T(8,128)(2,1)S(1)}, bf16[272,2048]{1,0:T(8,128)(2,1)}, bf16[512,128]{1,0:T(8,128)(2,1)S(1)}, bf16[512,128]{1,0:T(8,128)(2,1)S(1)}, s32[1,1]{1,0:T(1,128)}) custom-call(bf16[512,2048]{1,0:T(8,128)(2,1)S(1)} %copy-done, bf16[512,512]{1,0:T(8,128)(2,1)S(1)} %copy-done.2, bf16[512,512]{1,0:T(8,128)(2,1)} %far.1), custom_call_target="tpu_custom_call" | custom-call | bytes 6291456 | tf_op jit(solution)/shard_map/pallas_call | solution.py:68
  11.8 3.3 %collective-permute-start.4 = (bf16[512,128]{1,0:T(8,128)(2,1)S(1)}, bf16[512,128]{1,0:T(8,128)(2,1)S(1)}, u32[]{:S(2)}, u32[]{:S(2)}) collective-permute-start(bf16[512,128]{1,0:T(8,128)(2,1)S(1)} %get-tuple-element.55), channel_id=1, source_target_pairs={{0,4},{4,0},{8,12},{12,8},{16,20},{20,16},{24,28},{28,24},{1,5},{5... | collective-permute-start | bytes 393224 | tf_op jit(solution)/shard_map/ppermute | solution.py:39
  15.1 35.3 %collective-permute-done.3.z.refs_6_ = bf16[512,2048]{1,0:T(8,128)(2,1)S(1)} collective-permute-done((bf16[512,2048]{1,0:T(8,128)(2,1)}, bf16[512,2048]{1,0:T(8,128)(2,1)S(1)}, u32[]{:S(2)}, u32[]{:S(2)}) %collective-permute-start.3) | collective-permute-done | bytes 2097184 | tf_op jit(solution)/shard_map/ppermute | solution.py:34
  50.6 1.3 %slice.6 = bf16[256,2048]{1,0:T(8,128)(2,1)} slice(bf16[512,2048]{1,0:T(8,128)(2,1)S(1)} %collective-permute-done.3.z.refs_6_), slice={[256:512], [0:2048]} | slice | bytes 2097152 | tf_op jit(solution)/shard_map/slice | solution.py:326
  51.9 3.2 %collective-permute-done.4 = bf16[512,128]{1,0:T(8,128)(2,1)S(1)} collective-permute-done((bf16[512,128]{1,0:T(8,128)(2,1)S(1)}, bf16[512,128]{1,0:T(8,128)(2,1)S(1)}, u32[]{:S(2)}, u32[]{:S(2)}) %collective-permute-start.4) | collective-permute-done | bytes 131104 | tf_op jit(solution)/shard_map/ppermute | solution.py:39
  55.2 2.9 %collective-permute-start.12 = (bf16[256,2048]{1,0:T(8,128)(2,1)}, bf16[256,2048]{1,0:T(8,128)(2,1)}, u32[]{:S(2)}, u32[]{:S(2)}) collective-permute-start(bf16[256,2048]{1,0:T(8,128)(2,1)} %slice.6), channel_id=1, source_target_pairs={{0,4},{4,0},{8,12},{12,8},{16,20},{20,16},{24,28},{28,24},{1,5},{5... | collective-permute-start | bytes 3145736 | tf_op jit(solution)/shard_map/ppermute | solution.py:39
  58.8 2.7 %shard_map.38 = (f32[256,1024]{1,0:T(8,128)S(1)}, bf16[256,1024]{1,0:T(8,128)(2,1)S(1)}) custom-call(bf16[512,2048]{1,0:T(8,128)(2,1)S(1)} %copy-done.1, bf16[512,2048]{1,0:T(8,128)(2,1)S(1)} %collective-permute-done.2.y.refs_5_, bf16[512,2048]{1,0:T(8,128)(2,1)S(1)} %collective-permute-done.3.z.refs_6_), custom_call_target="tpu_custom_call" | custom-call | tf_op jit(solution)/shard_map/pallas_call | solution.py:102
  61.5 10.6 %conditional.1 = (bf16[128,1024]{1,0:T(8,128)(2,1)S(1)}, bf16[128,512]{1,0:T(8,128)(2,1)S(1)}, bf16[128,512]{1,0:T(8,128)(2,1)S(1)}, bf16[256,2048]{1,0:T(8,128)(2,1)}) conditional(s32[]{:T(128)} %bitcast, () %tuple.19, (bf16[256,1024]{1,0:T(8,128)(2,1)S(1)}, f32[256,1024]{1,0:T(8,128)S(1)}, bf16[512,512]{1,0:T(8,128)(2,1)S(1)}, ...), branch_computations={%region_0.0_spmd, %region_1.0_spmd} | conditional | flops 917504 | bytes 10223728 | solution.py:340
  61.6 1.9 %collective-permute-done.other = bf16[256,1024]{1,0:T(8,128)(2,1)S(1)} collective-permute-done((bf16[256,1024]{1,0:T(8,128)(2,1)S(1)}, bf16[256,1024]{1,0:T(8,128)(2,1)S(1)}, u32[]{:S(2)}, u32[]{:S(2)}) %collective-permute-start) | collective-permute-done | bytes 524320 | tf_op jit(solution)/shard_map/cond/branch_1_fun/ppermute | solution.py:39
  63.6 1.6 %collective-permute-start.1 = (bf16[128,1024]{1,0:T(8,128)(2,1)S(1)}, bf16[128,1024]{1,0:T(8,128)(2,1)S(1)}, u32[]{:S(2)}, u32[]{:S(2)}) collective-permute-start(bf16[128,1024]{1,0:T(8,128)(2,1)S(1)} %get-tuple-element.20), channel_id=1, source_target_pairs={{0,2},{1,3},{2,0},{3,1},{4,6},{5,7},{6,4},{7,5},{8,10},{9,11},{10,... | collective-permute-start | bytes 786440 | tf_op jit(solution)/shard_map/cond/branch_1_fun/ppermute | solution.py:39
  66.2 5.8 %collective-permute-done.1.other = bf16[128,1024]{1,0:T(8,128)(2,1)S(1)} collective-permute-done((bf16[128,1024]{1,0:T(8,128)(2,1)S(1)}, bf16[128,1024]{1,0:T(8,128)(2,1)S(1)}, u32[]{:S(2)}, u32[]{:S(2)}) %collective-permute-start.1) | collective-permute-done | bytes 262176 | tf_op jit(solution)/shard_map/cond/branch_1_fun/ppermute | solution.py:39
  72.1 2.2 %collective-permute-start.9 = (bf16[128,1024]{1,0:T(8,128)(2,1)S(1)}, bf16[128,1024]{1,0:T(8,128)(2,1)S(1)}, u32[]{:S(2)}, u32[]{:S(2)}) collective-permute-start(bf16[128,1024]{1,0:T(8,128)(2,1)S(1)} %get-tuple-element.58), channel_id=1, source_target_pairs={{0,8},{8,16},{16,24},{24,0},{1,9},{9,17},{17,25},{25,1},{2,10},{10... | collective-permute-start | bytes 786440 | tf_op jit(solution)/shard_map/ppermute | solution.py:34
  75.1 3.7 %collective-permute-done.13.refs_8_ = bf16[272,2048]{1,0:T(8,128)(2,1)S(1)} collective-permute-done((bf16[272,2048]{1,0:T(8,128)(2,1)}, bf16[272,2048]{1,0:T(8,128)(2,1)S(1)}, u32[]{:S(2)}, u32[]{:S(2)}) %collective-permute-start.13) | collective-permute-done | bytes 1114144 | tf_op jit(solution)/shard_map/ppermute | solution.py:34
  78.8 3.0 %collective-permute-done.12.refs_7_ = bf16[256,2048]{1,0:T(8,128)(2,1)} collective-permute-done((bf16[256,2048]{1,0:T(8,128)(2,1)}, bf16[256,2048]{1,0:T(8,128)(2,1)}, u32[]{:S(2)}, u32[]{:S(2)}) %collective-permute-start.12) | collective-permute-done | bytes 1048608 | tf_op jit(solution)/shard_map/ppermute | solution.py:39
  81.8 2.6 %collective-permute-start.17 = (bf16[256,2048]{1,0:T(8,128)(2,1)}, bf16[256,2048]{1,0:T(8,128)(2,1)S(1)}, u32[]{:S(2)}, u32[]{:S(2)}) collective-permute-start(bf16[256,2048]{1,0:T(8,128)(2,1)} %get-tuple-element.73), channel_id=1, source_target_pairs={{0,4},{4,0},{8,12},{12,8},{16,20},{20,16},{24,28},{28,24},{1,5},{5... | collective-permute-start | bytes 3145736 | tf_op jit(solution)/shard_map/ppermute | solution.py:39
  85.1 1.6 %collective-permute-start.14 = (bf16[128,1536]{1,0:T(8,128)(2,1)S(1)}, bf16[128,1536]{1,0:T(8,128)(2,1)S(1)}, u32[]{:S(2)}, u32[]{:S(2)}) collective-permute-start(bf16[128,1536]{1,0:T(8,128)(2,1)S(1)} %shard_map.40.refs_1_), channel_id=1, source_target_pairs={{0,2},{1,3},{2,0},{3,1},{4,6},{5,7},{6,4},{7,5},{8,10},{9,11},{10,... | collective-permute-start | bytes 1179656 | tf_op jit(solution)/shard_map/ppermute | solution.py:39
  88.2 7.3 %collective-permute-done.14.refs_2_ = bf16[128,1536]{1,0:T(8,128)(2,1)S(1)} collective-permute-done((bf16[128,1536]{1,0:T(8,128)(2,1)S(1)}, bf16[128,1536]{1,0:T(8,128)(2,1)S(1)}, u32[]{:S(2)}, u32[]{:S(2)}) %collective-permute-start.14) | collective-permute-done | bytes 393248 | tf_op jit(solution)/shard_map/ppermute | solution.py:39
  95.5 1.4 %collective-permute-done.6.a1 = bf16[128,512]{1,0:T(8,128)(2,1)S(1)} collective-permute-done((bf16[128,512]{1,0:T(8,128)(2,1)S(1)}, bf16[128,512]{1,0:T(8,128)(2,1)S(1)}, u32[]{:S(2)}, u32[]{:S(2)}) %collective-permute-start.6) | collective-permute-done | bytes 131104 | tf_op jit(solution)/shard_map/ppermute | solution.py:39
  96.9 1.3 %collective-permute-done.8.a3 = bf16[128,512]{1,0:T(8,128)(2,1)S(1)} collective-permute-done((bf16[128,512]{1,0:T(8,128)(2,1)S(1)}, bf16[128,512]{1,0:T(8,128)(2,1)S(1)}, u32[]{:S(2)}, u32[]{:S(2)}) %collective-permute-start.8) | collective-permute-done | bytes 131104 | tf_op jit(solution)/shard_map/ppermute | solution.py:39
  98.3 5.5 %shard_map.41 = (f32[512,2048]{1,0:T(8,128)S(1)}, bf16[512,496]{1,0:T(8,128)(2,1)S(1)}) custom-call(bf16[512,512]{1,0:T(8,128)(2,1)S(1)} %shard_map.39.refs_0_, bf16[128,1536]{1,0:T(8,128)(2,1)S(1)} %shard_map.40.refs_1_, bf16[128,1536]{1,0:T(8,128)(2,1)S(1)} %collective-permute-done.14.refs_2_, bf16[128,1536]{1,0:T(8,128)(2,1)S(1)} %collective-permute-done.15.refs_3_, ...), custom_call_target="tpu_custom_call" | custom-call | flops 1000000000 | tf_op jit(solution)/shard_map/pallas_call | solution.py:221
  103.9 1.2 %collective-permute-done.18.value.w = bf16[240,2048]{1,0:T(8,128)(2,1)S(1)} collective-permute-done((bf16[240,2048]{1,0:T(8,128)(2,1)}, bf16[240,2048]{1,0:T(8,128)(2,1)S(1)}, u32[]{:S(2)}, u32[]{:S(2)}) %collective-permute-start.18) | collective-permute-done | bytes 983072 | tf_op jit(solution)/shard_map/ppermute | solution.py:34
  105.7 2.1 %shard_map.43 = bf16[512,2048]{1,0:T(8,128)(2,1)} custom-call(bf16[512,496]{1,0:T(8,128)(2,1)S(1)} %get-tuple-element.68.weights, f32[512,2048]{1,0:T(8,128)S(1)} %get-tuple-element.69.total, bf16[256,2048]{1,0:T(8,128)(2,1)S(1)} %collective-permute-done.17.u, bf16[240,2048]{1,0:T(8,128)(2,1)S(1)} %collective-permute-done.18.value.w, f32[8,128]{1,0:T(8,128)S(1)} %shard_map.42._), custom_call_target="tpu_custom_call" | custom-call | flops 1040187392 | bytes 8323072 | tf_op jit(solution)/shard_map/pallas_call | solution.py:253
  (40 shorter events, 7.9 us)
Async XLA Ops:
  0.0 50.4 %collective-permute-start.3 = (bf16[512,2048]{1,0:T(8,128)(2,1)}, bf16[512,2048]{1,0:T(8,128)(2,1)S(1)}, u32[]{:S(2)}, u32[]{:S(2)}) collective-permute-start(bf16[512,2048]{1,0:T(8,128)(2,1)} %x.3), channel_id=1, source_target_pairs={{0,24},{4,12},{8,0},{12,20},{16,8},{20,28},{24,16},{28,4},{1,25},{... | collective-permute-start | bytes 6291464 | tf_op jit(solution)/shard_map/ppermute | solution.py:34
  5.0 50.1 %collective-permute-start.2 = (bf16[512,2048]{1,0:T(8,128)(2,1)}, bf16[512,2048]{1,0:T(8,128)(2,1)S(1)}, u32[]{:S(2)}, u32[]{:S(2)}) collective-permute-start(bf16[512,2048]{1,0:T(8,128)(2,1)} %x.3), channel_id=1, source_target_pairs={{0,4},{4,0},{8,12},{12,8},{16,20},{20,16},{24,28},{28,24},{1,5},{5... | collective-permute-start | bytes 6291464 | tf_op jit(solution)/shard_map/ppermute | solution.py:39
  5.1 1.7 %copy-start = (bf16[512,2048]{1,0:T(8,128)(2,1)S(1)}, bf16[512,2048]{1,0:T(8,128)(2,1)}, u32[]{:S(2)}) copy-start(bf16[512,2048]{1,0:T(8,128)(2,1)} %x.3) | copy-start | bytes 6291460
  7.8 51.0 %copy-start.1 = (bf16[512,2048]{1,0:T(8,128)(2,1)S(1)}, bf16[512,2048]{1,0:T(8,128)(2,1)}, u32[]{:S(2)}) copy-start(bf16[512,2048]{1,0:T(8,128)(2,1)} %x.3) | copy-start | bytes 6291460
  11.1 4.0 %collective-permute-start.5 = (bf16[512,128]{1,0:T(8,128)(2,1)S(1)}, bf16[512,128]{1,0:T(8,128)(2,1)S(1)}, u32[]{:S(2)}, u32[]{:S(2)}) collective-permute-start(bf16[512,128]{1,0:T(8,128)(2,1)S(1)} %get-tuple-element.56), channel_id=1, source_target_pairs={{4,12},{12,20},{20,28},{28,4},{5,13},{13,21},{21,29},{29,5},{6,14}... | collective-permute-start | bytes 393224 | tf_op jit(solution)/shard_map/ppermute | solution.py:34
  11.8 43.3 %collective-permute-start.4 = (bf16[512,128]{1,0:T(8,128)(2,1)S(1)}, bf16[512,128]{1,0:T(8,128)(2,1)S(1)}, u32[]{:S(2)}, u32[]{:S(2)}) collective-permute-start(bf16[512,128]{1,0:T(8,128)(2,1)S(1)} %get-tuple-element.55), channel_id=1, source_target_pairs={{0,4},{4,0},{8,12},{12,8},{16,20},{20,16},{24,28},{28,24},{1,5},{5... | collective-permute-start | bytes 393224 | tf_op jit(solution)/shard_map/ppermute | solution.py:39
  50.4 11.0 %copy-start.4 = (bf16[512,2048]{1,0:T(8,128)(2,1)}, bf16[512,2048]{1,0:T(8,128)(2,1)S(1)}, u32[]{:S(2)}) copy-start(bf16[512,2048]{1,0:T(8,128)(2,1)S(1)} %collective-permute-done.3.z.refs_6_) | copy-start | bytes 6291460
  50.4 28.3 %collective-permute-start.13 = (bf16[272,2048]{1,0:T(8,128)(2,1)}, bf16[272,2048]{1,0:T(8,128)(2,1)S(1)}, u32[]{:S(2)}, u32[]{:S(2)}) collective-permute-start(bf16[272,2048]{1,0:T(8,128)(2,1)} %get-tuple-element.63), channel_id=1, source_target_pairs={{0,8},{4,28},{8,16},{12,4},{16,24},{20,12},{24,0},{28,20},{1,9},{5... | collective-permute-start | bytes 3342344 | tf_op jit(solution)/shard_map/ppermute | solution.py:34
  55.2 26.6 %collective-permute-start.12 = (bf16[256,2048]{1,0:T(8,128)(2,1)}, bf16[256,2048]{1,0:T(8,128)(2,1)}, u32[]{:S(2)}, u32[]{:S(2)}) collective-permute-start(bf16[256,2048]{1,0:T(8,128)(2,1)} %slice.6), channel_id=1, source_target_pairs={{0,4},{4,0},{8,12},{12,8},{16,20},{20,16},{24,28},{28,24},{1,5},{5... | collective-permute-start | bytes 3145736 | tf_op jit(solution)/shard_map/ppermute | solution.py:39
  58.7 2.7 %copy-start.6 = (bf16[512,512]{1,0:T(8,128)(2,1)S(1)}, bf16[512,512]{1,0:T(8,128)(2,1)}, u32[]{:S(2)}) copy-start(bf16[512,512]{1,0:T(8,128)(2,1)} %far.1) | copy-start | bytes 1572868
  61.5 2.0 %collective-permute-start = (bf16[256,1024]{1,0:T(8,128)(2,1)S(1)}, bf16[256,1024]{1,0:T(8,128)(2,1)S(1)}, u32[]{:S(2)}, u32[]{:S(2)}) collective-permute-start(bf16[256,1024]{1,0:T(8,128)(2,1)S(1)} %get-tuple-element.18), channel_id=1, source_target_pairs={{0,1},{1,0},{2,3},{3,2},{4,5},{5,4},{6,7},{7,6},{8,9},{9,8},{10,11... | collective-permute-start | bytes 1572872 | tf_op jit(solution)/shard_map/cond/branch_1_fun/ppermute | solution.py:39
  63.6 8.4 %collective-permute-start.1 = (bf16[128,1024]{1,0:T(8,128)(2,1)S(1)}, bf16[128,1024]{1,0:T(8,128)(2,1)S(1)}, u32[]{:S(2)}, u32[]{:S(2)}) collective-permute-start(bf16[128,1024]{1,0:T(8,128)(2,1)S(1)} %get-tuple-element.20), channel_id=1, source_target_pairs={{0,2},{1,3},{2,0},{3,1},{4,6},{5,7},{6,4},{7,5},{8,10},{9,11},{10,... | collective-permute-start | bytes 786440 | tf_op jit(solution)/shard_map/cond/branch_1_fun/ppermute | solution.py:39
  72.1 12.9 %collective-permute-start.9 = (bf16[128,1024]{1,0:T(8,128)(2,1)S(1)}, bf16[128,1024]{1,0:T(8,128)(2,1)S(1)}, u32[]{:S(2)}, u32[]{:S(2)}) collective-permute-start(bf16[128,1024]{1,0:T(8,128)(2,1)S(1)} %get-tuple-element.58), channel_id=1, source_target_pairs={{0,8},{8,16},{16,24},{24,0},{1,9},{9,17},{17,25},{25,1},{2,10},{10... | collective-permute-start | bytes 786440 | tf_op jit(solution)/shard_map/ppermute | solution.py:34
  74.3 10.1 %collective-permute-start.11 = (bf16[128,512]{1,0:T(8,128)(2,1)S(1)}, bf16[128,512]{1,0:T(8,128)(2,1)S(1)}, u32[]{:S(2)}, u32[]{:S(2)}) collective-permute-start(bf16[128,512]{1,0:T(8,128)(2,1)S(1)} %get-tuple-element.67.own), channel_id=1, source_target_pairs={{0,4},{4,0},{8,12},{12,8},{16,20},{20,16},{24,28},{28,24},{1,5},{5... | collective-permute-start | bytes 393224 | tf_op jit(solution)/shard_map/ppermute | solution.py:39
  74.4 10.0 %collective-permute-start.10 = (bf16[128,512]{1,0:T(8,128)(2,1)S(1)}, bf16[128,512]{1,0:T(8,128)(2,1)S(1)}, u32[]{:S(2)}, u32[]{:S(2)}) collective-permute-start(bf16[128,512]{1,0:T(8,128)(2,1)S(1)} %get-tuple-element.57.a0), channel_id=1, source_target_pairs={{4,28},{12,4},{20,12},{28,20},{5,29},{13,5},{21,13},{29,21},{6,30}... | collective-permute-start | bytes 393224 | tf_op jit(solution)/shard_map/ppermute | solution.py:34
  78.8 26.2 %collective-permute-start.18 = (bf16[240,2048]{1,0:T(8,128)(2,1)}, bf16[240,2048]{1,0:T(8,128)(2,1)S(1)}, u32[]{:S(2)}, u32[]{:S(2)}) collective-permute-start(bf16[240,2048]{1,0:T(8,128)(2,1)} %copy-done.3), channel_id=1, source_target_pairs={{0,8},{4,28},{8,16},{12,4},{16,24},{20,12},{24,0},{28,20},{1,9},{5... | collective-permute-start | bytes 2949128 | tf_op jit(solution)/shard_map/ppermute | solution.py:34
  81.8 23.9 %collective-permute-start.17 = (bf16[256,2048]{1,0:T(8,128)(2,1)}, bf16[256,2048]{1,0:T(8,128)(2,1)S(1)}, u32[]{:S(2)}, u32[]{:S(2)}) collective-permute-start(bf16[256,2048]{1,0:T(8,128)(2,1)} %get-tuple-element.73), channel_id=1, source_target_pairs={{0,4},{4,0},{8,12},{12,8},{16,20},{20,16},{24,28},{28,24},{1,5},{5... | collective-permute-start | bytes 3145736 | tf_op jit(solution)/shard_map/ppermute | solution.py:39
  85.1 13.2 %copy-start.5 = (bf16[512,2048]{1,0:T(8,128)(2,1)S(1)}, bf16[512,2048]{1,0:T(8,128)(2,1)}, u32[]{:S(2)}) copy-start(bf16[512,2048]{1,0:T(8,128)(2,1)} %copy-done.4) | copy-start | bytes 6291460
  85.1 10.4 %collective-permute-start.14 = (bf16[128,1536]{1,0:T(8,128)(2,1)S(1)}, bf16[128,1536]{1,0:T(8,128)(2,1)S(1)}, u32[]{:S(2)}, u32[]{:S(2)}) collective-permute-start(bf16[128,1536]{1,0:T(8,128)(2,1)S(1)} %shard_map.40.refs_1_), channel_id=1, source_target_pairs={{0,2},{1,3},{2,0},{3,1},{4,6},{5,7},{6,4},{7,5},{8,10},{9,11},{10,... | collective-permute-start | bytes 1179656 | tf_op jit(solution)/shard_map/ppermute | solution.py:39
  86.7 1.3 %collective-permute-start.7 = (bf16[128,512]{1,0:T(8,128)(2,1)S(1)}, bf16[128,512]{1,0:T(8,128)(2,1)S(1)}, u32[]{:S(2)}, u32[]{:S(2)}) collective-permute-start(bf16[128,512]{1,0:T(8,128)(2,1)S(1)} %get-tuple-element.57.a0), channel_id=1, source_target_pairs={{0,1},{1,0},{2,3},{3,2},{4,5},{5,4},{6,7},{7,6},{8,9},{9,8},{10,11... | collective-permute-start | bytes 393224 | tf_op jit(solution)/shard_map/ppermute | solution.py:39
  86.7 10.2 %collective-permute-start.6 = (bf16[128,512]{1,0:T(8,128)(2,1)S(1)}, bf16[128,512]{1,0:T(8,128)(2,1)S(1)}, u32[]{:S(2)}, u32[]{:S(2)}) collective-permute-start(bf16[128,512]{1,0:T(8,128)(2,1)S(1)} %get-tuple-element.57.a0), channel_id=1, source_target_pairs={{0,2},{1,3},{2,0},{3,1},{4,6},{5,7},{6,4},{7,5},{8,10},{9,11},{10,... | collective-permute-start | bytes 393224 | tf_op jit(solution)/shard_map/ppermute | solution.py:39
  88.0 10.3 %collective-permute-start.15 = (bf16[128,1536]{1,0:T(8,128)(2,1)S(1)}, bf16[128,1536]{1,0:T(8,128)(2,1)S(1)}, u32[]{:S(2)}, u32[]{:S(2)}) collective-permute-start(bf16[128,1536]{1,0:T(8,128)(2,1)S(1)} %shard_map.40.refs_1_), channel_id=1, source_target_pairs={{0,1},{1,0},{2,3},{3,2},{4,5},{5,4},{6,7},{7,6},{8,9},{9,8},{10,11... | collective-permute-start | bytes 1179656 | tf_op jit(solution)/shard_map/ppermute | solution.py:39
  95.5 2.8 %collective-permute-start.16 = (bf16[128,1536]{1,0:T(8,128)(2,1)S(1)}, bf16[128,1536]{1,0:T(8,128)(2,1)S(1)}, u32[]{:S(2)}, u32[]{:S(2)}) collective-permute-start(bf16[128,1536]{1,0:T(8,128)(2,1)S(1)} %collective-permute-done.14.refs_2_), channel_id=1, source_target_pairs={{0,1},{1,0},{2,3},{3,2},{4,5},{5,4},{6,7},{7,6},{8,9},{9,8},{10,11... | collective-permute-start | bytes 1179656 | tf_op jit(solution)/shard_map/ppermute | solution.py:39
  96.9 1.3 %collective-permute-start.8 = (bf16[128,512]{1,0:T(8,128)(2,1)S(1)}, bf16[128,512]{1,0:T(8,128)(2,1)S(1)}, u32[]{:S(2)}, u32[]{:S(2)}) collective-permute-start(bf16[128,512]{1,0:T(8,128)(2,1)S(1)} %collective-permute-done.6.a1), channel_id=1, source_target_pairs={{0,1},{1,0},{2,3},{3,2},{4,5},{5,4},{6,7},{7,6},{8,9},{9,8},{10,11... | collective-permute-start | bytes 393224 | tf_op jit(solution)/shard_map/ppermute | solution.py:39
  (2 other events, 2.0 us)

commit v5 on v4

--- a/solution.py
+++ b/solution.py
@@ -235,7 +235,7 @@
 
 def last_kernel(weights, total, u, w, _, out, result, left):
     rows, columns = out.shape
-    last, tiles = u.shape[0], 4
+    last, tiles = u.shape[0], 8
     writes = []
     for k in range(tiles):
         here = slice(k * columns // tiles, (k + 1) * columns // tiles)
@@ -255,7 +255,7 @@
         in_specs=[VMEM] * 4 + [ANY],
         out_specs=ANY,
         out_shape=shape(rows, columns, BF16),
-        scratch_shapes=[pltpu.VMEM((rows, columns), BF16), pltpu.SemaphoreType.DMA((4,))],
+        scratch_shapes=[pltpu.VMEM((rows, columns), BF16), pltpu.SemaphoreType.DMA((8,))],
         compiler_params=pltpu.CompilerParams(vmem_limit_bytes=16 * MIB),
         cost_estimate=cost(4 * rows * last * columns, 6 * rows * columns + 4 * last * columns),
     )(weights, total, u, w, here)

time: 108 us -> 108 us (level)
  no operation moved by 1% of the time
where the time goes in v5:
time: 108 us
  waiting for transfers between devices  66.3 us (61%)
  starting transfers between devices  21.5 us (20%)
  Pallas kernels  13.2 us (12%)
  local copies, waits for them, and re-layouts  6.09 us (6%)
    ppermute x6, waiting for transfers between devices, moved(): return lax.ppermute(value, axis, pairs)  40.8 us
    ppermute x13, waiting for transfers between devices, swapped(): lax.ppermute(value, axis, [(i, i ^ distance) for i in range(devices)])  25.5 us
    ppermute x13, starting transfers between devices, swapped(): lax.ppermute(value, axis, [(i, i ^ distance) for i in range(devices)])  12.8 us
    ppermute x6, starting transfers between devices, moved(): return lax.ppermute(value, axis, pairs)  8.73 us
    pallas_call x1, Pallas kernels, apply_most(): pl.pallas_call(functools.partial(most_kernel, places, firsts), in_specs=[...  5.53 us
    unnamed x14, local copies, waits for them, and re-layouts  3.7 us
    pallas_call x1, Pallas kernels, gram(): pl.pallas_call(gram_kernel, in_specs=[VMEM] * 3, out_specs=[VMEM] * 2, ou...  2.69 us
    pallas_call x1, Pallas kernels, prepare(): pl.pallas_call(prepare_kernel, in_specs=[VMEM] * 3, out_specs=[VMEM] * 4...  2.39 us
  transfers between devices with their start and end apart: 19, of which 13 were waited for; matrix products, arithmetic and copies ran while one was open for 2% of the time, Pallas kernels for 10%

profile of v5, /device:TPU:0, one launch (start us, length us, event | category | flops | bytes accessed | tf_op | source)
XLA Modules:
  0.0 108.0 jit_solution(2412594002032368985)
XLA Ops:
  0.0 5.0 %collective-permute-start.3 = (bf16[512,2048]{1,0:T(8,128)(2,1)}, bf16[512,2048]{1,0:T(8,128)(2,1)S(1)}, u32[]{:S(2)}, u32[]{:S(2)}) collective-permute-start(bf16[512,2048]{1,0:T(8,128)(2,1)} %x.3), channel_id=1, source_target_pairs={{0,24},{4,12},{8,0},{12,20},{16,8},{20,28},{24,16},{28,4},{1,25},{... | collective-permute-start | bytes 6291464 | tf_op jit(solution)/shard_map/ppermute | solution.py:34
  5.1 1.7 %copy-done = bf16[512,2048]{1,0:T(8,128)(2,1)S(1)} copy-done((bf16[512,2048]{1,0:T(8,128)(2,1)S(1)}, bf16[512,2048]{1,0:T(8,128)(2,1)}, u32[]{:S(2)}) %copy-start) | copy-done | bytes 2097176
  7.8 2.4 %shard_map.37 = (bf16[240,2048]{1,0:T(8,128)(2,1)S(1)}, bf16[272,2048]{1,0:T(8,128)(2,1)}, bf16[512,128]{1,0:T(8,128)(2,1)S(1)}, bf16[512,128]{1,0:T(8,128)(2,1)S(1)}, s32[1,1]{1,0:T(1,128)}) custom-call(bf16[512,2048]{1,0:T(8,128)(2,1)S(1)} %copy-done, bf16[512,512]{1,0:T(8,128)(2,1)S(1)} %copy-done.2, bf16[512,512]{1,0:T(8,128)(2,1)} %far.1), custom_call_target="tpu_custom_call" | custom-call | bytes 6291456 | tf_op jit(solution)/shard_map/pallas_call | solution.py:68
  11.8 3.3 %collective-permute-start.4 = (bf16[512,128]{1,0:T(8,128)(2,1)S(1)}, bf16[512,128]{1,0:T(8,128)(2,1)S(1)}, u32[]{:S(2)}, u32[]{:S(2)}) collective-permute-start(bf16[512,128]{1,0:T(8,128)(2,1)S(1)} %get-tuple-element.55), channel_id=1, source_target_pairs={{0,4},{4,0},{8,12},{12,8},{16,20},{20,16},{24,28},{28,24},{1,5},{5... | collective-permute-start | bytes 393224 | tf_op jit(solution)/shard_map/ppermute | solution.py:39
  15.1 35.3 %collective-permute-done.3.z.refs_6_ = bf16[512,2048]{1,0:T(8,128)(2,1)S(1)} collective-permute-done((bf16[512,2048]{1,0:T(8,128)(2,1)}, bf16[512,2048]{1,0:T(8,128)(2,1)S(1)}, u32[]{:S(2)}, u32[]{:S(2)}) %collective-permute-start.3) | collective-permute-done | bytes 2097184 | tf_op jit(solution)/shard_map/ppermute | solution.py:34
  50.6 1.3 %slice.6 = bf16[256,2048]{1,0:T(8,128)(2,1)} slice(bf16[512,2048]{1,0:T(8,128)(2,1)S(1)} %collective-permute-done.3.z.refs_6_), slice={[256:512], [0:2048]} | slice | bytes 2097152 | tf_op jit(solution)/shard_map/slice | solution.py:326
  51.9 3.2 %collective-permute-done.4 = bf16[512,128]{1,0:T(8,128)(2,1)S(1)} collective-permute-done((bf16[512,128]{1,0:T(8,128)(2,1)S(1)}, bf16[512,128]{1,0:T(8,128)(2,1)S(1)}, u32[]{:S(2)}, u32[]{:S(2)}) %collective-permute-start.4) | collective-permute-done | bytes 131104 | tf_op jit(solution)/shard_map/ppermute | solution.py:39
  55.2 2.9 %collective-permute-start.12 = (bf16[256,2048]{1,0:T(8,128)(2,1)}, bf16[256,2048]{1,0:T(8,128)(2,1)}, u32[]{:S(2)}, u32[]{:S(2)}) collective-permute-start(bf16[256,2048]{1,0:T(8,128)(2,1)} %slice.6), channel_id=1, source_target_pairs={{0,4},{4,0},{8,12},{12,8},{16,20},{20,16},{24,28},{28,24},{1,5},{5... | collective-permute-start | bytes 3145736 | tf_op jit(solution)/shard_map/ppermute | solution.py:39
  58.8 2.7 %shard_map.38 = (f32[256,1024]{1,0:T(8,128)S(1)}, bf16[256,1024]{1,0:T(8,128)(2,1)S(1)}) custom-call(bf16[512,2048]{1,0:T(8,128)(2,1)S(1)} %copy-done.1, bf16[512,2048]{1,0:T(8,128)(2,1)S(1)} %collective-permute-done.2.y.refs_5_, bf16[512,2048]{1,0:T(8,128)(2,1)S(1)} %collective-permute-done.3.z.refs_6_), custom_call_target="tpu_custom_call" | custom-call | tf_op jit(solution)/shard_map/pallas_call | solution.py:102
  61.5 10.6 %conditional.1 = (bf16[128,1024]{1,0:T(8,128)(2,1)S(1)}, bf16[128,512]{1,0:T(8,128)(2,1)S(1)}, bf16[128,512]{1,0:T(8,128)(2,1)S(1)}, bf16[256,2048]{1,0:T(8,128)(2,1)}) conditional(s32[]{:T(128)} %bitcast, () %tuple.19, (bf16[256,1024]{1,0:T(8,128)(2,1)S(1)}, f32[256,1024]{1,0:T(8,128)S(1)}, bf16[512,512]{1,0:T(8,128)(2,1)S(1)}, ...), branch_computations={%region_0.0_spmd, %region_1.0_spmd} | conditional | flops 917504 | bytes 10223728 | solution.py:340
  61.6 1.9 %collective-permute-done.other = bf16[256,1024]{1,0:T(8,128)(2,1)S(1)} collective-permute-done((bf16[256,1024]{1,0:T(8,128)(2,1)S(1)}, bf16[256,1024]{1,0:T(8,128)(2,1)S(1)}, u32[]{:S(2)}, u32[]{:S(2)}) %collective-permute-start) | collective-permute-done | bytes 524320 | tf_op jit(solution)/shard_map/cond/branch_1_fun/ppermute | solution.py:39
  63.6 1.6 %collective-permute-start.1 = (bf16[128,1024]{1,0:T(8,128)(2,1)S(1)}, bf16[128,1024]{1,0:T(8,128)(2,1)S(1)}, u32[]{:S(2)}, u32[]{:S(2)}) collective-permute-start(bf16[128,1024]{1,0:T(8,128)(2,1)S(1)} %get-tuple-element.20), channel_id=1, source_target_pairs={{0,2},{1,3},{2,0},{3,1},{4,6},{5,7},{6,4},{7,5},{8,10},{9,11},{10,... | collective-permute-start | bytes 786440 | tf_op jit(solution)/shard_map/cond/branch_1_fun/ppermute | solution.py:39
  66.2 5.8 %collective-permute-done.1.other = bf16[128,1024]{1,0:T(8,128)(2,1)S(1)} collective-permute-done((bf16[128,1024]{1,0:T(8,128)(2,1)S(1)}, bf16[128,1024]{1,0:T(8,128)(2,1)S(1)}, u32[]{:S(2)}, u32[]{:S(2)}) %collective-permute-start.1) | collective-permute-done | bytes 262176 | tf_op jit(solution)/shard_map/cond/branch_1_fun/ppermute | solution.py:39
  72.1 2.2 %collective-permute-start.9 = (bf16[128,1024]{1,0:T(8,128)(2,1)S(1)}, bf16[128,1024]{1,0:T(8,128)(2,1)S(1)}, u32[]{:S(2)}, u32[]{:S(2)}) collective-permute-start(bf16[128,1024]{1,0:T(8,128)(2,1)S(1)} %get-tuple-element.58), channel_id=1, source_target_pairs={{0,8},{8,16},{16,24},{24,0},{1,9},{9,17},{17,25},{25,1},{2,10},{10... | collective-permute-start | bytes 786440 | tf_op jit(solution)/shard_map/ppermute | solution.py:34
  75.1 3.7 %collective-permute-done.13.refs_8_ = bf16[272,2048]{1,0:T(8,128)(2,1)S(1)} collective-permute-done((bf16[272,2048]{1,0:T(8,128)(2,1)}, bf16[272,2048]{1,0:T(8,128)(2,1)S(1)}, u32[]{:S(2)}, u32[]{:S(2)}) %collective-permute-start.13) | collective-permute-done | bytes 1114144 | tf_op jit(solution)/shard_map/ppermute | solution.py:34
  78.8 3.0 %collective-permute-done.12.refs_7_ = bf16[256,2048]{1,0:T(8,128)(2,1)} collective-permute-done((bf16[256,2048]{1,0:T(8,128)(2,1)}, bf16[256,2048]{1,0:T(8,128)(2,1)}, u32[]{:S(2)}, u32[]{:S(2)}) %collective-permute-start.12) | collective-permute-done | bytes 1048608 | tf_op jit(solution)/shard_map/ppermute | solution.py:39
  81.8 2.6 %collective-permute-start.17 = (bf16[256,2048]{1,0:T(8,128)(2,1)}, bf16[256,2048]{1,0:T(8,128)(2,1)S(1)}, u32[]{:S(2)}, u32[]{:S(2)}) collective-permute-start(bf16[256,2048]{1,0:T(8,128)(2,1)} %get-tuple-element.73), channel_id=1, source_target_pairs={{0,4},{4,0},{8,12},{12,8},{16,20},{20,16},{24,28},{28,24},{1,5},{5... | collective-permute-start | bytes 3145736 | tf_op jit(solution)/shard_map/ppermute | solution.py:39
  85.1 1.6 %collective-permute-start.14 = (bf16[128,1536]{1,0:T(8,128)(2,1)S(1)}, bf16[128,1536]{1,0:T(8,128)(2,1)S(1)}, u32[]{:S(2)}, u32[]{:S(2)}) collective-permute-start(bf16[128,1536]{1,0:T(8,128)(2,1)S(1)} %shard_map.40.refs_1_), channel_id=1, source_target_pairs={{0,2},{1,3},{2,0},{3,1},{4,6},{5,7},{6,4},{7,5},{8,10},{9,11},{10,... | collective-permute-start | bytes 1179656 | tf_op jit(solution)/shard_map/ppermute | solution.py:39
  88.2 7.3 %collective-permute-done.14.refs_2_ = bf16[128,1536]{1,0:T(8,128)(2,1)S(1)} collective-permute-done((bf16[128,1536]{1,0:T(8,128)(2,1)S(1)}, bf16[128,1536]{1,0:T(8,128)(2,1)S(1)}, u32[]{:S(2)}, u32[]{:S(2)}) %collective-permute-start.14) | collective-permute-done | bytes 393248 | tf_op jit(solution)/shard_map/ppermute | solution.py:39
  95.5 1.4 %collective-permute-done.6.a1 = bf16[128,512]{1,0:T(8,128)(2,1)S(1)} collective-permute-done((bf16[128,512]{1,0:T(8,128)(2,1)S(1)}, bf16[128,512]{1,0:T(8,128)(2,1)S(1)}, u32[]{:S(2)}, u32[]{:S(2)}) %collective-permute-start.6) | collective-permute-done | bytes 131104 | tf_op jit(solution)/shard_map/ppermute | solution.py:39
  96.9 1.3 %collective-permute-done.8.a3 = bf16[128,512]{1,0:T(8,128)(2,1)S(1)} collective-permute-done((bf16[128,512]{1,0:T(8,128)(2,1)S(1)}, bf16[128,512]{1,0:T(8,128)(2,1)S(1)}, u32[]{:S(2)}, u32[]{:S(2)}) %collective-permute-start.8) | collective-permute-done | bytes 131104 | tf_op jit(solution)/shard_map/ppermute | solution.py:39
  98.3 5.5 %shard_map.41 = (f32[512,2048]{1,0:T(8,128)S(1)}, bf16[512,496]{1,0:T(8,128)(2,1)S(1)}) custom-call(bf16[512,512]{1,0:T(8,128)(2,1)S(1)} %shard_map.39.refs_0_, bf16[128,1536]{1,0:T(8,128)(2,1)S(1)} %shard_map.40.refs_1_, bf16[128,1536]{1,0:T(8,128)(2,1)S(1)} %collective-permute-done.14.refs_2_, bf16[128,1536]{1,0:T(8,128)(2,1)S(1)} %collective-permute-done.15.refs_3_, ...), custom_call_target="tpu_custom_call" | custom-call | flops 1000000000 | tf_op jit(solution)/shard_map/pallas_call | solution.py:221
  103.9 1.2 %collective-permute-done.18.value.w = bf16[240,2048]{1,0:T(8,128)(2,1)S(1)} collective-permute-done((bf16[240,2048]{1,0:T(8,128)(2,1)}, bf16[240,2048]{1,0:T(8,128)(2,1)S(1)}, u32[]{:S(2)}, u32[]{:S(2)}) %collective-permute-start.18) | collective-permute-done | bytes 983072 | tf_op jit(solution)/shard_map/ppermute | solution.py:34
  105.7 2.3 %shard_map.43 = bf16[512,2048]{1,0:T(8,128)(2,1)} custom-call(bf16[512,496]{1,0:T(8,128)(2,1)S(1)} %get-tuple-element.68.weights, f32[512,2048]{1,0:T(8,128)S(1)} %get-tuple-element.69.total, bf16[256,2048]{1,0:T(8,128)(2,1)S(1)} %collective-permute-done.17.u, bf16[240,2048]{1,0:T(8,128)(2,1)S(1)} %collective-permute-done.18.value.w, f32[8,128]{1,0:T(8,128)S(1)} %shard_map.42._), custom_call_target="tpu_custom_call" | custom-call | flops 1040187392 | bytes 8323072 | tf_op jit(solution)/shard_map/pallas_call | solution.py:253
  (40 shorter events, 7.9 us)
Async XLA Ops:
  0.0 50.4 %collective-permute-start.3 = (bf16[512,2048]{1,0:T(8,128)(2,1)}, bf16[512,2048]{1,0:T(8,128)(2,1)S(1)}, u32[]{:S(2)}, u32[]{:S(2)}) collective-permute-start(bf16[512,2048]{1,0:T(8,128)(2,1)} %x.3), channel_id=1, source_target_pairs={{0,24},{4,12},{8,0},{12,20},{16,8},{20,28},{24,16},{28,4},{1,25},{... | collective-permute-start | bytes 6291464 | tf_op jit(solution)/shard_map/ppermute | solution.py:34
  5.0 50.1 %collective-permute-start.2 = (bf16[512,2048]{1,0:T(8,128)(2,1)}, bf16[512,2048]{1,0:T(8,128)(2,1)S(1)}, u32[]{:S(2)}, u32[]{:S(2)}) collective-permute-start(bf16[512,2048]{1,0:T(8,128)(2,1)} %x.3), channel_id=1, source_target_pairs={{0,4},{4,0},{8,12},{12,8},{16,20},{20,16},{24,28},{28,24},{1,5},{5... | collective-permute-start | bytes 6291464 | tf_op jit(solution)/shard_map/ppermute | solution.py:39
  5.1 1.7 %copy-start = (bf16[512,2048]{1,0:T(8,128)(2,1)S(1)}, bf16[512,2048]{1,0:T(8,128)(2,1)}, u32[]{:S(2)}) copy-start(bf16[512,2048]{1,0:T(8,128)(2,1)} %x.3) | copy-start | bytes 6291460
  7.8 51.0 %copy-start.1 = (bf16[512,2048]{1,0:T(8,128)(2,1)S(1)}, bf16[512,2048]{1,0:T(8,128)(2,1)}, u32[]{:S(2)}) copy-start(bf16[512,2048]{1,0:T(8,128)(2,1)} %x.3) | copy-start | bytes 6291460
  11.1 4.0 %collective-permute-start.5 = (bf16[512,128]{1,0:T(8,128)(2,1)S(1)}, bf16[512,128]{1,0:T(8,128)(2,1)S(1)}, u32[]{:S(2)}, u32[]{:S(2)}) collective-permute-start(bf16[512,128]{1,0:T(8,128)(2,1)S(1)} %get-tuple-element.56), channel_id=1, source_target_pairs={{4,12},{12,20},{20,28},{28,4},{5,13},{13,21},{21,29},{29,5},{6,14}... | collective-permute-start | bytes 393224 | tf_op jit(solution)/shard_map/ppermute | solution.py:34
  11.8 43.3 %collective-permute-start.4 = (bf16[512,128]{1,0:T(8,128)(2,1)S(1)}, bf16[512,128]{1,0:T(8,128)(2,1)S(1)}, u32[]{:S(2)}, u32[]{:S(2)}) collective-permute-start(bf16[512,128]{1,0:T(8,128)(2,1)S(1)} %get-tuple-element.55), channel_id=1, source_target_pairs={{0,4},{4,0},{8,12},{12,8},{16,20},{20,16},{24,28},{28,24},{1,5},{5... | collective-permute-start | bytes 393224 | tf_op jit(solution)/shard_map/ppermute | solution.py:39
  50.4 11.0 %copy-start.4 = (bf16[512,2048]{1,0:T(8,128)(2,1)}, bf16[512,2048]{1,0:T(8,128)(2,1)S(1)}, u32[]{:S(2)}) copy-start(bf16[512,2048]{1,0:T(8,128)(2,1)S(1)} %collective-permute-done.3.z.refs_6_) | copy-start | bytes 6291460
  50.4 28.3 %collective-permute-start.13 = (bf16[272,2048]{1,0:T(8,128)(2,1)}, bf16[272,2048]{1,0:T(8,128)(2,1)S(1)}, u32[]{:S(2)}, u32[]{:S(2)}) collective-permute-start(bf16[272,2048]{1,0:T(8,128)(2,1)} %get-tuple-element.63), channel_id=1, source_target_pairs={{0,8},{4,28},{8,16},{12,4},{16,24},{20,12},{24,0},{28,20},{1,9},{5... | collective-permute-start | bytes 3342344 | tf_op jit(solution)/shard_map/ppermute | solution.py:34
  55.2 26.6 %collective-permute-start.12 = (bf16[256,2048]{1,0:T(8,128)(2,1)}, bf16[256,2048]{1,0:T(8,128)(2,1)}, u32[]{:S(2)}, u32[]{:S(2)}) collective-permute-start(bf16[256,2048]{1,0:T(8,128)(2,1)} %slice.6), channel_id=1, source_target_pairs={{0,4},{4,0},{8,12},{12,8},{16,20},{20,16},{24,28},{28,24},{1,5},{5... | collective-permute-start | bytes 3145736 | tf_op jit(solution)/shard_map/ppermute | solution.py:39
  58.7 2.7 %copy-start.6 = (bf16[512,512]{1,0:T(8,128)(2,1)S(1)}, bf16[512,512]{1,0:T(8,128)(2,1)}, u32[]{:S(2)}) copy-start(bf16[512,512]{1,0:T(8,128)(2,1)} %far.1) | copy-start | bytes 1572868
  61.5 2.0 %collective-permute-start = (bf16[256,1024]{1,0:T(8,128)(2,1)S(1)}, bf16[256,1024]{1,0:T(8,128)(2,1)S(1)}, u32[]{:S(2)}, u32[]{:S(2)}) collective-permute-start(bf16[256,1024]{1,0:T(8,128)(2,1)S(1)} %get-tuple-element.18), channel_id=1, source_target_pairs={{0,1},{1,0},{2,3},{3,2},{4,5},{5,4},{6,7},{7,6},{8,9},{9,8},{10,11... | collective-permute-start | bytes 1572872 | tf_op jit(solution)/shard_map/cond/branch_1_fun/ppermute | solution.py:39
  63.6 8.4 %collective-permute-start.1 = (bf16[128,1024]{1,0:T(8,128)(2,1)S(1)}, bf16[128,1024]{1,0:T(8,128)(2,1)S(1)}, u32[]{:S(2)}, u32[]{:S(2)}) collective-permute-start(bf16[128,1024]{1,0:T(8,128)(2,1)S(1)} %get-tuple-element.20), channel_id=1, source_target_pairs={{0,2},{1,3},{2,0},{3,1},{4,6},{5,7},{6,4},{7,5},{8,10},{9,11},{10,... | collective-permute-start | bytes 786440 | tf_op jit(solution)/shard_map/cond/branch_1_fun/ppermute | solution.py:39
  72.1 12.9 %collective-permute-start.9 = (bf16[128,1024]{1,0:T(8,128)(2,1)S(1)}, bf16[128,1024]{1,0:T(8,128)(2,1)S(1)}, u32[]{:S(2)}, u32[]{:S(2)}) collective-permute-start(bf16[128,1024]{1,0:T(8,128)(2,1)S(1)} %get-tuple-element.58), channel_id=1, source_target_pairs={{0,8},{8,16},{16,24},{24,0},{1,9},{9,17},{17,25},{25,1},{2,10},{10... | collective-permute-start | bytes 786440 | tf_op jit(solution)/shard_map/ppermute | solution.py:34
  74.3 10.1 %collective-permute-start.11 = (bf16[128,512]{1,0:T(8,128)(2,1)S(1)}, bf16[128,512]{1,0:T(8,128)(2,1)S(1)}, u32[]{:S(2)}, u32[]{:S(2)}) collective-permute-start(bf16[128,512]{1,0:T(8,128)(2,1)S(1)} %get-tuple-element.67.own), channel_id=1, source_target_pairs={{0,4},{4,0},{8,12},{12,8},{16,20},{20,16},{24,28},{28,24},{1,5},{5... | collective-permute-start | bytes 393224 | tf_op jit(solution)/shard_map/ppermute | solution.py:39
  74.4 10.0 %collective-permute-start.10 = (bf16[128,512]{1,0:T(8,128)(2,1)S(1)}, bf16[128,512]{1,0:T(8,128)(2,1)S(1)}, u32[]{:S(2)}, u32[]{:S(2)}) collective-permute-start(bf16[128,512]{1,0:T(8,128)(2,1)S(1)} %get-tuple-element.57.a0), channel_id=1, source_target_pairs={{4,28},{12,4},{20,12},{28,20},{5,29},{13,5},{21,13},{29,21},{6,30}... | collective-permute-start | bytes 393224 | tf_op jit(solution)/shard_map/ppermute | solution.py:34
  78.8 26.2 %collective-permute-start.18 = (bf16[240,2048]{1,0:T(8,128)(2,1)}, bf16[240,2048]{1,0:T(8,128)(2,1)S(1)}, u32[]{:S(2)}, u32[]{:S(2)}) collective-permute-start(bf16[240,2048]{1,0:T(8,128)(2,1)} %copy-done.3), channel_id=1, source_target_pairs={{0,8},{4,28},{8,16},{12,4},{16,24},{20,12},{24,0},{28,20},{1,9},{5... | collective-permute-start | bytes 2949128 | tf_op jit(solution)/shard_map/ppermute | solution.py:34
  81.8 23.9 %collective-permute-start.17 = (bf16[256,2048]{1,0:T(8,128)(2,1)}, bf16[256,2048]{1,0:T(8,128)(2,1)S(1)}, u32[]{:S(2)}, u32[]{:S(2)}) collective-permute-start(bf16[256,2048]{1,0:T(8,128)(2,1)} %get-tuple-element.73), channel_id=1, source_target_pairs={{0,4},{4,0},{8,12},{12,8},{16,20},{20,16},{24,28},{28,24},{1,5},{5... | collective-permute-start | bytes 3145736 | tf_op jit(solution)/shard_map/ppermute | solution.py:39
  85.1 13.2 %copy-start.5 = (bf16[512,2048]{1,0:T(8,128)(2,1)S(1)}, bf16[512,2048]{1,0:T(8,128)(2,1)}, u32[]{:S(2)}) copy-start(bf16[512,2048]{1,0:T(8,128)(2,1)} %copy-done.4) | copy-start | bytes 6291460
  85.1 10.4 %collective-permute-start.14 = (bf16[128,1536]{1,0:T(8,128)(2,1)S(1)}, bf16[128,1536]{1,0:T(8,128)(2,1)S(1)}, u32[]{:S(2)}, u32[]{:S(2)}) collective-permute-start(bf16[128,1536]{1,0:T(8,128)(2,1)S(1)} %shard_map.40.refs_1_), channel_id=1, source_target_pairs={{0,2},{1,3},{2,0},{3,1},{4,6},{5,7},{6,4},{7,5},{8,10},{9,11},{10,... | collective-permute-start | bytes 1179656 | tf_op jit(solution)/shard_map/ppermute | solution.py:39
  86.7 1.3 %collective-permute-start.7 = (bf16[128,512]{1,0:T(8,128)(2,1)S(1)}, bf16[128,512]{1,0:T(8,128)(2,1)S(1)}, u32[]{:S(2)}, u32[]{:S(2)}) collective-permute-start(bf16[128,512]{1,0:T(8,128)(2,1)S(1)} %get-tuple-element.57.a0), channel_id=1, source_target_pairs={{0,1},{1,0},{2,3},{3,2},{4,5},{5,4},{6,7},{7,6},{8,9},{9,8},{10,11... | collective-permute-start | bytes 393224 | tf_op jit(solution)/shard_map/ppermute | solution.py:39
  86.7 10.2 %collective-permute-start.6 = (bf16[128,512]{1,0:T(8,128)(2,1)S(1)}, bf16[128,512]{1,0:T(8,128)(2,1)S(1)}, u32[]{:S(2)}, u32[]{:S(2)}) collective-permute-start(bf16[128,512]{1,0:T(8,128)(2,1)S(1)} %get-tuple-element.57.a0), channel_id=1, source_target_pairs={{0,2},{1,3},{2,0},{3,1},{4,6},{5,7},{6,4},{7,5},{8,10},{9,11},{10,... | collective-permute-start | bytes 393224 | tf_op jit(solution)/shard_map/ppermute | solution.py:39
  88.0 10.3 %collective-permute-start.15 = (bf16[128,1536]{1,0:T(8,128)(2,1)S(1)}, bf16[128,1536]{1,0:T(8,128)(2,1)S(1)}, u32[]{:S(2)}, u32[]{:S(2)}) collective-permute-start(bf16[128,1536]{1,0:T(8,128)(2,1)S(1)} %shard_map.40.refs_1_), channel_id=1, source_target_pairs={{0,1},{1,0},{2,3},{3,2},{4,5},{5,4},{6,7},{7,6},{8,9},{9,8},{10,11... | collective-permute-start | bytes 1179656 | tf_op jit(solution)/shard_map/ppermute | solution.py:39
  95.5 2.8 %collective-permute-start.16 = (bf16[128,1536]{1,0:T(8,128)(2,1)S(1)}, bf16[128,1536]{1,0:T(8,128)(2,1)S(1)}, u32[]{:S(2)}, u32[]{:S(2)}) collective-permute-start(bf16[128,1536]{1,0:T(8,128)(2,1)S(1)} %collective-permute-done.14.refs_2_), channel_id=1, source_target_pairs={{0,1},{1,0},{2,3},{3,2},{4,5},{5,4},{6,7},{7,6},{8,9},{9,8},{10,11... | collective-permute-start | bytes 1179656 | tf_op jit(solution)/shard_map/ppermute | solution.py:39
  96.9 1.3 %collective-permute-start.8 = (bf16[128,512]{1,0:T(8,128)(2,1)S(1)}, bf16[128,512]{1,0:T(8,128)(2,1)S(1)}, u32[]{:S(2)}, u32[]{:S(2)}) collective-permute-start(bf16[128,512]{1,0:T(8,128)(2,1)S(1)} %collective-permute-done.6.a1), channel_id=1, source_target_pairs={{0,1},{1,0},{2,3},{3,2},{4,5},{5,4},{6,7},{7,6},{8,9},{9,8},{10,11... | collective-permute-start | bytes 393224 | tf_op jit(solution)/shard_map/ppermute | solution.py:39
  (2 other events, 2.0 us)

commit v6 on v5

--- a/solution.py
+++ b/solution.py
@@ -8,7 +8,7 @@
 from jax.sharding import PartitionSpec as P
 
 MIB = 1024 * 1024
-SEEN_COST, MOST_COST, SETTLE_COST = 10, 10, 25
+SEEN_COST, MOST_COST, SETTLE_COST = 45, 0, 10
 F32, BF16 = jnp.float32, jnp.bfloat16
 VMEM = pl.BlockSpec(memory_space=pltpu.VMEM)
 ANY = pl.BlockSpec(memory_space=pl.ANY)
@@ -53,11 +53,13 @@
     return pl.ds(pl.multiple_of(quarter_index(distance) * size, size), size)
 
 
-def prepare_kernel(x, near, far, upper, lower, near_out, far_out, flag):
+def prepare_kernel(x, near, far, left, right, lower, near_out, far_out, flag):
     rows = near.shape[0]
     here = quarter_rows(rows)
-    upper[...] = x[: upper.shape[0], :]
-    lower[...] = x[upper.shape[0] :, :]
+    first, half = left.shape
+    left[...] = x[:first, :half]
+    right[...] = x[:first, half:]
+    lower[...] = x[first:, :]
     near_out[...] = near[:, here]
     far_out[...] = far[:, here]
     flag[0, 0] = (jnp.max(near[:8, :128].astype(F32)) < 1e30).astype(jnp.int32)
@@ -68,8 +70,9 @@
     return pl.pallas_call(
         prepare_kernel,
         in_specs=[VMEM] * 3,
-        out_specs=[VMEM] * 4 + [pl.BlockSpec(memory_space=pltpu.SMEM)],
-        out_shape=[shape(first, columns, BF16), shape(rows - first, columns, BF16)]
+        out_specs=[VMEM] * 5 + [pl.BlockSpec(memory_space=pltpu.SMEM)],
+        out_shape=[shape(first, columns // 2, BF16)] * 2
+        + [shape(rows - first, columns, BF16)]
         + [shape(rows, rows // 4, BF16)] * 2
         + [shape(1, 1, jnp.int32)],
         compiler_params=pltpu.CompilerParams(vmem_limit_bytes=12 * MIB),
@@ -233,47 +236,55 @@
     )(ahead, *back, *values)
 
 
-def last_kernel(weights, total, u, w, _, out, result, left):
-    rows, columns = out.shape
-    last, tiles = u.shape[0], 8
+def last_kernel(side, weights, total, u, w, *rest):
+    out, result, left = rest[-3:]
+    last, width = u.shape
+    tiles = 4
     writes = []
     for k in range(tiles):
-        here = slice(k * columns // tiles, (k + 1) * columns // tiles)
+        here = slice(k * width // tiles, (k + 1) * width // tiles)
+        there = slice(side * width + here.start, side * width + here.stop)
         added = inner(weights[:, :last], u[:, here]) + inner(weights[:, last:], w[:, here])
-        result[:, here] = (total[:, here] + added).astype(BF16)
-        writes.append(pltpu.make_async_copy(result.at[:, here], out.at[:, here], left.at[k]))
+        result[:, here] = (total[:, there] + added).astype(BF16)
+        writes.append(pltpu.make_async_copy(result.at[:, here], out.at[:, there], left.at[k]))
         writes[-1].start()
     for write in writes:
         write.wait()
 
 
-def apply_last(weights, total, u, w, here):
+def apply_last(weights, total, u, w, *rest):
+    *before, side = rest
+    return apply_side(weights, total, u, w, before, side)
+
+
+def apply_side(weights, total, u, w, before, side):
     rows, columns = total.shape
-    last = (u.shape[0] + w.shape[0]) // 2
-    return pl.pallas_call(
-        last_kernel,
-        in_specs=[VMEM] * 4 + [ANY],
+    last, width = u.shape
+    return pl.pallas_call(
+        functools.partial(last_kernel, side),
+        in_specs=[VMEM] * 4 + [ANY] * len(before),
         out_specs=ANY,
         out_shape=shape(rows, columns, BF16),
-        scratch_shapes=[pltpu.VMEM((rows, columns), BF16), pltpu.SemaphoreType.DMA((8,))],
+        scratch_shapes=[pltpu.VMEM((rows, width), BF16), pltpu.SemaphoreType.DMA((4,))],
+        input_output_aliases={4: 0} if side else {},
         compiler_params=pltpu.CompilerParams(vmem_limit_bytes=16 * MIB),
-        cost_estimate=cost(4 * rows * last * columns, 6 * rows * columns + 4 * last * columns),
-    )(weights, total, u, w, here)
-
-
-def seen_kernel(value, out):
+        cost_estimate=cost(4 * rows * last * width, 6 * rows * width + 4 * last * width),
+    )(weights, total, u, w, *before)
+
+
+def seen_kernel(one, other, out):
     out[...] = jnp.ones_like(out)
 
 
-def seen(value):
+def seen(one, other):
     return pl.pallas_call(
         seen_kernel,
-        in_specs=[ANY],
+        in_specs=[ANY] * 2,
         out_specs=VMEM,
         out_shape=shape(8, 128, F32),
         compiler_params=pltpu.CompilerParams(vmem_limit_bytes=MIB),
         cost_estimate=cost(SEEN_COST * 10**8, 0),
-    )(value)
+    )(one, other)
 
 
 def merge_kernel(even_back, odd_back, by_y, own, out):
@@ -317,7 +328,7 @@
 
     z, y = moved(x, "blk", inward), swapped(x, "blk", 1)
     size, first = rows // 2, rows // 2 - 16
-    x_half, x_more, near_part, far_part, flag = prepare(x, near, far, first)
+    x_left, x_right, x_more, near_part, far_part, flag = prepare(x, near, far, first)
     near_part = swapped(near_part, "blk", 1)
     far_part = moved(far_part, "blk", [p for p in inward if p[0] % 2])
 
@@ -330,31 +341,40 @@
     def summed(keep, send, far, near_part, far_part, z):
         mine, send = fold(keep, swapped(send, "orb", 1))
         by_x = swapped(send, "orb", 2)
-        return *weigh(mine, by_x, far, near_part, far_part), z[:size]
+        return *weigh(mine, by_x, far, near_part, far_part), z[:size, : columns // 2], z[:size, columns // 2 :]
 
     def no_sum(*_):
         parts = tuple(jnp.zeros((rows // 4, n * rows), BF16) for n in (2, 1, 1))
-        return *parts, jnp.zeros((size, columns), BF16)
+        half = jnp.zeros((size, columns // 2), BF16)
+        return *parts, half, half
 
     keep, send = gram(x, y, z)
-    pair, xz, own, z_half = lax.cond(always, summed, no_sum, keep, send, far, near_part, far_part, z)
+    pair, xz, own, z_left, z_right = lax.cond(
+        always, summed, no_sum, keep, send, far, near_part, far_part, z
+    )
     even_back = moved(pair, "blk", [p for p in outward if p[0] % 2 == 0])
     odd_back = moved(xz, "blk", [p for p in outward if p[0] % 2])
     by_y = swapped(own, "blk", 1)
-    zk, xk = after((z_half, x_half), xz, w_more)
-    w_half = moved(xk, "blk", outward)
-    (zk,) = after((zk,), u_more)
-    u_half = swapped(zk, "blk", 1)
+    xl, xr = after((x_left, x_right), xz, w_more)
+    zl, zr = after((z_left, z_right), u_more, w_more)
+    w_half = moved(xl, "blk", outward), moved(xr, "blk", outward)
+    u_half = swapped(zl, "blk", 1), swapped(zr, "blk", 1)
     ahead = settle(gather(xz))
     back = after((even_back, odd_back, by_y, own), u_more, w_more)
-    back = gather(merge(*back))
+    back = merge(*back)
+    by_x = swapped(back, "orb", 2)
+    (far_x,) = after((by_x,), w_half[0], u_half[0])
+    back = back, by_x, swapped(back, "orb", 1), swapped(far_x, "orb", 1)
 
     places, place = [], 0
     for height in (rows, rows, rows - size, rows - first):
         places.append((place, place + height))
         place += height
     total, weights = apply_most(places, (size, first), ahead, back, (y, z, u_more, w_more))
-    return apply_last(weights, total, u_half, w_half, seen(*after((w_half,), total)))
+    here = jnp.zeros((8, 128), F32)
+    out = apply_last(weights, total, u_half[0], w_half[0], here, 0)
+    here = seen(*after((w_half[1], u_half[1]), out))
+    return apply_last(weights, total, u_half[1], w_half[1], out, here, 1)
 
 
 def from_behind(value, by):

time: 108 us -> 110 us (1.019)
  starting transfers between devices: 21.5 us -> 24 us
  waiting for transfers between devices: 66.3 us -> 64 us
    ppermute x6 -> x7, waiting for transfers between devices: 40.8 us -> 34.7 us  [moved(): return lax.ppermute(value, axis, pairs)]
    ppermute x13 -> x14, waiting for transfers between devices: 25.5 us -> 29.2 us  [swapped(): lax.ppermute(value, axis, [(i, i ^ distance) for i in range(devices)])]
    ppermute x13 -> x14, starting transfers between devices: 12.8 us -> 15 us  [swapped(): lax.ppermute(value, axis, [(i, i ^ distance) for i in range(devices)])]
    pallas_call x3 -> x4, Pallas kernels: 4.67 us -> 5.55 us  [the longest x2 3.18 us: apply_side(): pl.pallas_call(functools.partial(last_kernel, side), in_specs=[VMEM] * 4...]
    unnamed x14 -> x16, local copies, waits for them, and re-layouts: 3.7 us -> 4.3 us
    ppermute x6 -> x7, starting transfers between devices: 8.73 us -> 9.01 us  [moved(): return lax.ppermute(value, axis, pairs)]
  transfers between devices with their start and end apart: 19 -> 21, of which waited for: 13 -> 10; matrix products, arithmetic and copies ran while one was open for 2% -> 2% of each run, Pallas kernels for 10% -> 11%
where the time goes in v6:
time: 110 us; the launch traced here: 109 us
  waiting for transfers between devices  64 us (58%)
  starting transfers between devices  24 us (22%)
  Pallas kernels  14.1 us (13%)
  local copies, waits for them, and re-layouts  6.44 us (6%)
    ppermute x7, waiting for transfers between devices, moved(): return lax.ppermute(value, axis, pairs)  34.7 us
    ppermute x14, waiting for transfers between devices, swapped(): lax.ppermute(value, axis, [(i, i ^ distance) for i in range(devices)])  29.2 us
    ppermute x14, starting transfers between devices, swapped(): lax.ppermute(value, axis, [(i, i ^ distance) for i in range(devices)])  15 us
    ppermute x7, starting transfers between devices, moved(): return lax.ppermute(value, axis, pairs)  9.01 us
    pallas_call x1, Pallas kernels, apply_most(): pl.pallas_call(functools.partial(most_kernel, places, firsts), in_specs=[...  5.53 us
    unnamed x16, local copies, waits for them, and re-layouts  4.3 us
    pallas_call x2, Pallas kernels, apply_side(): pl.pallas_call(functools.partial(last_kernel, side), in_specs=[VMEM] * 4...  3.18 us
    pallas_call x1, Pallas kernels, gram(): pl.pallas_call(gram_kernel, in_specs=[VMEM] * 3, out_specs=[VMEM] * 2, ou...  2.69 us
  transfers between devices with their start and end apart: 21, of which 10 were waited for; matrix products, arithmetic and copies ran while one was open for 2% of the time, Pallas kernels for 11%

profile of v6, /device:TPU:0, one launch (start us, length us, event | category | flops | bytes accessed | tf_op | source)
XLA Modules:
  0.0 109.4 jit_solution(11670530417076628868)
XLA Ops:
  0.0 5.0 %collective-permute-start.3 = (bf16[512,2048]{1,0:T(8,128)(2,1)}, bf16[512,2048]{1,0:T(8,128)(2,1)S(1)}, u32[]{:S(2)}, u32[]{:S(2)}) collective-permute-start(bf16[512,2048]{1,0:T(8,128)(2,1)} %x.3), channel_id=1, source_target_pairs={{0,24},{4,12},{8,0},{12,20},{16,8},{20,28},{24,16},{28,4},{1,25},{... | collective-permute-start | bytes 6291464 | tf_op jit(solution)/shard_map/ppermute | solution.py:34
  5.1 1.7 %copy-done = bf16[512,2048]{1,0:T(8,128)(2,1)S(1)} copy-done((bf16[512,2048]{1,0:T(8,128)(2,1)S(1)}, bf16[512,2048]{1,0:T(8,128)(2,1)}, u32[]{:S(2)}) %copy-start) | copy-done | bytes 2097176
  7.8 2.4 %shard_map.37 = (bf16[240,1024]{1,0:T(8,128)(2,1)S(1)}, bf16[240,1024]{1,0:T(8,128)(2,1)S(1)}, bf16[272,2048]{1,0:T(8,128)(2,1)}, bf16[512,128]{1,0:T(8,128)(2,1...) custom-call(bf16[512,2048]{1,0:T(8,128)(2,1)S(1)} %copy-done, bf16[512,512]{1,0:T(8,128)(2,1)S(1)} %copy-done.2, ...), custom_call_target="tpu_custom_call" | custom-call | bytes 6291456 | tf_op jit(solution)/shard_map/pallas_call | solution.py:70
  12.4 3.3 %collective-permute-start.4 = (bf16[512,128]{1,0:T(8,128)(2,1)S(1)}, bf16[512,128]{1,0:T(8,128)(2,1)S(1)}, u32[]{:S(2)}, u32[]{:S(2)}) collective-permute-start(bf16[512,128]{1,0:T(8,128)(2,1)S(1)} %get-tuple-element.60), channel_id=1, source_target_pairs={{0,4},{4,0},{8,12},{12,8},{16,20},{20,16},{24,28},{28,24},{1,5},{5... | collective-permute-start | bytes 393224 | tf_op jit(solution)/shard_map/ppermute | solution.py:39
  15.7 34.7 %collective-permute-done.3.z.refs_6_ = bf16[512,2048]{1,0:T(8,128)(2,1)S(1)} collective-permute-done((bf16[512,2048]{1,0:T(8,128)(2,1)}, bf16[512,2048]{1,0:T(8,128)(2,1)S(1)}, u32[]{:S(2)}, u32[]{:S(2)}) %collective-permute-start.3) | collective-permute-done | bytes 2097184 | tf_op jit(solution)/shard_map/ppermute | solution.py:34
  50.6 1.3 %slice.9 = bf16[256,2048]{1,0:T(8,128)(2,1)} slice(bf16[512,2048]{1,0:T(8,128)(2,1)S(1)} %collective-permute-done.3.z.refs_6_), slice={[256:512], [0:2048]} | slice | bytes 2097152 | tf_op jit(solution)/shard_map/slice | solution.py:337
  51.9 3.3 %collective-permute-done.4 = bf16[512,128]{1,0:T(8,128)(2,1)S(1)} collective-permute-done((bf16[512,128]{1,0:T(8,128)(2,1)S(1)}, bf16[512,128]{1,0:T(8,128)(2,1)S(1)}, u32[]{:S(2)}, u32[]{:S(2)}) %collective-permute-start.4) | collective-permute-done | bytes 131104 | tf_op jit(solution)/shard_map/ppermute | solution.py:39
  55.2 2.9 %collective-permute-start.12 = (bf16[256,2048]{1,0:T(8,128)(2,1)}, bf16[256,2048]{1,0:T(8,128)(2,1)}, u32[]{:S(2)}, u32[]{:S(2)}) collective-permute-start(bf16[256,2048]{1,0:T(8,128)(2,1)} %slice.9), channel_id=1, source_target_pairs={{0,4},{4,0},{8,12},{12,8},{16,20},{20,16},{24,28},{28,24},{1,5},{5... | collective-permute-start | bytes 3145736 | tf_op jit(solution)/shard_map/ppermute | solution.py:39
  58.7 2.7 %shard_map.38 = (f32[256,1024]{1,0:T(8,128)S(1)}, bf16[256,1024]{1,0:T(8,128)(2,1)S(1)}) custom-call(bf16[512,2048]{1,0:T(8,128)(2,1)S(1)} %copy-done.1, bf16[512,2048]{1,0:T(8,128)(2,1)S(1)} %collective-permute-done.2.y.refs_5_, bf16[512,2048]{1,0:T(8,128)(2,1)S(1)} %collective-permute-done.3.z.refs_6_), custom_call_target="tpu_custom_call" | custom-call | tf_op jit(solution)/shard_map/pallas_call | solution.py:105
  61.4 10.6 %conditional.1 = (bf16[128,1024]{1,0:T(8,128)(2,1)S(1)}, bf16[128,512]{1,0:T(8,128)(2,1)S(1)}, bf16[128,512]{1,0:T(8,128)(2,1)S(1)}, bf16[256,1024]{1,0:T(8,128)(2,1)S(1)}, bf16[256,1024]{1,0:T(8,128)(2,1)}) conditional(s32[]{:T(128)} %bitcast, () %tuple.20, (bf16[256,1024]{1,0:T(8,128)(2,1)S(1)}, f32[256,1024]{1,0:T(8,128)S(1)}, ...), branch_computations={%region_0.0_spmd, %region_1.0_spmd} | conditional | flops 917504 | bytes 10223736 | solution.py:352
  61.5 1.9 %collective-permute-done.other = bf16[256,1024]{1,0:T(8,128)(2,1)S(1)} collective-permute-done((bf16[256,1024]{1,0:T(8,128)(2,1)S(1)}, bf16[256,1024]{1,0:T(8,128)(2,1)S(1)}, u32[]{:S(2)}, u32[]{:S(2)}) %collective-permute-start) | collective-permute-done | bytes 524320 | tf_op jit(solution)/shard_map/cond/branch_1_fun/ppermute | solution.py:39
  63.5 1.6 %collective-permute-start.1 = (bf16[128,1024]{1,0:T(8,128)(2,1)S(1)}, bf16[128,1024]{1,0:T(8,128)(2,1)S(1)}, u32[]{:S(2)}, u32[]{:S(2)}) collective-permute-start(bf16[128,1024]{1,0:T(8,128)(2,1)S(1)} %get-tuple-element.20), channel_id=1, source_target_pairs={{0,2},{1,3},{2,0},{3,1},{4,6},{5,7},{6,4},{7,5},{8,10},{9,11},{10,... | collective-permute-start | bytes 786440 | tf_op jit(solution)/shard_map/cond/branch_1_fun/ppermute | solution.py:39
  65.9 6.0 %collective-permute-done.1.other = bf16[128,1024]{1,0:T(8,128)(2,1)S(1)} collective-permute-done((bf16[128,1024]{1,0:T(8,128)(2,1)S(1)}, bf16[128,1024]{1,0:T(8,128)(2,1)S(1)}, u32[]{:S(2)}, u32[]{:S(2)}) %collective-permute-start.1) | collective-permute-done | bytes 262176 | tf_op jit(solution)/shard_map/cond/branch_1_fun/ppermute | solution.py:39
  72.1 2.2 %collective-permute-start.9 = (bf16[128,1024]{1,0:T(8,128)(2,1)S(1)}, bf16[128,1024]{1,0:T(8,128)(2,1)S(1)}, u32[]{:S(2)}, u32[]{:S(2)}) collective-permute-start(bf16[128,1024]{1,0:T(8,128)(2,1)S(1)} %get-tuple-element.63), channel_id=1, source_target_pairs={{0,8},{8,16},{16,24},{24,0},{1,9},{9,17},{17,25},{25,1},{2,10},{10... | collective-permute-start | bytes 786440 | tf_op jit(solution)/shard_map/ppermute | solution.py:34
  75.3 7.0 %collective-permute-done.12.refs_7_ = bf16[256,2048]{1,0:T(8,128)(2,1)} collective-permute-done((bf16[256,2048]{1,0:T(8,128)(2,1)}, bf16[256,2048]{1,0:T(8,128)(2,1)}, u32[]{:S(2)}, u32[]{:S(2)}) %collective-permute-start.12) | collective-permute-done | bytes 1048608 | tf_op jit(solution)/shard_map/ppermute | solution.py:39
  82.4 2.0 %collective-permute-start.17 = (bf16[256,1024]{1,0:T(8,128)(2,1)S(1)}, bf16[256,1024]{1,0:T(8,128)(2,1)S(1)}, u32[]{:S(2)}, u32[]{:S(2)}) collective-permute-start(bf16[256,1024]{1,0:T(8,128)(2,1)S(1)} %get-tuple-element.78), channel_id=1, source_target_pairs={{0,4},{4,0},{8,12},{12,8},{16,20},{20,16},{24,28},{28,24},{1,5},{5... | collective-permute-start | bytes 1572872 | tf_op jit(solution)/shard_map/ppermute | solution.py:39
  85.1 1.6 %collective-permute-start.14 = (bf16[128,1536]{1,0:T(8,128)(2,1)S(1)}, bf16[128,1536]{1,0:T(8,128)(2,1)S(1)}, u32[]{:S(2)}, u32[]{:S(2)}) collective-permute-start(bf16[128,1536]{1,0:T(8,128)(2,1)S(1)} %shard_map.40.refs_1_), channel_id=1, source_target_pairs={{0,2},{1,3},{2,0},{3,1},{4,6},{5,7},{6,4},{7,5},{8,10},{9,11},{10,... | collective-permute-start | bytes 1179656 | tf_op jit(solution)/shard_map/ppermute | solution.py:39
  87.2 2.0 %collective-permute-start.19 = (bf16[256,1024]{1,0:T(8,128)(2,1)}, bf16[256,1024]{1,0:T(8,128)(2,1)S(1)}, u32[]{:S(2)}, u32[]{:S(2)}) collective-permute-start(bf16[256,1024]{1,0:T(8,128)(2,1)} %get-tuple-element.82), channel_id=1, source_target_pairs={{0,4},{4,0},{8,12},{12,8},{16,20},{20,16},{24,28},{28,24},{1,5},{5... | collective-permute-start | bytes 1572872 | tf_op jit(solution)/shard_map/ppermute | solution.py:39
  89.2 6.3 %collective-permute-done.14.refs_2_ = bf16[128,1536]{1,0:T(8,128)(2,1)S(1)} collective-permute-done((bf16[128,1536]{1,0:T(8,128)(2,1)S(1)}, bf16[128,1536]{1,0:T(8,128)(2,1)S(1)}, u32[]{:S(2)}, u32[]{:S(2)}) %collective-permute-start.14) | collective-permute-done | bytes 393248 | tf_op jit(solution)/shard_map/ppermute | solution.py:39
  95.5 1.7 %collective-permute-done.17.u = bf16[256,1024]{1,0:T(8,128)(2,1)S(1)} collective-permute-done((bf16[256,1024]{1,0:T(8,128)(2,1)S(1)}, bf16[256,1024]{1,0:T(8,128)(2,1)S(1)}, u32[]{:S(2)}, u32[]{:S(2)}) %collective-permute-start.17) | collective-permute-done | bytes 524320 | tf_op jit(solution)/shard_map/ppermute | solution.py:39
  97.8 1.4 %collective-permute-done.7.a2 = bf16[128,512]{1,0:T(8,128)(2,1)S(1)} collective-permute-done((bf16[128,512]{1,0:T(8,128)(2,1)S(1)}, bf16[128,512]{1,0:T(8,128)(2,1)S(1)}, u32[]{:S(2)}, u32[]{:S(2)}) %collective-permute-start.7) | collective-permute-done | bytes 131104 | tf_op jit(solution)/shard_map/ppermute | solution.py:39
  100.6 5.5 %shard_map.41 = (f32[512,2048]{1,0:T(8,128)S(1)}, bf16[512,496]{1,0:T(8,128)(2,1)S(1)}) custom-call(bf16[512,512]{1,0:T(8,128)(2,1)S(1)} %shard_map.39.refs_0_, bf16[128,1536]{1,0:T(8,128)(2,1)S(1)} %shard_map.40.refs_1_, bf16[128,1536]{1,0:T(8,128)(2,1)S(1)} %collective-permute-done.14.refs_2_, bf16[128,1536]{1,0:T(8,128)(2,1)S(1)} %collective-permute-done.15.refs_3_, ...), custom_call_target="tpu_custom_call" | custom-call | tf_op jit(solution)/shard_map/pallas_call | solution.py:224
  106.1 1.6 %shard_map.42.rest_0_ = bf16[512,2048]{1,0:T(8,128)(2,1)} custom-call(bf16[512,496]{1,0:T(8,128)(2,1)S(1)} %get-tuple-element.80.weights, f32[512,2048]{1,0:T(8,128)S(1)} %get-tuple-element.81.total, bf16[256,1024]{1,0:T(8,128)(2,1)S(1)} %collective-permute-done.17.u, bf16[240,1024]{1,0:T(8,128)(2,1)S(1)} %collective-permute-done.16.w, ...), custom_call_target="tpu_custom_call" | custom-call | flops 536870912 | bytes 4194304 | tf_op jit(solution)/shard_map/pallas_call | solution.py:263
  107.8 1.6 %shard_map.44 = bf16[512,2048]{1,0:T(8,128)(2,1)} custom-call(bf16[512,496]{1,0:T(8,128)(2,1)S(1)} %get-tuple-element.80.weights, f32[512,2048]{1,0:T(8,128)S(1)} %get-tuple-element.81.total, bf16[256,1024]{1,0:T(8,128)(2,1)S(1)} %collective-permute-done.19.other.u, ...), custom_call_target="tpu_custom_call", output_to_operand_aliasing={{}: (4, {})} | custom-call | flops 536870912 | bytes 4194304 | tf_op jit(solution)/shard_map/pallas_call | solution.py:263
  (48 shorter events, 8.9 us)
Async XLA Ops:
  0.0 50.4 %collective-permute-start.3 = (bf16[512,2048]{1,0:T(8,128)(2,1)}, bf16[512,2048]{1,0:T(8,128)(2,1)S(1)}, u32[]{:S(2)}, u32[]{:S(2)}) collective-permute-start(bf16[512,2048]{1,0:T(8,128)(2,1)} %x.3), channel_id=1, source_target_pairs={{0,24},{4,12},{8,0},{12,20},{16,8},{20,28},{24,16},{28,4},{1,25},{... | collective-permute-start | bytes 6291464 | tf_op jit(solution)/shard_map/ppermute | solution.py:34
  5.0 50.1 %collective-permute-start.2 = (bf16[512,2048]{1,0:T(8,128)(2,1)}, bf16[512,2048]{1,0:T(8,128)(2,1)S(1)}, u32[]{:S(2)}, u32[]{:S(2)}) collective-permute-start(bf16[512,2048]{1,0:T(8,128)(2,1)} %x.3), channel_id=1, source_target_pairs={{0,4},{4,0},{8,12},{12,8},{16,20},{20,16},{24,28},{28,24},{1,5},{5... | collective-permute-start | bytes 6291464 | tf_op jit(solution)/shard_map/ppermute | solution.py:39
  7.8 50.9 %copy-start.1 = (bf16[512,2048]{1,0:T(8,128)(2,1)S(1)}, bf16[512,2048]{1,0:T(8,128)(2,1)}, u32[]{:S(2)}) copy-start(bf16[512,2048]{1,0:T(8,128)(2,1)} %x.3) | copy-start | bytes 6291460
  11.7 4.0 %collective-permute-start.5 = (bf16[512,128]{1,0:T(8,128)(2,1)S(1)}, bf16[512,128]{1,0:T(8,128)(2,1)S(1)}, u32[]{:S(2)}, u32[]{:S(2)}) collective-permute-start(bf16[512,128]{1,0:T(8,128)(2,1)S(1)} %get-tuple-element.61), channel_id=1, source_target_pairs={{4,12},{12,20},{20,28},{28,4},{5,13},{13,21},{21,29},{29,5},{6,14}... | collective-permute-start | bytes 393224 | tf_op jit(solution)/shard_map/ppermute | solution.py:34
  12.4 42.8 %collective-permute-start.4 = (bf16[512,128]{1,0:T(8,128)(2,1)S(1)}, bf16[512,128]{1,0:T(8,128)(2,1)S(1)}, u32[]{:S(2)}, u32[]{:S(2)}) collective-permute-start(bf16[512,128]{1,0:T(8,128)(2,1)S(1)} %get-tuple-element.60), channel_id=1, source_target_pairs={{0,4},{4,0},{8,12},{12,8},{16,20},{20,16},{24,28},{28,24},{1,5},{5... | collective-permute-start | bytes 393224 | tf_op jit(solution)/shard_map/ppermute | solution.py:39
  50.4 11.0 %copy-start.5 = (bf16[512,2048]{1,0:T(8,128)(2,1)}, bf16[512,2048]{1,0:T(8,128)(2,1)S(1)}, u32[]{:S(2)}) copy-start(bf16[512,2048]{1,0:T(8,128)(2,1)S(1)} %collective-permute-done.3.z.refs_6_) | copy-start | bytes 6291460
  50.4 31.9 %collective-permute-start.13 = (bf16[272,2048]{1,0:T(8,128)(2,1)}, bf16[272,2048]{1,0:T(8,128)(2,1)S(1)}, u32[]{:S(2)}, u32[]{:S(2)}) collective-permute-start(bf16[272,2048]{1,0:T(8,128)(2,1)} %get-tuple-element.68), channel_id=1, source_target_pairs={{0,8},{4,28},{8,16},{12,4},{16,24},{20,12},{24,0},{28,20},{1,9},{5... | collective-permute-start | bytes 3342344 | tf_op jit(solution)/shard_map/ppermute | solution.py:34
  55.2 27.2 %collective-permute-start.12 = (bf16[256,2048]{1,0:T(8,128)(2,1)}, bf16[256,2048]{1,0:T(8,128)(2,1)}, u32[]{:S(2)}, u32[]{:S(2)}) collective-permute-start(bf16[256,2048]{1,0:T(8,128)(2,1)} %slice.9), channel_id=1, source_target_pairs={{0,4},{4,0},{8,12},{12,8},{16,20},{20,16},{24,28},{28,24},{1,5},{5... | collective-permute-start | bytes 3145736 | tf_op jit(solution)/shard_map/ppermute | solution.py:39
  61.4 2.0 %collective-permute-start = (bf16[256,1024]{1,0:T(8,128)(2,1)S(1)}, bf16[256,1024]{1,0:T(8,128)(2,1)S(1)}, u32[]{:S(2)}, u32[]{:S(2)}) collective-permute-start(bf16[256,1024]{1,0:T(8,128)(2,1)S(1)} %get-tuple-element.18), channel_id=1, source_target_pairs={{0,1},{1,0},{2,3},{3,2},{4,5},{5,4},{6,7},{7,6},{8,9},{9,8},{10,11... | collective-permute-start | bytes 1572872 | tf_op jit(solution)/shard_map/cond/branch_1_fun/ppermute | solution.py:39
  63.5 8.4 %collective-permute-start.1 = (bf16[128,1024]{1,0:T(8,128)(2,1)S(1)}, bf16[128,1024]{1,0:T(8,128)(2,1)S(1)}, u32[]{:S(2)}, u32[]{:S(2)}) collective-permute-start(bf16[128,1024]{1,0:T(8,128)(2,1)S(1)} %get-tuple-element.20), channel_id=1, source_target_pairs={{0,2},{1,3},{2,0},{3,1},{4,6},{5,7},{6,4},{7,5},{8,10},{9,11},{10,... | collective-permute-start | bytes 786440 | tf_op jit(solution)/shard_map/cond/branch_1_fun/ppermute | solution.py:39
  72.1 13.0 %collective-permute-start.9 = (bf16[128,1024]{1,0:T(8,128)(2,1)S(1)}, bf16[128,1024]{1,0:T(8,128)(2,1)S(1)}, u32[]{:S(2)}, u32[]{:S(2)}) collective-permute-start(bf16[128,1024]{1,0:T(8,128)(2,1)S(1)} %get-tuple-element.63), channel_id=1, source_target_pairs={{0,8},{8,16},{16,24},{24,0},{1,9},{9,17},{17,25},{25,1},{2,10},{10... | collective-permute-start | bytes 786440 | tf_op jit(solution)/shard_map/ppermute | solution.py:34
  74.3 10.4 %collective-permute-start.10 = (bf16[128,512]{1,0:T(8,128)(2,1)S(1)}, bf16[128,512]{1,0:T(8,128)(2,1)S(1)}, u32[]{:S(2)}, u32[]{:S(2)}) collective-permute-start(bf16[128,512]{1,0:T(8,128)(2,1)S(1)} %get-tuple-element.62.a0), channel_id=1, source_target_pairs={{4,28},{12,4},{20,12},{28,20},{5,29},{13,5},{21,13},{29,21},{6,30}... | collective-permute-start | bytes 393224 | tf_op jit(solution)/shard_map/ppermute | solution.py:34
  74.9 10.1 %collective-permute-start.11 = (bf16[128,512]{1,0:T(8,128)(2,1)S(1)}, bf16[128,512]{1,0:T(8,128)(2,1)S(1)}, u32[]{:S(2)}, u32[]{:S(2)}) collective-permute-start(bf16[128,512]{1,0:T(8,128)(2,1)S(1)} %get-tuple-element.72.own), channel_id=1, source_target_pairs={{0,4},{4,0},{8,12},{12,8},{16,20},{20,16},{24,28},{28,24},{1,5},{5... | collective-permute-start | bytes 393224 | tf_op jit(solution)/shard_map/ppermute | solution.py:39
  82.4 14.9 %collective-permute-start.17 = (bf16[256,1024]{1,0:T(8,128)(2,1)S(1)}, bf16[256,1024]{1,0:T(8,128)(2,1)S(1)}, u32[]{:S(2)}, u32[]{:S(2)}) collective-permute-start(bf16[256,1024]{1,0:T(8,128)(2,1)S(1)} %get-tuple-element.78), channel_id=1, source_target_pairs={{0,4},{4,0},{8,12},{12,8},{16,20},{20,16},{24,28},{28,24},{1,5},{5... | collective-permute-start | bytes 1572872 | tf_op jit(solution)/shard_map/ppermute | solution.py:39
  84.4 11.1 %collective-permute-start.16 = (bf16[240,1024]{1,0:T(8,128)(2,1)}, bf16[240,1024]{1,0:T(8,128)(2,1)S(1)}, u32[]{:S(2)}, u32[]{:S(2)}) collective-permute-start(bf16[240,1024]{1,0:T(8,128)(2,1)} %copy-done.4), channel_id=1, source_target_pairs={{0,8},{4,28},{8,16},{12,4},{16,24},{20,12},{24,0},{28,20},{1,9},{5... | collective-permute-start | bytes 1474568 | tf_op jit(solution)/shard_map/ppermute | solution.py:34
  85.1 15.5 %copy-start.6 = (bf16[512,2048]{1,0:T(8,128)(2,1)S(1)}, bf16[512,2048]{1,0:T(8,128)(2,1)}, u32[]{:S(2)}) copy-start(bf16[512,2048]{1,0:T(8,128)(2,1)} %copy-done.5) | copy-start | bytes 6291460
  85.1 10.4 %collective-permute-start.14 = (bf16[128,1536]{1,0:T(8,128)(2,1)S(1)}, bf16[128,1536]{1,0:T(8,128)(2,1)S(1)}, u32[]{:S(2)}, u32[]{:S(2)}) collective-permute-start(bf16[128,1536]{1,0:T(8,128)(2,1)S(1)} %shard_map.40.refs_1_), channel_id=1, source_target_pairs={{0,2},{1,3},{2,0},{3,1},{4,6},{5,7},{6,4},{7,5},{8,10},{9,11},{10,... | collective-permute-start | bytes 1179656 | tf_op jit(solution)/shard_map/ppermute | solution.py:39
  86.7 10.6 %collective-permute-start.6 = (bf16[128,512]{1,0:T(8,128)(2,1)S(1)}, bf16[128,512]{1,0:T(8,128)(2,1)S(1)}, u32[]{:S(2)}, u32[]{:S(2)}) collective-permute-start(bf16[128,512]{1,0:T(8,128)(2,1)S(1)} %get-tuple-element.62.a0), channel_id=1, source_target_pairs={{0,2},{1,3},{2,0},{3,1},{4,6},{5,7},{6,4},{7,5},{8,10},{9,11},{10,... | collective-permute-start | bytes 393224 | tf_op jit(solution)/shard_map/ppermute | solution.py:39
  87.2 20.5 %collective-permute-start.19 = (bf16[256,1024]{1,0:T(8,128)(2,1)}, bf16[256,1024]{1,0:T(8,128)(2,1)S(1)}, u32[]{:S(2)}, u32[]{:S(2)}) collective-permute-start(bf16[256,1024]{1,0:T(8,128)(2,1)} %get-tuple-element.82), channel_id=1, source_target_pairs={{0,4},{4,0},{8,12},{12,8},{16,20},{20,16},{24,28},{28,24},{1,5},{5... | collective-permute-start | bytes 1572872 | tf_op jit(solution)/shard_map/ppermute | solution.py:39
  95.5 12.2 %collective-permute-start.20 = (bf16[240,1024]{1,0:T(8,128)(2,1)}, bf16[240,1024]{1,0:T(8,128)(2,1)S(1)}, u32[]{:S(2)}, u32[]{:S(2)}) collective-permute-start(bf16[240,1024]{1,0:T(8,128)(2,1)} %copy-done.3), channel_id=1, source_target_pairs={{0,8},{4,28},{8,16},{12,4},{16,24},{20,12},{24,0},{28,20},{1,9},{5... | collective-permute-start | bytes 1474568 | tf_op jit(solution)/shard_map/ppermute | solution.py:34
  95.5 5.0 %collective-permute-start.15 = (bf16[128,1536]{1,0:T(8,128)(2,1)S(1)}, bf16[128,1536]{1,0:T(8,128)(2,1)S(1)}, u32[]{:S(2)}, u32[]{:S(2)}) collective-permute-start(bf16[128,1536]{1,0:T(8,128)(2,1)S(1)} %shard_map.40.refs_1_), channel_id=1, source_target_pairs={{0,1},{1,0},{2,3},{3,2},{4,5},{5,4},{6,7},{7,6},{8,9},{9,8},{10,11... | collective-permute-start | bytes 1179656 | tf_op jit(solution)/shard_map/ppermute | solution.py:39
  97.2 3.3 %collective-permute-start.18 = (bf16[128,1536]{1,0:T(8,128)(2,1)S(1)}, bf16[128,1536]{1,0:T(8,128)(2,1)S(1)}, u32[]{:S(2)}, u32[]{:S(2)}) collective-permute-start(bf16[128,1536]{1,0:T(8,128)(2,1)S(1)} %collective-permute-done.14.refs_2_), channel_id=1, source_target_pairs={{0,1},{1,0},{2,3},{3,2},{4,5},{5,4},{6,7},{7,6},{8,9},{9,8},{10,11... | collective-permute-start | bytes 1179656 | tf_op jit(solution)/shard_map/ppermute | solution.py:39
  97.2 1.9 %collective-permute-start.7 = (bf16[128,512]{1,0:T(8,128)(2,1)S(1)}, bf16[128,512]{1,0:T(8,128)(2,1)S(1)}, u32[]{:S(2)}, u32[]{:S(2)}) collective-permute-start(bf16[128,512]{1,0:T(8,128)(2,1)S(1)} %get-tuple-element.62.a0), channel_id=1, source_target_pairs={{0,1},{1,0},{2,3},{3,2},{4,5},{5,4},{6,7},{7,6},{8,9},{9,8},{10,11... | collective-permute-start | bytes 393224 | tf_op jit(solution)/shard_map/ppermute | solution.py:39
  99.2 1.3 %collective-permute-start.8 = (bf16[128,512]{1,0:T(8,128)(2,1)S(1)}, bf16[128,512]{1,0:T(8,128)(2,1)S(1)}, u32[]{:S(2)}, u32[]{:S(2)}) collective-permute-start(bf16[128,512]{1,0:T(8,128)(2,1)S(1)} %collective-permute-done.6.a1), channel_id=1, source_target_pairs={{0,1},{1,0},{2,3},{3,2},{4,5},{5,4},{6,7},{7,6},{8,9},{9,8},{10,11... | collective-permute-start | bytes 393224 | tf_op jit(solution)/shard_map/ppermute | solution.py:39
  (5 other events, 7.0 us)

commit v7 on v5

--- a/solution.py
+++ b/solution.py
@@ -8,7 +8,7 @@
 from jax.sharding import PartitionSpec as P
 
 MIB = 1024 * 1024
-SEEN_COST, MOST_COST, SETTLE_COST = 10, 10, 25
+SEEN_COST, MOST_COST, SETTLE_COST = 10, 10, 40
 F32, BF16 = jnp.float32, jnp.bfloat16
 VMEM = pl.BlockSpec(memory_space=pltpu.VMEM)
 ANY = pl.BlockSpec(memory_space=pl.ANY)

time: 108 us -> 108 us (level)
  no operation moved by 1% of the time
where the time goes in v7:
time: 108 us
  waiting for transfers between devices  65.9 us (61%)
  starting transfers between devices  21.9 us (20%)
  Pallas kernels  13.2 us (12%)
  local copies, waits for them, and re-layouts  6.09 us (6%)
    ppermute x6, waiting for transfers between devices, moved(): return lax.ppermute(value, axis, pairs)  39.8 us
    ppermute x13, waiting for transfers between devices, swapped(): lax.ppermute(value, axis, [(i, i ^ distance) for i in range(devices)])  26.1 us
    ppermute x13, starting transfers between devices, swapped(): lax.ppermute(value, axis, [(i, i ^ distance) for i in range(devices)])  13.2 us
    ppermute x6, starting transfers between devices, moved(): return lax.ppermute(value, axis, pairs)  8.73 us
    pallas_call x1, Pallas kernels, apply_most(): pl.pallas_call(functools.partial(most_kernel, places, firsts), in_specs=[...  5.52 us
    unnamed x14, local copies, waits for them, and re-layouts  3.7 us
    pallas_call x1, Pallas kernels, gram(): pl.pallas_call(gram_kernel, in_specs=[VMEM] * 3, out_specs=[VMEM] * 2, ou...  2.69 us
    pallas_call x1, Pallas kernels, prepare(): pl.pallas_call(prepare_kernel, in_specs=[VMEM] * 3, out_specs=[VMEM] * 4...  2.39 us
  transfers between devices with their start and end apart: 19, of which 13 were waited for; matrix products, arithmetic and copies ran while one was open for 2% of the time, Pallas kernels for 10%

profile of v7, /device:TPU:0, one launch (start us, length us, event | category | flops | bytes accessed | tf_op | source)
XLA Modules:
  0.0 108.0 jit_solution(18439588871466029873)
XLA Ops:
  0.0 5.0 %collective-permute-start.3 = (bf16[512,2048]{1,0:T(8,128)(2,1)}, bf16[512,2048]{1,0:T(8,128)(2,1)S(1)}, u32[]{:S(2)}, u32[]{:S(2)}) collective-permute-start(bf16[512,2048]{1,0:T(8,128)(2,1)} %x.3), channel_id=1, source_target_pairs={{0,24},{4,12},{8,0},{12,20},{16,8},{20,28},{24,16},{28,4},{1,25},{... | collective-permute-start | bytes 6291464 | tf_op jit(solution)/shard_map/ppermute | solution.py:34
  5.1 1.7 %copy-done = bf16[512,2048]{1,0:T(8,128)(2,1)S(1)} copy-done((bf16[512,2048]{1,0:T(8,128)(2,1)S(1)}, bf16[512,2048]{1,0:T(8,128)(2,1)}, u32[]{:S(2)}) %copy-start) | copy-done | bytes 2097176
  6.7 1.0 copy-done.2
  7.8 2.4 %shard_map.37 = (bf16[240,2048]{1,0:T(8,128)(2,1)S(1)}, bf16[272,2048]{1,0:T(8,128)(2,1)}, bf16[512,128]{1,0:T(8,128)(2,1)S(1)}, bf16[512,128]{1,0:T(8,128)(2,1)S(1)}, s32[1,1]{1,0:T(1,128)}) custom-call(bf16[512,2048]{1,0:T(8,128)(2,1)S(1)} %copy-done, bf16[512,512]{1,0:T(8,128)(2,1)S(1)} %copy-done.2, bf16[512,512]{1,0:T(8,128)(2,1)} %far.1), custom_call_target="tpu_custom_call" | custom-call | bytes 6291456 | tf_op jit(solution)/shard_map/pallas_call | solution.py:68
  10.2 1.0 copy-done.3
  11.8 3.3 %collective-permute-start.4 = (bf16[512,128]{1,0:T(8,128)(2,1)S(1)}, bf16[512,128]{1,0:T(8,128)(2,1)S(1)}, u32[]{:S(2)}, u32[]{:S(2)}) collective-permute-start(bf16[512,128]{1,0:T(8,128)(2,1)S(1)} %get-tuple-element.55), channel_id=1, source_target_pairs={{0,4},{4,0},{8,12},{12,8},{16,20},{20,16},{24,28},{28,24},{1,5},{5... | collective-permute-start | bytes 393224 | tf_op jit(solution)/shard_map/ppermute | solution.py:39
  15.1 35.3 %collective-permute-done.3.z.refs_6_ = bf16[512,2048]{1,0:T(8,128)(2,1)S(1)} collective-permute-done((bf16[512,2048]{1,0:T(8,128)(2,1)}, bf16[512,2048]{1,0:T(8,128)(2,1)S(1)}, u32[]{:S(2)}, u32[]{:S(2)}) %collective-permute-start.3) | collective-permute-done | bytes 2097184 | tf_op jit(solution)/shard_map/ppermute | solution.py:34
  50.6 1.3 %slice.6 = bf16[256,2048]{1,0:T(8,128)(2,1)} slice(bf16[512,2048]{1,0:T(8,128)(2,1)S(1)} %collective-permute-done.3.z.refs_6_), slice={[256:512], [0:2048]} | slice | bytes 2097152 | tf_op jit(solution)/shard_map/slice | solution.py:326
  51.9 3.2 %collective-permute-done.4 = bf16[512,128]{1,0:T(8,128)(2,1)S(1)} collective-permute-done((bf16[512,128]{1,0:T(8,128)(2,1)S(1)}, bf16[512,128]{1,0:T(8,128)(2,1)S(1)}, u32[]{:S(2)}, u32[]{:S(2)}) %collective-permute-start.4) | collective-permute-done | bytes 131104 | tf_op jit(solution)/shard_map/ppermute | solution.py:39
  55.2 2.9 %collective-permute-start.12 = (bf16[256,2048]{1,0:T(8,128)(2,1)}, bf16[256,2048]{1,0:T(8,128)(2,1)}, u32[]{:S(2)}, u32[]{:S(2)}) collective-permute-start(bf16[256,2048]{1,0:T(8,128)(2,1)} %slice.6), channel_id=1, source_target_pairs={{0,4},{4,0},{8,12},{12,8},{16,20},{20,16},{24,28},{28,24},{1,5},{5... | collective-permute-start | bytes 3145736 | tf_op jit(solution)/shard_map/ppermute | solution.py:39
  58.8 2.7 %shard_map.38 = (f32[256,1024]{1,0:T(8,128)S(1)}, bf16[256,1024]{1,0:T(8,128)(2,1)S(1)}) custom-call(bf16[512,2048]{1,0:T(8,128)(2,1)S(1)} %copy-done.1, bf16[512,2048]{1,0:T(8,128)(2,1)S(1)} %collective-permute-done.2.y.refs_5_, bf16[512,2048]{1,0:T(8,128)(2,1)S(1)} %collective-permute-done.3.z.refs_6_), custom_call_target="tpu_custom_call" | custom-call | tf_op jit(solution)/shard_map/pallas_call | solution.py:102
  61.5 10.6 %conditional.1 = (bf16[128,1024]{1,0:T(8,128)(2,1)S(1)}, bf16[128,512]{1,0:T(8,128)(2,1)S(1)}, bf16[128,512]{1,0:T(8,128)(2,1)S(1)}, bf16[256,2048]{1,0:T(8,128)(2,1)}) conditional(s32[]{:T(128)} %bitcast, () %tuple.19, (bf16[256,1024]{1,0:T(8,128)(2,1)S(1)}, f32[256,1024]{1,0:T(8,128)S(1)}, bf16[512,512]{1,0:T(8,128)(2,1)S(1)}, ...), branch_computations={%region_0.0_spmd, %region_1.0_spmd} | conditional | flops 917504 | bytes 10223728 | solution.py:340
  61.6 1.9 %collective-permute-done.other = bf16[256,1024]{1,0:T(8,128)(2,1)S(1)} collective-permute-done((bf16[256,1024]{1,0:T(8,128)(2,1)S(1)}, bf16[256,1024]{1,0:T(8,128)(2,1)S(1)}, u32[]{:S(2)}, u32[]{:S(2)}) %collective-permute-start) | collective-permute-done | bytes 524320 | tf_op jit(solution)/shard_map/cond/branch_1_fun/ppermute | solution.py:39
  63.6 1.6 %collective-permute-start.1 = (bf16[128,1024]{1,0:T(8,128)(2,1)S(1)}, bf16[128,1024]{1,0:T(8,128)(2,1)S(1)}, u32[]{:S(2)}, u32[]{:S(2)}) collective-permute-start(bf16[128,1024]{1,0:T(8,128)(2,1)S(1)} %get-tuple-element.20), channel_id=1, source_target_pairs={{0,2},{1,3},{2,0},{3,1},{4,6},{5,7},{6,4},{7,5},{8,10},{9,11},{10,... | collective-permute-start | bytes 786440 | tf_op jit(solution)/shard_map/cond/branch_1_fun/ppermute | solution.py:39
  65.1 1.1 %slice.4 = bf16[256,2048]{1,0:T(8,128)(2,1)} slice(bf16[512,2048]{1,0:T(8,128)(2,1)S(1)} %get-tuple-element.27), slice={[0:256], [0:2048]} | slice | bytes 2097152 | tf_op jit(solution)/shard_map/cond/branch_1_fun/slice | solution.py:333
  66.2 5.8 %collective-permute-done.1.other = bf16[128,1024]{1,0:T(8,128)(2,1)S(1)} collective-permute-done((bf16[128,1024]{1,0:T(8,128)(2,1)S(1)}, bf16[128,1024]{1,0:T(8,128)(2,1)S(1)}, u32[]{:S(2)}, u32[]{:S(2)}) %collective-permute-start.1) | collective-permute-done | bytes 262176 | tf_op jit(solution)/shard_map/cond/branch_1_fun/ppermute | solution.py:39
  72.1 2.2 %collective-permute-start.9 = (bf16[128,1024]{1,0:T(8,128)(2,1)S(1)}, bf16[128,1024]{1,0:T(8,128)(2,1)S(1)}, u32[]{:S(2)}, u32[]{:S(2)}) collective-permute-start(bf16[128,1024]{1,0:T(8,128)(2,1)S(1)} %get-tuple-element.58), channel_id=1, source_target_pairs={{0,8},{8,16},{16,24},{24,0},{1,9},{9,17},{17,25},{25,1},{2,10},{10... | collective-permute-start | bytes 786440 | tf_op jit(solution)/shard_map/ppermute | solution.py:34
  75.1 3.7 %collective-permute-done.13.refs_8_ = bf16[272,2048]{1,0:T(8,128)(2,1)S(1)} collective-permute-done((bf16[272,2048]{1,0:T(8,128)(2,1)}, bf16[272,2048]{1,0:T(8,128)(2,1)S(1)}, u32[]{:S(2)}, u32[]{:S(2)}) %collective-permute-start.13) | collective-permute-done | bytes 1114144 | tf_op jit(solution)/shard_map/ppermute | solution.py:34
  78.8 3.0 %collective-permute-done.12.refs_7_ = bf16[256,2048]{1,0:T(8,128)(2,1)} collective-permute-done((bf16[256,2048]{1,0:T(8,128)(2,1)}, bf16[256,2048]{1,0:T(8,128)(2,1)}, u32[]{:S(2)}, u32[]{:S(2)}) %collective-permute-start.12) | collective-permute-done | bytes 1048608 | tf_op jit(solution)/shard_map/ppermute | solution.py:39
  81.8 2.6 %collective-permute-start.17 = (bf16[256,2048]{1,0:T(8,128)(2,1)}, bf16[256,2048]{1,0:T(8,128)(2,1)S(1)}, u32[]{:S(2)}, u32[]{:S(2)}) collective-permute-start(bf16[256,2048]{1,0:T(8,128)(2,1)} %get-tuple-element.73), channel_id=1, source_target_pairs={{0,4},{4,0},{8,12},{12,8},{16,20},{20,16},{24,28},{28,24},{1,5},{5... | collective-permute-start | bytes 3145736 | tf_op jit(solution)/shard_map/ppermute | solution.py:39
  85.1 1.6 %collective-permute-start.14 = (bf16[128,1536]{1,0:T(8,128)(2,1)S(1)}, bf16[128,1536]{1,0:T(8,128)(2,1)S(1)}, u32[]{:S(2)}, u32[]{:S(2)}) collective-permute-start(bf16[128,1536]{1,0:T(8,128)(2,1)S(1)} %shard_map.40.refs_1_), channel_id=1, source_target_pairs={{0,2},{1,3},{2,0},{3,1},{4,6},{5,7},{6,4},{7,5},{8,10},{9,11},{10,... | collective-permute-start | bytes 1179656 | tf_op jit(solution)/shard_map/ppermute | solution.py:39
  87.2 9.7 %collective-permute-done.6.a1 = bf16[128,512]{1,0:T(8,128)(2,1)S(1)} collective-permute-done((bf16[128,512]{1,0:T(8,128)(2,1)S(1)}, bf16[128,512]{1,0:T(8,128)(2,1)S(1)}, u32[]{:S(2)}, u32[]{:S(2)}) %collective-permute-start.6) | collective-permute-done | bytes 131104 | tf_op jit(solution)/shard_map/ppermute | solution.py:39
  99.4 5.5 %shard_map.41 = (f32[512,2048]{1,0:T(8,128)S(1)}, bf16[512,496]{1,0:T(8,128)(2,1)S(1)}) custom-call(bf16[512,512]{1,0:T(8,128)(2,1)S(1)} %shard_map.39.refs_0_, bf16[128,1536]{1,0:T(8,128)(2,1)S(1)} %shard_map.40.refs_1_, bf16[128,1536]{1,0:T(8,128)(2,1)S(1)} %collective-permute-done.14.refs_2_, bf16[128,1536]{1,0:T(8,128)(2,1)S(1)} %collective-permute-done.15.refs_3_, ...), custom_call_target="tpu_custom_call" | custom-call | flops 1000000000 | tf_op jit(solution)/shard_map/pallas_call | solution.py:221
  105.7 2.3 %shard_map.43 = bf16[512,2048]{1,0:T(8,128)(2,1)} custom-call(bf16[512,496]{1,0:T(8,128)(2,1)S(1)} %get-tuple-element.68.weights, f32[512,2048]{1,0:T(8,128)S(1)} %get-tuple-element.69.total, bf16[256,2048]{1,0:T(8,128)(2,1)S(1)} %collective-permute-done.17.u, bf16[240,2048]{1,0:T(8,128)(2,1)S(1)} %collective-permute-done.18.value.w, f32[8,128]{1,0:T(8,128)S(1)} %shard_map.42._), custom_call_target="tpu_custom_call" | custom-call | flops 1040187392 | bytes 8323072 | tf_op jit(solution)/shard_map/pallas_call | solution.py:253
  (40 shorter events, 6.4 us)
Async XLA Ops:
  0.0 50.4 %collective-permute-start.3 = (bf16[512,2048]{1,0:T(8,128)(2,1)}, bf16[512,2048]{1,0:T(8,128)(2,1)S(1)}, u32[]{:S(2)}, u32[]{:S(2)}) collective-permute-start(bf16[512,2048]{1,0:T(8,128)(2,1)} %x.3), channel_id=1, source_target_pairs={{0,24},{4,12},{8,0},{12,20},{16,8},{20,28},{24,16},{28,4},{1,25},{... | collective-permute-start | bytes 6291464 | tf_op jit(solution)/shard_map/ppermute | solution.py:34
  5.0 50.1 %collective-permute-start.2 = (bf16[512,2048]{1,0:T(8,128)(2,1)}, bf16[512,2048]{1,0:T(8,128)(2,1)S(1)}, u32[]{:S(2)}, u32[]{:S(2)}) collective-permute-start(bf16[512,2048]{1,0:T(8,128)(2,1)} %x.3), channel_id=1, source_target_pairs={{0,4},{4,0},{8,12},{12,8},{16,20},{20,16},{24,28},{28,24},{1,5},{5... | collective-permute-start | bytes 6291464 | tf_op jit(solution)/shard_map/ppermute | solution.py:39
  5.1 1.7 %copy-start = (bf16[512,2048]{1,0:T(8,128)(2,1)S(1)}, bf16[512,2048]{1,0:T(8,128)(2,1)}, u32[]{:S(2)}) copy-start(bf16[512,2048]{1,0:T(8,128)(2,1)} %x.3) | copy-start | bytes 6291460
  7.8 51.0 %copy-start.1 = (bf16[512,2048]{1,0:T(8,128)(2,1)S(1)}, bf16[512,2048]{1,0:T(8,128)(2,1)}, u32[]{:S(2)}) copy-start(bf16[512,2048]{1,0:T(8,128)(2,1)} %x.3) | copy-start | bytes 6291460
  11.1 4.0 %collective-permute-start.5 = (bf16[512,128]{1,0:T(8,128)(2,1)S(1)}, bf16[512,128]{1,0:T(8,128)(2,1)S(1)}, u32[]{:S(2)}, u32[]{:S(2)}) collective-permute-start(bf16[512,128]{1,0:T(8,128)(2,1)S(1)} %get-tuple-element.56), channel_id=1, source_target_pairs={{4,12},{12,20},{20,28},{28,4},{5,13},{13,21},{21,29},{29,5},{6,14}... | collective-permute-start | bytes 393224 | tf_op jit(solution)/shard_map/ppermute | solution.py:34
  11.8 43.3 %collective-permute-start.4 = (bf16[512,128]{1,0:T(8,128)(2,1)S(1)}, bf16[512,128]{1,0:T(8,128)(2,1)S(1)}, u32[]{:S(2)}, u32[]{:S(2)}) collective-permute-start(bf16[512,128]{1,0:T(8,128)(2,1)S(1)} %get-tuple-element.55), channel_id=1, source_target_pairs={{0,4},{4,0},{8,12},{12,8},{16,20},{20,16},{24,28},{28,24},{1,5},{5... | collective-permute-start | bytes 393224 | tf_op jit(solution)/shard_map/ppermute | solution.py:39
  50.4 11.0 %copy-start.4 = (bf16[512,2048]{1,0:T(8,128)(2,1)}, bf16[512,2048]{1,0:T(8,128)(2,1)S(1)}, u32[]{:S(2)}) copy-start(bf16[512,2048]{1,0:T(8,128)(2,1)S(1)} %collective-permute-done.3.z.refs_6_) | copy-start | bytes 6291460
  50.4 28.3 %collective-permute-start.13 = (bf16[272,2048]{1,0:T(8,128)(2,1)}, bf16[272,2048]{1,0:T(8,128)(2,1)S(1)}, u32[]{:S(2)}, u32[]{:S(2)}) collective-permute-start(bf16[272,2048]{1,0:T(8,128)(2,1)} %get-tuple-element.63), channel_id=1, source_target_pairs={{0,8},{4,28},{8,16},{12,4},{16,24},{20,12},{24,0},{28,20},{1,9},{5... | collective-permute-start | bytes 3342344 | tf_op jit(solution)/shard_map/ppermute | solution.py:34
  55.2 26.6 %collective-permute-start.12 = (bf16[256,2048]{1,0:T(8,128)(2,1)}, bf16[256,2048]{1,0:T(8,128)(2,1)}, u32[]{:S(2)}, u32[]{:S(2)}) collective-permute-start(bf16[256,2048]{1,0:T(8,128)(2,1)} %slice.6), channel_id=1, source_target_pairs={{0,4},{4,0},{8,12},{12,8},{16,20},{20,16},{24,28},{28,24},{1,5},{5... | collective-permute-start | bytes 3145736 | tf_op jit(solution)/shard_map/ppermute | solution.py:39
  58.7 2.7 %copy-start.6 = (bf16[512,512]{1,0:T(8,128)(2,1)S(1)}, bf16[512,512]{1,0:T(8,128)(2,1)}, u32[]{:S(2)}) copy-start(bf16[512,512]{1,0:T(8,128)(2,1)} %far.1) | copy-start | bytes 1572868
  61.5 2.0 %collective-permute-start = (bf16[256,1024]{1,0:T(8,128)(2,1)S(1)}, bf16[256,1024]{1,0:T(8,128)(2,1)S(1)}, u32[]{:S(2)}, u32[]{:S(2)}) collective-permute-start(bf16[256,1024]{1,0:T(8,128)(2,1)S(1)} %get-tuple-element.18), channel_id=1, source_target_pairs={{0,1},{1,0},{2,3},{3,2},{4,5},{5,4},{6,7},{7,6},{8,9},{9,8},{10,11... | collective-permute-start | bytes 1572872 | tf_op jit(solution)/shard_map/cond/branch_1_fun/ppermute | solution.py:39
  63.6 8.4 %collective-permute-start.1 = (bf16[128,1024]{1,0:T(8,128)(2,1)S(1)}, bf16[128,1024]{1,0:T(8,128)(2,1)S(1)}, u32[]{:S(2)}, u32[]{:S(2)}) collective-permute-start(bf16[128,1024]{1,0:T(8,128)(2,1)S(1)} %get-tuple-element.20), channel_id=1, source_target_pairs={{0,2},{1,3},{2,0},{3,1},{4,6},{5,7},{6,4},{7,5},{8,10},{9,11},{10,... | collective-permute-start | bytes 786440 | tf_op jit(solution)/shard_map/cond/branch_1_fun/ppermute | solution.py:39
  72.1 12.9 %collective-permute-start.9 = (bf16[128,1024]{1,0:T(8,128)(2,1)S(1)}, bf16[128,1024]{1,0:T(8,128)(2,1)S(1)}, u32[]{:S(2)}, u32[]{:S(2)}) collective-permute-start(bf16[128,1024]{1,0:T(8,128)(2,1)S(1)} %get-tuple-element.58), channel_id=1, source_target_pairs={{0,8},{8,16},{16,24},{24,0},{1,9},{9,17},{17,25},{25,1},{2,10},{10... | collective-permute-start | bytes 786440 | tf_op jit(solution)/shard_map/ppermute | solution.py:34
  74.3 10.1 %collective-permute-start.11 = (bf16[128,512]{1,0:T(8,128)(2,1)S(1)}, bf16[128,512]{1,0:T(8,128)(2,1)S(1)}, u32[]{:S(2)}, u32[]{:S(2)}) collective-permute-start(bf16[128,512]{1,0:T(8,128)(2,1)S(1)} %get-tuple-element.67.own), channel_id=1, source_target_pairs={{0,4},{4,0},{8,12},{12,8},{16,20},{20,16},{24,28},{28,24},{1,5},{5... | collective-permute-start | bytes 393224 | tf_op jit(solution)/shard_map/ppermute | solution.py:39
  74.4 10.0 %collective-permute-start.10 = (bf16[128,512]{1,0:T(8,128)(2,1)S(1)}, bf16[128,512]{1,0:T(8,128)(2,1)S(1)}, u32[]{:S(2)}, u32[]{:S(2)}) collective-permute-start(bf16[128,512]{1,0:T(8,128)(2,1)S(1)} %get-tuple-element.57.a0), channel_id=1, source_target_pairs={{4,28},{12,4},{20,12},{28,20},{5,29},{13,5},{21,13},{29,21},{6,30}... | collective-permute-start | bytes 393224 | tf_op jit(solution)/shard_map/ppermute | solution.py:34
  78.8 26.2 %collective-permute-start.18 = (bf16[240,2048]{1,0:T(8,128)(2,1)}, bf16[240,2048]{1,0:T(8,128)(2,1)S(1)}, u32[]{:S(2)}, u32[]{:S(2)}) collective-permute-start(bf16[240,2048]{1,0:T(8,128)(2,1)} %copy-done.3), channel_id=1, source_target_pairs={{0,8},{4,28},{8,16},{12,4},{16,24},{20,12},{24,0},{28,20},{1,9},{5... | collective-permute-start | bytes 2949128 | tf_op jit(solution)/shard_map/ppermute | solution.py:34
  81.8 23.9 %collective-permute-start.17 = (bf16[256,2048]{1,0:T(8,128)(2,1)}, bf16[256,2048]{1,0:T(8,128)(2,1)S(1)}, u32[]{:S(2)}, u32[]{:S(2)}) collective-permute-start(bf16[256,2048]{1,0:T(8,128)(2,1)} %get-tuple-element.73), channel_id=1, source_target_pairs={{0,4},{4,0},{8,12},{12,8},{16,20},{20,16},{24,28},{28,24},{1,5},{5... | collective-permute-start | bytes 3145736 | tf_op jit(solution)/shard_map/ppermute | solution.py:39
  85.1 14.3 %copy-start.5 = (bf16[512,2048]{1,0:T(8,128)(2,1)S(1)}, bf16[512,2048]{1,0:T(8,128)(2,1)}, u32[]{:S(2)}) copy-start(bf16[512,2048]{1,0:T(8,128)(2,1)} %copy-done.4) | copy-start | bytes 6291460
  85.1 12.3 %collective-permute-start.14 = (bf16[128,1536]{1,0:T(8,128)(2,1)S(1)}, bf16[128,1536]{1,0:T(8,128)(2,1)S(1)}, u32[]{:S(2)}, u32[]{:S(2)}) collective-permute-start(bf16[128,1536]{1,0:T(8,128)(2,1)S(1)} %shard_map.40.refs_1_), channel_id=1, source_target_pairs={{0,2},{1,3},{2,0},{3,1},{4,6},{5,7},{6,4},{7,5},{8,10},{9,11},{10,... | collective-permute-start | bytes 1179656 | tf_op jit(solution)/shard_map/ppermute | solution.py:39
  86.7 10.2 %collective-permute-start.6 = (bf16[128,512]{1,0:T(8,128)(2,1)S(1)}, bf16[128,512]{1,0:T(8,128)(2,1)S(1)}, u32[]{:S(2)}, u32[]{:S(2)}) collective-permute-start(bf16[128,512]{1,0:T(8,128)(2,1)S(1)} %get-tuple-element.57.a0), channel_id=1, source_target_pairs={{0,2},{1,3},{2,0},{3,1},{4,6},{5,7},{6,4},{7,5},{8,10},{9,11},{10,... | collective-permute-start | bytes 393224 | tf_op jit(solution)/shard_map/ppermute | solution.py:39
  87.2 9.7 %collective-permute-start.7 = (bf16[128,512]{1,0:T(8,128)(2,1)S(1)}, bf16[128,512]{1,0:T(8,128)(2,1)S(1)}, u32[]{:S(2)}, u32[]{:S(2)}) collective-permute-start(bf16[128,512]{1,0:T(8,128)(2,1)S(1)} %get-tuple-element.57.a0), channel_id=1, source_target_pairs={{0,1},{1,0},{2,3},{3,2},{4,5},{5,4},{6,7},{7,6},{8,9},{9,8},{10,11... | collective-permute-start | bytes 393224 | tf_op jit(solution)/shard_map/ppermute | solution.py:39
  96.9 1.3 %collective-permute-start.8 = (bf16[128,512]{1,0:T(8,128)(2,1)S(1)}, bf16[128,512]{1,0:T(8,128)(2,1)S(1)}, u32[]{:S(2)}, u32[]{:S(2)}) collective-permute-start(bf16[128,512]{1,0:T(8,128)(2,1)S(1)} %collective-permute-done.6.a1), channel_id=1, source_target_pairs={{0,1},{1,0},{2,3},{3,2},{4,5},{5,4},{6,7},{7,6},{8,9},{9,8},{10,11... | collective-permute-start | bytes 393224 | tf_op jit(solution)/shard_map/ppermute | solution.py:39
  96.9 1.9 %collective-permute-start.15 = (bf16[128,1536]{1,0:T(8,128)(2,1)S(1)}, bf16[128,1536]{1,0:T(8,128)(2,1)S(1)}, u32[]{:S(2)}, u32[]{:S(2)}) collective-permute-start(bf16[128,1536]{1,0:T(8,128)(2,1)S(1)} %shard_map.40.refs_1_), channel_id=1, source_target_pairs={{0,1},{1,0},{2,3},{3,2},{4,5},{5,4},{6,7},{7,6},{8,9},{9,8},{10,11... | collective-permute-start | bytes 1179656 | tf_op jit(solution)/shard_map/ppermute | solution.py:39
  97.4 2.0 %collective-permute-start.16 = (bf16[128,1536]{1,0:T(8,128)(2,1)S(1)}, bf16[128,1536]{1,0:T(8,128)(2,1)S(1)}, u32[]{:S(2)}, u32[]{:S(2)}) collective-permute-start(bf16[128,1536]{1,0:T(8,128)(2,1)S(1)} %collective-permute-done.14.refs_2_), channel_id=1, source_target_pairs={{0,1},{1,0},{2,3},{3,2},{4,5},{5,4},{6,7},{7,6},{8,9},{9,8},{10,11... | collective-permute-start | bytes 1179656 | tf_op jit(solution)/shard_map/ppermute | solution.py:39
  (2 other events, 2.0 us)
